TPU v7x, 32 devices: a whole 2x2x4 slice. The times are simulated.
32 devices in a mesh: ctx: 2 (over x), head: 4 (over y, core), rep: 4 (over z).
Axes of the slice: x: 2, y: 2, z: 4, core: 2. Of those that a mesh axis runs over, the one named last changes fastest.
Arguments:
- kv_cache: float32 [8, 2, 512, 8, 128], P('head', None, 'ctx', 'rep'), may hold values from -8 to 8
- prefill_q: float32 [8, 256, 64, 128], P('head', 'ctx', 'rep'), may hold values from -512 to 512
- decode_q: float32 [8, 8, 4, 64, 128], P(None, ('ctx', 'rep'), None, 'head'), may hold values from -512 to 512
- decode_kv: float32 [8, 8, 4, 2, 8, 128], P(None, ('ctx', 'rep'), None, None, 'head'), may hold values from -12 to 12
- lengths: int32 [8], replicated, may hold values from 256 to 512, as said below
- row_length: int32 [8, 8], P(None, ('ctx', 'rep')), may hold values from 2 to 512, as said below
Outputs:
- prefill_out: float32 [8, 256, 64, 128], P('head', 'ctx', 'rep')
- decode_out: float32 [8, 8, 4, 64, 128], P(None, ('ctx', 'rep'), None, 'head')
Inputs may be any that keep to these rules, and one draw needn't show every extreme that they name: `lengths`: multiples of 128; some request has length 512. `row_length`: a row reads at most its request's length; every request has a row that reads its whole length.
All inputs are finite; a program needn't handle non-finite values.
Results may differ from a plain program's by a relative error of at most 0.0003.
Values sent between devices are 32-bit elements; how exact they have to be, the bound alone decides.
No kernel may reach another device: no remote copies, remote signals or barrier semaphores. Data moves between devices by JAX's collectives and lax.ppermute only.
A program may use at most 128 MiB of HBM per device.

v0:
```python
import math

import jax
import jax.numpy as jnp
from jax import lax
from jax.sharding import PartitionSpec as P

NEG_FILL = -1e30
HIGH_PRECISION = lax.Precision.HIGHEST


def broadcast(value, axis, source):
    kept = jnp.where(lax.axis_index(axis) == source, value, 0).astype(value.dtype)
    return lax.psum(kept, axis)


def online_fold(running, scores, value_rows, pattern):
    run_max, run_total, run_acc = running
    new_max = jnp.maximum(run_max, jnp.max(scores, axis=-1))
    weights = jnp.exp(scores - new_max[..., None])
    new_total = jnp.sum(weights, axis=-1)
    new_acc = jnp.einsum(pattern, weights, value_rows, precision=HIGH_PRECISION)
    return (new_max, new_total, new_acc)


def empty_state(lead_shape, head_dim):
    return (
        jnp.full(lead_shape, NEG_FILL, jnp.float32),
        jnp.zeros(lead_shape, jnp.float32),
        jnp.zeros(lead_shape + (head_dim,), jnp.float32),
    )


def block_fold(running, query_rows, key_block, first_pos, limits, score_scale, strict):
    block_len = key_block.shape[2]
    scores = (
        jnp.einsum("bkrd,bnkd->bkrn", query_rows, key_block[:, 0], precision=HIGH_PRECISION)
        * score_scale
    )
    positions = first_pos + jnp.arange(block_len, dtype=jnp.int32)
    if strict:
        allowed = positions[None, None, :] < limits[:, :, None]
    else:
        allowed = positions[None, None, :] <= limits[:, :, None]
    scores = jnp.where(allowed[:, None], scores, NEG_FILL)
    return online_fold(running, scores, key_block[:, 1], "bkrn,bnkd->bkrd")


def source_major(values, slot_count, kv_heads, sources, count_rows, step_count, group_size):
    tail_shape = values.shape[3:]
    spread_out = values.reshape(
        (slot_count, kv_heads, sources, count_rows, step_count, group_size) + tail_shape
    )
    axes_order = (2, 0, 3, 4, 1, 5) + tuple(range(6, 6 + len(tail_shape)))
    moved = jnp.transpose(spread_out, axes_order)
    return moved.reshape(
        (sources, slot_count, count_rows, step_count, kv_heads * group_size) + tail_shape
    )


def on_device(kv_cache, prefill_q, decode_q, decode_kv, lengths, row_length):
    ctx_count = lax.axis_size("ctx")
    ctx_index = lax.axis_index("ctx")
    head_index = lax.axis_index("head")
    req_group, span_rows, rep_heads, head_dim = prefill_q.shape
    rep_kv = kv_cache.shape[3]
    group_size = rep_heads // rep_kv
    block_len = kv_cache.shape[2]
    score_scale = 1.0 / math.sqrt(head_dim)
    group_lengths = lax.dynamic_slice_in_dim(lengths, head_index * req_group, req_group)
    span_pos = (
        group_lengths[:, None]
        - span_rows * ctx_count
        + ctx_index * span_rows
        + jnp.arange(span_rows, dtype=jnp.int32)[None, :]
    )
    row_pos = jnp.repeat(span_pos, group_size, axis=1)
    prefill_rows = jnp.transpose(
        prefill_q.reshape(req_group, span_rows, rep_kv, group_size, head_dim), (0, 2, 1, 3, 4)
    ).reshape(req_group, rep_kv, span_rows * group_size, head_dim)
    start_state = empty_state((req_group, rep_kv, span_rows * group_size), head_dim)
    run_max, run_total, run_acc = block_fold(
        start_state,
        prefill_rows,
        lax.all_gather(kv_cache, "ctx", axis=2, tiled=True),
        jnp.int32(0),
        row_pos,
        score_scale,
        False,
    )
    prefill_vals = run_acc / run_total[..., None]
    prefill_out = jnp.transpose(
        prefill_vals.reshape(req_group, rep_kv, span_rows, group_size, head_dim), (0, 2, 1, 3, 4)
    ).reshape(prefill_q.shape)
    all_requests = lax.all_gather(kv_cache, "head", axis=0, tiled=True)
    head_cache = broadcast(all_requests, "rep", head_index)
    requests, row_count, step_count, local_heads, unused_dim = decode_q.shape
    kv_heads = local_heads // group_size
    gathered_rows, gathered_limits = (
        lax.all_gather(decode_q, "ctx", axis=1, tiled=True),
        lax.all_gather(row_length, "ctx", axis=1, tiled=True),
    )
    total_rows = gathered_rows.shape[1]
    grouped = jnp.transpose(
        gathered_rows.reshape(requests, total_rows, step_count, kv_heads, group_size, head_dim),
        (0, 3, 1, 2, 4, 5),
    ).reshape(requests, kv_heads, -1, head_dim)
    limits = jnp.broadcast_to(
        gathered_limits[:, :, None, None], (requests, total_rows, step_count, group_size)
    ).reshape(requests, -1)
    running = empty_state((requests, kv_heads, grouped.shape[2]), head_dim)
    running = block_fold(
        running, grouped, head_cache, ctx_index * block_len, limits, score_scale, True
    )
    shaped = tuple(
        (
            source_major(values, requests, kv_heads, ctx_count, row_count, step_count, group_size)
            for values in running
        )
    )
    home_max, home_total, home_acc = (
        lax.all_to_all(shaped[0], "ctx", split_axis=0, concat_axis=0, tiled=True),
        lax.all_to_all(shaped[1], "ctx", split_axis=0, concat_axis=0, tiled=True),
        lax.all_to_all(shaped[2], "ctx", split_axis=0, concat_axis=0, tiled=True),
    )
    ctx_max = jnp.max(home_max, axis=0)
    factor = jnp.exp(home_max - ctx_max[None])
    ctx_total = jnp.sum(home_total * factor, axis=0)
    ctx_acc = jnp.sum(home_acc * factor[..., None], axis=0)
    home_rows = decode_q.reshape(requests, row_count, step_count, kv_heads, group_size, head_dim)
    draft_scores = (
        jnp.einsum(
            "artkgd,arskd->artkgs", home_rows, decode_kv[:, :, :, 0], precision=HIGH_PRECISION
        )
        * score_scale
    )
    step_ids = jnp.arange(step_count, dtype=jnp.int32)
    causal = step_ids[None, :] <= step_ids[:, None]
    draft_scores = jnp.where(causal[None, None, :, None, None, :], draft_scores, NEG_FILL)
    ctx_max = ctx_max.reshape(requests, row_count, step_count, kv_heads, group_size)
    ctx_total = ctx_total.reshape(requests, row_count, step_count, kv_heads, group_size)
    ctx_acc = ctx_acc.reshape(requests, row_count, step_count, kv_heads, group_size, head_dim)
    joint_max = jnp.maximum(ctx_max, jnp.max(draft_scores, axis=-1))
    draft_weights = jnp.exp(draft_scores - joint_max[..., None])
    ctx_factor = jnp.exp(ctx_max - joint_max)
    denominator = ctx_total * ctx_factor + jnp.sum(draft_weights, axis=-1)
    numerator = ctx_acc * ctx_factor[..., None] + jnp.einsum(
        "artkgs,arskd->artkgd", draft_weights, decode_kv[:, :, :, 1], precision=HIGH_PRECISION
    )
    decode_out = (numerator / denominator[..., None]).reshape(decode_q.shape)
    return (prefill_out, decode_out)


def solution(mesh):
    in_specs = (
        P("head", None, "ctx", "rep", None),
        P("head", "ctx", "rep", None),
        P(None, ("ctx", "rep"), None, "head", None),
        P(None, ("ctx", "rep"), None, None, "head", None),
        P(),
        P(None, ("ctx", "rep")),
    )
    out_specs = (P("head", "ctx", "rep", None), P(None, ("ctx", "rep"), None, "head", None))
    return jax.shard_map(
        on_device, mesh=mesh, in_specs=in_specs, out_specs=out_specs, check_vma=False
    )
```

profile of v0, /device:TPU:7, one launch (start us, length us, event | category | flops | bytes accessed | tf_op | source)
XLA Modules:
  0.0 280.7 jit_solution(5755422686790085839)
XLA Ops:
  7.2 0.0 copy-start
  7.2 0.0 all-gather.6.cloned.1.call-start
  7.2 2.4 copy.82
  9.6 0.0 all-gather.6.cloned.1.call-update
  9.7 0.0 all-gather.4.cloned.1.call-start
  9.7 0.7 all-gather.4.cloned.1.call-update
  10.4 0.0 all-reduce.2.cloned.1.call-start
  10.5 34.9 %all-gather.6.cloned.1.call-done = f32[8,2,256,2,128]{4,2,3,0,1:T(8,128)} async-done(((f32[2,2,256,2,128]{4,2,3,0,1:T(8,128)}), f32[8,2,256,2,128]{4,2,3,0,1:T(8,128)}) %all-gather.6.cloned.1.call-update) | async-done | bytes 4194320 | tf_op jit(solution)/shard_map/all_gather | solution.py:95
  45.3 2.4 broadcast_select_fusion
  47.8 0.0 all-reduce.2.cloned.1.call-update
  47.8 0.6 copy-done.5
  48.4 3.1 %all-gather = s32[2,1,8]{2,1,0:T(1,128)S(1)} all-gather(s32[1,1,8]{2,1,0:T(1,128)S(1)} %bitcast.147), channel_id=1, replica_groups=mesh['ctx'=2,'head'=4,'rep'=4] {'ctx'}, dimensions={0}, use_global_device_ids=true | all-gather | bytes 96 | tf_op jit(solution)/shard_map/all_gather | solution.py:101
  51.5 0.1 copy.85
  51.5 0.1 broadcast_in_dim.76
  51.6 0.1 lt.24
  51.7 0.0 copy-done.4
  51.7 0.1 add_add_fusion
  51.8 0.1 iota_add_fusion.1
  51.9 0.1 broadcast_in_dim.48
  52.0 0.1 le.37
  52.1 0.0 copy-done.1
  52.1 8.6 %all_gather.15 = f32[8,2,4,16,128]{4,3,2,1,0:T(8,128)S(1)} all-gather(f32[8,1,4,16,128]{4,3,2,1,0:T(8,128)S(1)} %copy-done.1), channel_id=1, replica_groups=mesh['ctx'=2,'head'=4,'rep'=4] {'ctx'}, dimensions={1}, use_global_device_ids=true | all-gather | bytes 786432 | tf_op jit(solution)/shard_map/all_gather | solution.py:100
  60.7 0.9 copy.87
  61.6 0.1 broadcast_compare_fusion
  61.8 3.6 %fusion.31 = (f32[8,4,2,8]{3,1,2,0:T(4,128)S(1)}, f32[8,1,4,2,8,4]{4,5,2,3,0,1:T(4,128)S(1)}) fusion(f32[8,1,4,1,2,128]{5,4,3,2,1,0:T(2,128)S(1)} %get-tuple-element.13, pred[4,4]{1,0:T(4,128)(4,1)S(1)} %iota_compare_fusion.1, f32[8,1,4,16,128]{4,3,2,1,0:T(8,128)S(1)} %copy-done.1), kind=kOutput, calls=%fused_computation.63 | convolution fusion | flops 3151360 | bytes 305168 | tf_op jit(solution)/shard_map/artkgd,arskd->artkgs/dot_general | solution.py:132
  65.3 0.6 iota_compare_fusion
  66.0 17.8 %all-gather.4.cloned.1.call-done = f32[2,2,512,2,128]{4,2,3,0,1:T(8,128)} async-done(((f32[2,2,256,2,128]{4,2,3,0,1:T(8,128)}), f32[2,2,512,2,128]{4,2,3,0,1:T(8,128)}) %all-gather.4.cloned.1.call-update) | async-done | bytes 2097168 | tf_op jit(solution)/shard_map/all_gather | solution.py:85
  83.8 0.0 copy-done
  83.8 9.6 %fusion = (f32[2,2,1024]{2,1,0:T(2,128)S(1)}, f32[2,2,1024,512]{2,3,1,0:T(8,128)S(1)}) fusion(pred[2,1024,512]{1,2,0:T(8,128)(4,1)S(1)} %iota_compare_fusion, f32[2,2,512,2,128]{4,2,3,0,1:T(8,128)} %all-gather.4.cloned.1.call-done, f32[2,128,16,128]{3,2,1,0:T(8,128)S(1)} %copy-done), kind=kOutput, calls=%fused_computation.2 | convolution fusion | flops 3227512832 | bytes 12599296 | tf_op jit(solution)/shard_map/bkrd,bnkd->bkrn/dot_general | solution.py:37
  93.3 0.0 copy-start.2
  93.4 2.2 fusion.1
  95.6 0.0 copy-done.2
  95.6 15.4 %divide_bitcast_fusion = f32[2,128,2,8,128]{4,3,1,2,0:T(8,128)S(1)} fusion(f32[2,2,1024]{2,1,0:T(2,128)S(1)} %fusion.1, f32[2,2,512,2,128]{4,2,3,0,1:T(8,128)S(1)} %copy-done.2, f32[2,2,1024,512]{2,3,1,0:T(8,128)S(1)} %get-tuple-element.17, f32[2,2,1024]{2,1,0:T(2,128)S(1)} %broadcast_maximum_fusion, pred[2,1024,512]{1,2,0:T(8,128)(4,1)S(1)} %iota_compare_fusion), kind=kOutput, calls=%fused_computation.19 | convolution fusion | flops 3228041216 | bytes 12615680 | tf_op jit(solution)/shard_map/bkrn,bnkd->bkrd/dot_general | solution.py:22
  111.0 1.5 copy.141
  112.5 131.2 %all-reduce.2.cloned.1.call-done = f32[8,2,256,2,128]{4,2,3,0,1:T(8,128)} async-done(((f32[8,2,256,2,128]{4,2,3,0,1:T(8,128)}), f32[8,2,256,2,128]{4,2,3,0,1:T(8,128)}) %all-reduce.2.cloned.1.call-update) | async-done | bytes 4194320 | tf_op jit(solution)/shard_map/psum | solution.py:14
  243.7 4.1 %fusion.30 = (f32[8,2,64]{2,1,0:T(2,128)S(1)}, f32[8,2,64,256]{3,2,1,0:T(8,128)S(1)}) fusion(f32[8,2,64,128]{3,2,1,0:T(8,128)} %bitcast.142, f32[8,2,256,2,128]{4,2,3,0,1:T(8,128)} %all-reduce.2.cloned.1.call-done, pred[8,64,256]{2,1,0:T(8,128)(4,1)S(1)} %broadcast_compare_fusion), kind=kOutput, calls=%fused_computation.62 | convolution fusion | flops 403438592 | bytes 3805184 | tf_op jit(solution)/shard_map/bkrd,bnkd->bkrn/dot_general | solution.py:37
  247.9 0.4 fusion.19
  248.3 0.1 reshape.223
  248.4 0.1 copy.101
  248.5 0.1 reshape.224
  248.6 0.7 reshape.235
  249.3 3.5 %all-to-all-start.2 = ((f32[2,1,512]{2,1,0:T(1,128)}), f32[2,1,512]{2,1,0:T(1,128)S(1)}, u32[]{:S(2)}, u32[]{:S(2)}) async-start(f32[2,1,512]{2,1,0:T(1,128)} %reshape.235), calls=%async_computation.2 | async-start | bytes 8192 | tf_op jit(solution)/shard_map/all_to_all | solution.py:123
  252.8 0.1 max_broadcast_in_dim.26
  252.9 0.1 copy.91
  252.9 0.1 reshape.216
  253.0 0.7 reshape.233
  253.7 0.2 all-to-all-done.2
  253.9 4.7 %all-to-all-start.1 = ((f32[2,1,512]{2,1,0:T(1,128)}), f32[2,1,512]{2,1,0:T(1,128)S(1)}, u32[]{:S(2)}, u32[]{:S(2)}) async-start(f32[2,1,512]{2,1,0:T(1,128)} %reshape.233), calls=%async_computation.1 | async-start | bytes 8192 | tf_op jit(solution)/shard_map/all_to_all | solution.py:122
  258.6 3.3 %fusion.7 = f32[8,2,64,128]{3,2,1,0:T(8,128)S(1)} fusion(f32[8,2,256,2,128]{4,2,3,0,1:T(8,128)} %all-reduce.2.cloned.1.call-done, f32[8,2,64,256]{3,2,1,0:T(8,128)S(1)} %get-tuple-element.19, f32[8,2,64]{2,1,0:T(2,128)S(1)} %broadcast_maximum_fusion.1), kind=kOutput, calls=%fused_computation.11 | convolution fusion | flops 402915328 | bytes 3674112 | tf_op jit(solution)/shard_map/bkrn,bnkd->bkrd/dot_general | solution.py:22
  261.9 0.8 copy.142
  262.8 0.6 broadcast.71
  263.4 0.7 reduce.6
  264.1 0.1 reshape.236
  264.1 0.0 all-to-all-done.1
  264.2 3.5 %all-to-all-start = ((f32[2,8,1,4,16,128]{5,4,3,1,2,0:T(8,128)}), f32[2,8,1,4,16,128]{5,4,3,1,2,0:T(8,128)S(1)}, u32[]{:S(2)}, u32[]{:S(2)}) async-start(f32[2,8,1,4,16,128]{5,4,3,1,2,0:T(8,128)} %bitcast.137), calls=%async_computation | async-start | bytes 1048576 | tf_op jit(solution)/shard_map/all_to_all | solution.py:124
  267.7 0.7 reduce.5
  268.4 0.1 reshape.234
  268.5 0.1 reshape.218
  268.6 0.1 fusion.23
  268.7 0.1 reshape.225
  268.9 3.7 %all-to-all-done = f32[2,8,1,4,16,128]{5,4,3,1,2,0:T(8,128)S(1)} async-done(((f32[2,8,1,4,16,128]{5,4,3,1,2,0:T(8,128)}), f32[2,8,1,4,16,128]{5,4,3,1,2,0:T(8,128)S(1)}, u32[]{:S(2)}, u32[]{:S(2)}) %all-to-all-start) | async-done | bytes 524320 | tf_op jit(solution)/shard_map/all_to_all | solution.py:124
  272.6 0.2 multiply_reduce_fusion
  272.8 0.7 fusion.16
  273.5 0.7 copy.143
  (19 shorter events, 0.2 us)
Async XLA Ops:
  7.2 76.6 %copy-start = (f32[2,128,16,128]{3,2,1,0:T(8,128)S(1)}, f32[2,128,16,128]{3,2,1,0:T(8,128)}, u32[]{:S(2)}) copy-start(f32[2,128,16,128]{3,2,1,0:T(8,128)} %param.7) | copy-start | bytes 6291460
  7.2 38.2 %all-gather.6.cloned.1.call-start = ((), (), s32[]{:S(2)}) async-start(), calls=%async_computation.4 | async-start | bytes 5242880 | tf_op jit(solution)/shard_map/all_gather | solution.py:95
  9.7 74.1 %all-gather.4.cloned.1.call-start = ((), (), s32[]{:S(2)}) async-start(), calls=%async_computation.3 | async-start | bytes 3145728 | tf_op jit(solution)/shard_map/all_gather | solution.py:85
  10.4 233.3 %all-reduce.2.cloned.1.call-start = ((), (), s32[]{:S(2)}) async-start(), calls=%async_computation.5 | async-start | bytes 8388608 | tf_op jit(solution)/shard_map/psum | solution.py:14
  47.7 0.7 copy-start.5
  47.8 4.0 %copy-start.4 = (s32[8]{0:T(128)S(1)}, s32[8]{0:T(128)}, u32[]{:S(2)}) copy-start(s32[8]{0:T(128)} %param.10) | copy-start | bytes 100
  47.8 4.3 %copy-start.1 = (f32[8,1,4,16,128]{4,3,2,1,0:T(8,128)S(1)}, f32[8,1,4,16,128]{4,3,2,1,0:T(8,128)}, u32[]{:S(2)}) copy-start(f32[8,1,4,16,128]{4,3,2,1,0:T(8,128)} %param.8) | copy-start | bytes 786436
  47.8 13.8 %copy-start.3 = (f32[8,1,4,2,2,128]{5,4,3,2,1,0:T(2,128)S(1)}, f32[8,1,4,2,2,128]{5,4,3,2,1,0:T(2,128)}, u32[]{:S(2)}) copy-start(f32[8,1,4,2,2,128]{5,4,3,2,1,0:T(2,128)} %param.9) | copy-start | bytes 196612
  93.3 2.2 copy-start.2
  249.3 4.7 %all-to-all-start.2 = ((f32[2,1,512]{2,1,0:T(1,128)}), f32[2,1,512]{2,1,0:T(1,128)S(1)}, u32[]{:S(2)}, u32[]{:S(2)}) async-start(f32[2,1,512]{2,1,0:T(1,128)} %reshape.235), calls=%async_computation.2 | async-start | bytes 8192 | tf_op jit(solution)/shard_map/all_to_all | solution.py:123
  253.9 10.2 %all-to-all-start.1 = ((f32[2,1,512]{2,1,0:T(1,128)}), f32[2,1,512]{2,1,0:T(1,128)S(1)}, u32[]{:S(2)}, u32[]{:S(2)}) async-start(f32[2,1,512]{2,1,0:T(1,128)} %reshape.233), calls=%async_computation.1 | async-start | bytes 8192 | tf_op jit(solution)/shard_map/all_to_all | solution.py:122
  264.2 8.5 %all-to-all-start = ((f32[2,8,1,4,16,128]{5,4,3,1,2,0:T(8,128)}), f32[2,8,1,4,16,128]{5,4,3,1,2,0:T(8,128)S(1)}, u32[]{:S(2)}, u32[]{:S(2)}) async-start(f32[2,8,1,4,16,128]{5,4,3,1,2,0:T(8,128)} %bitcast.137), calls=%async_computation | async-start | bytes 1048576 | tf_op jit(solution)/shard_map/all_to_all | solution.py:124
Sparse Core Ops, SparseCore 0:
  10.2 35.1 all-gather.5
  47.5 36.2 all-gather.3
  86.1 157.5 all-reduce.1
where the time goes:
time: 286 us; the launch traced here: 281 us
  waiting for transfers between devices  189 us (66%)
  matrix products  36.7 us (13%)
  between operations  14 us (5%)
  starting transfers between devices  11.8 us (4%)
  blocking collectives  11.6 us (4%)
  local copies, waits for them, and re-layouts  10.3 us (4%)
  other arithmetic  7.82 us (3%)
    psum x1, waiting for transfers between devices, broadcast(): return lax.psum(kept, axis)  131 us
    all_gather x1, waiting for transfers between devices, on_device(): all_requests = lax.all_gather(kv_cache, 'head', axis=0, tiled=True)  34.9 us
    dot_general x2, matrix products, online_fold(): new_acc = jnp.einsum(pattern, weights, value_rows, precision=HIGH_PRECISION)  18.8 us
    all_gather x1, waiting for transfers between devices, on_device(): lax.all_gather(kv_cache, 'ctx', axis=2, tiled=True)  17.8 us
    dot_general x2, matrix products, block_fold(): jnp.einsum('bkrd,bnkd->bkrn', query_rows, key_block[:, 0], precision=HIGH...  13.7 us
    all_gather x1, blocking collectives, on_device(): lax.all_gather(decode_q, 'ctx', axis=1, tiled=True)  8.56 us
  transfers between devices with their start and end apart: 6, of which 5 were waited for; matrix products, arithmetic and copies ran while one was open for 16% of the time, Pallas kernels for 0%

commit v1 on v0

v1 whole, which is shorter than its diff:
```python
import functools
import math

import jax
import jax.numpy as jnp
from jax import lax
from jax.experimental import pallas as pl
from jax.experimental.pallas import tpu as pltpu
from jax.sharding import PartitionSpec as P

NEG_FILL = -1e30
LOG2E = math.log2(math.e)
F32 = jnp.float32
BF16 = jnp.bfloat16


def split_two(x):
    high = x.astype(BF16)
    return high, (x - high.astype(F32)).astype(BF16)


def split_three(x):
    high = x.astype(BF16)
    rest = x - high.astype(F32)
    mid = rest.astype(BF16)
    return high, mid, (rest - mid.astype(F32)).astype(BF16)


def query_terms(q):
    a, b, c = split_three(q)
    return jnp.concatenate([a, b, a, b, a, c], axis=-1)


def key_terms(k):
    a, b, c = split_three(k)
    return jnp.concatenate([a, a, b, b, c, a], axis=-1)


def value_terms(v):
    return jnp.concatenate(split_two(v), axis=-1)


def scores_of(q6, k6):
    return lax.dot_general(q6, k6, (((1,), (1,)), ((), ())), preferred_element_type=F32)


def weighted(p, vv):
    half = vv.shape[1] // 2
    a, b = split_two(p)
    both = jnp.dot(a, vv, preferred_element_type=F32) + jnp.dot(b, vv, preferred_element_type=F32)
    return both[:, :half] + both[:, half:]


def attend(q6, groups):
    state = None
    for group in groups:
        parts = [jnp.where(mask(), scores_of(q6, k6), NEG_FILL) for k6, _, mask in group]
        top = functools.reduce(jnp.maximum, [jnp.max(s, axis=-1, keepdims=True) for s in parts])
        if state is not None:
            top = jnp.maximum(top, state[0])
        weights = [jnp.exp2(s - top) for s in parts]
        total = functools.reduce(jnp.add, [jnp.sum(w, axis=-1, keepdims=True) for w in weights])
        acc = functools.reduce(jnp.add, [weighted(w, vv) for w, (_, vv, _) in zip(weights, group)])
        if state is not None:
            factor = jnp.exp2(state[0] - top)
            total = total + state[1] * factor
            acc = acc + state[2] * factor
        state = (top, total, acc)
    return state[2] / state[1]


def in_pairs(blocks):
    return [blocks[i : i + 2] for i in range(0, len(blocks), 2)]


def cache_head(ref, which, head, heads):
    rows = ref.shape[2] // heads
    return ref[0, which, pl.ds(head, rows, stride=heads), :]


def prefill_kernel(blocks, heads, group, scale, marks, q_ref, *refs):
    kv_refs, o_ref = refs[:blocks], refs[-1]
    span = q_ref.shape[1]
    dim = q_ref.shape[3]
    head = pl.program_id(0)
    keys = [key_terms(cache_head(ref, 0, head, heads)) for ref in kv_refs]
    vals = [value_terms(cache_head(ref, 1, head, heads)) for ref in kv_refs]
    chunk = min(span, 64)
    for first in range(0, span, chunk):
        q = q_ref[0, first : first + chunk].reshape(chunk * group, dim) * scale
        q6 = query_terms(q)

        def mask_of(b, first=first):
            shape = (chunk * group, keys[b].shape[0])
            pos = marks[1 + b] + lax.broadcasted_iota(jnp.int32, shape, 1)
            row = lax.broadcasted_iota(jnp.int32, shape, 0) // group
            return pos <= row + (marks[0] + first)

        todo = [(keys[b], vals[b], functools.partial(mask_of, b)) for b in range(blocks)]
        out = attend(q6, in_pairs(todo))
        o_ref[0, first : first + chunk] = out.reshape(chunk, group, dim)


def prefill_request(index, marks, prefill_q, kv_list, carried, heads, scale):
    nreq, span, q_heads, dim = prefill_q.shape
    group = q_heads // heads
    blocks = len(kv_list)
    q_spec = pl.BlockSpec((1, span, group, dim), lambda k, m: (index, 0, k, 0))
    kv_specs = [pl.BlockSpec(kv.shape, lambda k, m: (0, 0, 0, 0)) for kv in kv_list]
    extra_specs, extra, alias = [], [], {}
    if carried is not None:
        extra_specs, extra = [pl.BlockSpec(memory_space=pl.ANY)], [carried]
        alias = {2 + blocks: 0}
    keys = sum(kv.shape[2] for kv in kv_list)
    return pl.pallas_call(
        functools.partial(prefill_kernel, blocks, heads, group, scale),
        grid_spec=pltpu.PrefetchScalarGridSpec(
            num_scalar_prefetch=1,
            grid=(heads,),
            in_specs=[q_spec] + kv_specs + extra_specs,
            out_specs=q_spec,
        ),
        out_shape=jax.ShapeDtypeStruct(prefill_q.shape, F32),
        input_output_aliases=alias,
        compiler_params=pltpu.CompilerParams(vmem_limit_bytes=40 * 2**20),
        cost_estimate=pl.CostEstimate(
            flops=2 * 10 * span * group * keys * dim,
            bytes_accessed=4 * (2 * span * q_heads * dim + 2 * keys * dim),
            transcendentals=span * group * keys,
        ),
        name="prefill",
    )(marks, prefill_q, *kv_list, *extra)


def decode_kernel(blocks, packets, heads, group, steps, scale, marks, *refs):
    pk_refs = refs[:packets]
    kv_refs = refs[packets : packets + blocks]
    out_refs = refs[-packets:]
    per = pk_refs[0].shape[1]
    dim = pk_refs[0].shape[3]
    q_rows = steps * heads * group
    rows = steps * group
    slots = [(ref, n) for ref in pk_refs for n in range(per)]
    limit = jnp.concatenate(
        [
            jnp.broadcast_to(ref[0, n, q_rows + 4 * steps : q_rows + 4 * steps + 1, 0:1], (rows, 1))
            for ref, n in slots
        ],
        axis=0,
    ).astype(jnp.int32)
    for head in range(heads):
        q = jnp.concatenate(
            [
                ref[0, n, 0:q_rows].reshape(steps, heads * group, dim)[:, head * group : (head + 1) * group].reshape(rows, dim)
                for ref, n in slots
            ],
            axis=0,
        )
        q6 = query_terms(q * scale)
        todo = []
        for b, ref in enumerate(kv_refs):
            k6 = key_terms(cache_head(ref, 0, head, heads))
            vv = value_terms(cache_head(ref, 1, head, heads))

            def visible(b=b, count=k6.shape[0]):
                pos = marks[1 + b] + lax.broadcasted_iota(jnp.int32, (q.shape[0], count), 1)
                return pos < limit

            todo.append((k6, vv, visible))
        drafts = [
            jnp.concatenate(
                [ref[0, n, pl.ds(q_rows + which * heads + head, steps, stride=2 * heads), :] for ref, n in slots], axis=0
            )
            for which in range(2)
        ]

        def causal(count=drafts[0].shape[0]):
            row = lax.broadcasted_iota(jnp.int32, (q.shape[0], count), 0)
            col = lax.broadcasted_iota(jnp.int32, (q.shape[0], count), 1)
            return (row // rows == col // steps) & (col % steps <= row % rows // group)

        groups = in_pairs(todo)
        groups[0] = groups[0] + [(key_terms(drafts[0]), value_terms(drafts[1]), causal)]
        out = attend(q6, groups)
        for i in range(packets):
            for n in range(per):
                at = (i * per + n) * rows
                for step in range(steps):
                    first = step * heads * group + head * group
                    out_refs[i][0, n, first : first + group] = out[at + step * group : at + (step + 1) * group]


def decode_request(index, marks, packets, kv_list, carried, heads, group, steps, scale):
    nreq, per, packet_rows, dim = packets[0].shape
    blocks = len(kv_list)
    count = len(packets)
    q_rows = steps * heads * group
    pk_spec = pl.BlockSpec((1, per, packet_rows, dim), lambda i, m: (index, 0, 0, 0))
    out_spec = pl.BlockSpec((1, per, q_rows, dim), lambda i, m: (index, 0, 0, 0))
    kv_specs = [pl.BlockSpec(kv.shape, lambda i, m: (0, 0, 0, 0)) for kv in kv_list]
    extra_specs, extra, alias = [], [], {}
    if carried is not None:
        extra_specs, extra = [pl.BlockSpec(memory_space=pl.ANY)] * count, list(carried)
        alias = {1 + count + blocks + i: i for i in range(count)}
    keys = sum(kv.shape[2] for kv in kv_list)
    return pl.pallas_call(
        functools.partial(decode_kernel, blocks, count, heads, group, steps, scale),
        grid_spec=pltpu.PrefetchScalarGridSpec(
            num_scalar_prefetch=1,
            grid=(1,),
            in_specs=[pk_spec] * count + kv_specs + extra_specs,
            out_specs=[out_spec] * count,
        ),
        out_shape=[jax.ShapeDtypeStruct((nreq, per, q_rows, dim), F32)] * count,
        input_output_aliases=alias,
        compiler_params=pltpu.CompilerParams(vmem_limit_bytes=40 * 2**20),
        cost_estimate=pl.CostEstimate(
            flops=2 * 10 * count * per * steps * group * keys * dim,
            bytes_accessed=4 * (2 * count * per * packet_rows * dim + 2 * keys * dim),
            transcendentals=count * per * steps * group * keys,
        ),
        name="decode",
    )(marks, *packets, *kv_list, *extra)


def place_kernel(count, at, *refs):
    o_ref = refs[-1]
    nreq = refs[0].shape[0]
    for i in range(count):
        o_ref[pl.ds(at[i] * nreq, nreq)] = refs[i][...]


def place(at, pieces):
    nreq, per, rows, dim = pieces[0].shape
    count = len(pieces)
    return pl.pallas_call(
        functools.partial(place_kernel, count),
        in_specs=[pl.BlockSpec(memory_space=pltpu.SMEM)] + [pl.BlockSpec(memory_space=pltpu.VMEM)] * count,
        out_specs=pl.BlockSpec(memory_space=pltpu.VMEM),
        out_shape=jax.ShapeDtypeStruct((count * nreq, per, rows, dim), F32),
        name="place",
    )(at, *pieces)


def on_device(kv_cache, prefill_q, decode_q, decode_kv, lengths, row_length):
    ctx_count, head_count, rep_count = lax.axis_size("ctx"), lax.axis_size("head"), lax.axis_size("rep")
    ctx_index, head_index, rep_index = lax.axis_index("ctx"), lax.axis_index("head"), lax.axis_index("rep")
    nreq, _, block_len, heads, dim = kv_cache.shape
    span = prefill_q.shape[1]
    group = prefill_q.shape[2] // heads
    requests, per, steps, q_heads, _ = decode_q.shape
    scale = LOG2E / math.sqrt(dim)

    flat = kv_cache.reshape(nreq, 2, block_len * heads, dim)
    own = [flat[i : i + 1] for i in range(nreq)]
    shifts = range(1, ctx_count)
    held = [[own[i]] for i in range(nreq)]
    for shift in shifts:
        perm = [((i + shift) % ctx_count, i) for i in range(ctx_count)]
        for i in range(nreq):
            held[i].append(lax.ppermute(own[i], "ctx", perm))
    starts = jnp.stack([(ctx_index + shift) % ctx_count * block_len for shift in range(ctx_count)]).astype(jnp.int32)

    rows_f = jnp.broadcast_to(row_length.astype(F32)[:, :, None, None], (requests, per, 8, dim))
    packet = jnp.concatenate(
        [
            decode_q.reshape(requests, per, steps * q_heads, dim),
            decode_kv.reshape(requests, per, steps * 2 * heads, dim),
            rows_f,
        ],
        axis=2,
    )
    targets = [(rep_index + k) % head_count for k in range(head_count)]
    routes = [
        [(s * rep_count + t, (t + k) % head_count * rep_count + s) for s in range(head_count) for t in range(rep_count)]
        for k in range(head_count)
    ]
    packets = [
        lax.ppermute(lax.dynamic_slice_in_dim(packet, targets[k] * nreq, nreq, 0), ("head", "rep"), routes[k])
        for k in range(head_count)
    ]

    results = None
    prefill_out = None
    for i in range(nreq):
        length = lengths[head_index * nreq + i]
        first = length - span * ctx_count + ctx_index * span
        marks = jnp.concatenate([first[None].astype(jnp.int32), starts])
        results = decode_request(i, marks, packets, held[i], results, heads, group, steps, scale)
        prefill_out = prefill_request(i, marks, prefill_q, held[i], prefill_out, heads, scale)
    homes = [
        lax.ppermute(results[k], ("head", "rep"), [(b, a) for a, b in routes[k]]) for k in range(head_count)
    ]
    decode_out = place(jnp.stack(targets).astype(jnp.int32), homes).reshape(decode_q.shape)
    return (prefill_out, decode_out)


def solution(mesh):
    in_specs = (
        P("head", None, "ctx", "rep", None),
        P("head", "ctx", "rep", None),
        P(None, ("ctx", "rep"), None, "head", None),
        P(None, ("ctx", "rep"), None, None, "head", None),
        P(),
        P(None, ("ctx", "rep")),
    )
    out_specs = (P("head", "ctx", "rep", None), P(None, ("ctx", "rep"), None, "head", None))
    return jax.shard_map(on_device, mesh=mesh, in_specs=in_specs, out_specs=out_specs, check_vma=False)
```

time: 286 us -> 54.9 us (0.19)
  the two profiles are of different devices: /device:TPU:7 before, /device:TPU:0 now
where the time goes in v1:
time: 54.9 us; the launch traced here: 54.7 us
  starting transfers between devices  17.5 us (32%)
  Pallas kernels  16.3 us (30%)
  waiting for transfers between devices  14.8 us (27%)
  local copies, waits for them, and re-layouts  3.31 us (6%)
  between operations  2.08 us (4%)
  other arithmetic  0.75 us (1%)
    pallas_call x2, Pallas kernels, prefill_request(): pl.pallas_call(functools.partial(prefill_kernel, blocks, heads, group, sc...  10.5 us
    ppermute x4, starting transfers between devices, on_device(): lax.ppermute(results[k], ('head', 'rep'), [(b, a) for a, b in routes[k]])  8.93 us
    ppermute x2, waiting for transfers between devices, on_device(): held[i].append(lax.ppermute(own[i], 'ctx', perm))  8.69 us
    ppermute x4, waiting for transfers between devices, on_device(): lax.ppermute(lax.dynamic_slice_in_dim(packet, targets[k] * nreq, nreq, 0)...  6.11 us
    ppermute x4, starting transfers between devices, on_device(): lax.ppermute(lax.dynamic_slice_in_dim(packet, targets[k] * nreq, nreq, 0)...  5.47 us
    pallas_call x2, Pallas kernels, decode_request(): pl.pallas_call(functools.partial(decode_kernel, blocks, count, heads, gro...  4.11 us
    ppermute x2, starting transfers between devices, on_device(): held[i].append(lax.ppermute(own[i], 'ctx', perm))  3.08 us
    pallas_call x1, Pallas kernels, place(): pl.pallas_call(functools.partial(place_kernel, count), in_specs=[pl.Block...  1.67 us
  transfers between devices with their start and end apart: 10, of which 2 were waited for; matrix products, arithmetic and copies ran while one was open for 3% of the time, Pallas kernels for 23%

profile of v1, /device:TPU:0, one launch (start us, length us, event | category | flops | bytes accessed | tf_op | source)
XLA Modules:
  0.0 54.7 jit_solution(10405196411491514836)
XLA Ops:
  0.6 0.0 copy-start.8
  0.6 0.0 copy-start.6
  0.7 0.0 copy-start.1
  0.7 0.0 copy-start.7
  0.7 1.3 %fusion = (f32[1,2,256,2,128]{4,3,2,1,0:T(2,128)S(1)}, f32[1,2,256,2,128]{4,3,2,1,0:T(2,128)S(1)}) fusion(f32[2,2,256,2,128]{4,3,2,1,0:T(2,128)} %param.6), kind=kLoop, calls=%fused_computation.9 | loop fusion | bytes 2097152 | tf_op jit(solution)/shard_map/slice | solution.py:255
  2.0 3.0 %collective-permute-start = (f32[1,2,512,128]{3,2,1,0:T(8,128)S(1)}, f32[1,2,512,128]{3,2,1,0:T(8,128)S(1)}, u32[]{:S(2)}, u32[]{:S(2)}) collective-permute-start(f32[1,2,512,128]{3,2,1,0:T(8,128)S(1)} %bitcast.22), channel_id=1, source_target_pairs={{16,0},{0,16},{17,1},{1,17},{18,2},{2,18},{19,3},{3,19},{20,4},{4,... | collective-permute-start | bytes 1572872 | tf_op jit(solution)/shard_map/ppermute | solution.py:261
  5.0 0.1 collective-permute-start.1
  5.1 0.0 copy-done.8
  5.1 0.1 broadcast_in_dim.17
  5.2 0.0 copy-done.6
  5.2 0.0 copy-done.1
  5.2 0.9 %collective-permute-start.5 = (f32[2,1,88,128]{3,2,1,0:T(8,128)S(1)}, f32[2,1,88,128]{3,2,1,0:T(8,128)S(1)}, u32[]{:S(2)}, u32[]{:S(2)}) collective-permute-start(f32[2,1,88,128]{3,2,1,0:T(8,128)S(1)} %get-tuple-element.22), channel_id=1, source_target_pairs={{0,12},{1,0},{2,4},{3,8},{4,13},{5,1},{6,5},{7,9},{8,14},{9,2},{10... | collective-permute-start | bytes 270344 | tf_op jit(solution)/shard_map/ppermute | solution.py:279
  6.2 2.6 %collective-permute-start.4 = (f32[2,1,88,128]{3,2,1,0:T(8,128)S(1)}, f32[2,1,88,128]{3,2,1,0:T(8,128)S(1)}, u32[]{:S(2)}, u32[]{:S(2)}) collective-permute-start(f32[2,1,88,128]{3,2,1,0:T(8,128)S(1)} %get-tuple-element.23), channel_id=1, source_target_pairs={{0,8},{1,12},{2,0},{3,4},{4,9},{5,13},{6,1},{7,5},{8,10},{9,14},{1... | collective-permute-start | bytes 270344 | tf_op jit(solution)/shard_map/ppermute | solution.py:279
  8.8 1.2 %collective-permute-start.3 = (f32[2,1,88,128]{3,2,1,0:T(8,128)S(1)}, f32[2,1,88,128]{3,2,1,0:T(8,128)S(1)}, u32[]{:S(2)}, u32[]{:S(2)}) collective-permute-start(f32[2,1,88,128]{3,2,1,0:T(8,128)S(1)} %get-tuple-element.24), channel_id=1, source_target_pairs={{0,4},{1,8},{2,12},{3,0},{4,5},{5,9},{6,13},{7,1},{8,6},{9,10},{10... | collective-permute-start | bytes 270344 | tf_op jit(solution)/shard_map/ppermute | solution.py:279
  9.9 0.0 copy-done.7
  9.9 0.6 %fusion.1 = (s32[1]{0:T(128)}, s32[1]{0:T(128)}) fusion(s32[8]{0:T(128)S(1)} %copy-done.7, s32[]{:T(128)S(6)} %select_n.48, s32[]{:T(128)S(6)} %select_n.45), kind=kLoop, calls=%fused_computation.10 | loop fusion | bytes 24 | tf_op jit(solution)/shard_map/dynamic_slice | solution.py:286
  11.8 0.0 copy-start
  11.8 0.1 add_add_fusion
  11.9 0.0 collective-permute-done.5.refs_3_
  11.9 0.8 %collective-permute-start.2 = (f32[2,1,88,128]{3,2,1,0:T(8,128)S(1)}, f32[2,1,88,128]{3,2,1,0:T(8,128)S(1)}, u32[]{:S(2)}, u32[]{:S(2)}) collective-permute-start(f32[2,1,88,128]{3,2,1,0:T(8,128)S(1)} %get-tuple-element.25), channel_id=1, source_target_pairs={{0,0},{1,4},{2,8},{3,12},{4,1},{5,5},{6,9},{7,13},{8,2},{9,6},{10,... | collective-permute-start | bytes 270344 | tf_op jit(solution)/shard_map/ppermute | solution.py:279
  12.7 0.6 %pad_add_fusion.at = s32[4]{0:T(128)} fusion(s32[1]{0:T(128)} %bitcast.11, s32[1]{0:T(128)} %bitcast.10, s32[1]{0:T(128)} %bitcast.9, s32[1]{0:T(128)} %bitcast.8), kind=kLoop, calls=%fused_computation.7 | loop fusion | flops 12 | bytes 32 | tf_op jit(solution)/shard_map/stack | solution.py:294
  13.4 6.1 %collective-permute-done.4.refs_2_ = f32[2,1,88,128]{3,2,1,0:T(8,128)S(1)} collective-permute-done((f32[2,1,88,128]{3,2,1,0:T(8,128)S(1)}, f32[2,1,88,128]{3,2,1,0:T(8,128)S(1)}, u32[]{:S(2)}, u32[]{:S(2)}) %collective-permute-start.4) | collective-permute-done | bytes 90144 | tf_op jit(solution)/shard_map/ppermute | solution.py:279
  19.5 0.0 collective-permute-done.3.refs_1_
  19.5 0.0 collective-permute-done.2.refs_0_
  19.5 8.7 %collective-permute-done.1.refs_1_.refs_5_ = f32[1,2,512,128]{3,2,1,0:T(8,128)S(1)} collective-permute-done((f32[1,2,512,128]{3,2,1,0:T(8,128)S(1)}, f32[1,2,512,128]{3,2,1,0:T(8,128)S(1)}, u32[]{:S(2)}, u32[]{:S(2)}) %collective-permute-start.1) | collective-permute-done | bytes 524320 | tf_op jit(solution)/shard_map/ppermute | solution.py:261
  28.2 2.0 %decode.2 = (f32[2,1,64,128]{3,2,1,0:T(8,128)S(1)}, f32[2,1,64,128]{3,2,1,0:T(8,128)S(1)}, f32[2,1,64,128]{3,2,1,0:T(8,128)S(1)}, f32[2,1,64,128]{3,2,1,0:T(8,128)S(1)}) custom-call(s32[3]{0:T(128)S(1)} %get-tuple-element.29.marks, f32[2,1,88,128]{3,2,1,0:T(8,128)S(1)} %collective-permute-done.2.refs_0_, ...), custom_call_target="tpu_custom_call" | custom-call | flops 335544320 | bytes 1409024 | tf_op jit(solution)/shard_map/decode/pallas_call | solution.py:206
  30.2 0.0 collective-permute-done.refs_1_.refs_5_
  30.2 2.1 %decode.3 = (f32[2,1,64,128]{3,2,1,0:T(8,128)S(1)}, f32[2,1,64,128]{3,2,1,0:T(8,128)S(1)}, f32[2,1,64,128]{3,2,1,0:T(8,128)S(1)}, f32[2,1,64,128]{3,2,1,0:T(8,128)S(1)}) custom-call(s32[3]{0:T(128)S(1)} %get-tuple-element.28.marks, ...), custom_call_target="tpu_custom_call", output_to_operand_aliasing={{0}: (7, {}), {1}: (8, {}), {2}: (9, {}), {3}: (10, {})} | custom-call | flops 335544320 | bytes 1409024 | tf_op jit(solution)/shard_map/decode/pallas_call | solution.py:206
  32.3 0.7 %collective-permute-start.6 = (f32[2,1,64,128]{3,2,1,0:T(8,128)S(1)}, f32[2,1,64,128]{3,2,1,0:T(8,128)S(1)}, u32[]{:S(2)}, u32[]{:S(2)}) collective-permute-start(f32[2,1,64,128]{3,2,1,0:T(8,128)S(1)} %get-tuple-element.14), channel_id=1, source_target_pairs={{0,0},{4,1},{8,2},{12,3},{1,4},{5,5},{9,6},{13,7},{2,8},{6,9},{10,... | collective-permute-start | bytes 196616 | tf_op jit(solution)/shard_map/ppermute | solution.py:292
  33.0 5.2 %collective-permute-start.7 = (f32[2,1,64,128]{3,2,1,0:T(8,128)S(1)}, f32[2,1,64,128]{3,2,1,0:T(8,128)S(1)}, u32[]{:S(2)}, u32[]{:S(2)}) collective-permute-start(f32[2,1,64,128]{3,2,1,0:T(8,128)S(1)} %get-tuple-element.15), channel_id=1, source_target_pairs={{4,0},{8,1},{12,2},{0,3},{5,4},{9,5},{13,6},{1,7},{6,8},{10,9},{14... | collective-permute-start | bytes 196616 | tf_op jit(solution)/shard_map/ppermute | solution.py:292
  38.1 1.5 %collective-permute-start.8 = (f32[2,1,64,128]{3,2,1,0:T(8,128)S(1)}, f32[2,1,64,128]{3,2,1,0:T(8,128)S(1)}, u32[]{:S(2)}, u32[]{:S(2)}) collective-permute-start(f32[2,1,64,128]{3,2,1,0:T(8,128)S(1)} %get-tuple-element.16), channel_id=1, source_target_pairs={{8,0},{12,1},{0,2},{4,3},{9,4},{13,5},{1,6},{5,7},{10,8},{14,9},{2... | collective-permute-start | bytes 196616 | tf_op jit(solution)/shard_map/ppermute | solution.py:292
  39.7 1.6 %collective-permute-start.9 = (f32[2,1,64,128]{3,2,1,0:T(8,128)S(1)}, f32[2,1,64,128]{3,2,1,0:T(8,128)S(1)}, u32[]{:S(2)}, u32[]{:S(2)}) collective-permute-start(f32[2,1,64,128]{3,2,1,0:T(8,128)S(1)} %get-tuple-element.17), channel_id=1, source_target_pairs={{12,0},{0,1},{4,2},{8,3},{13,4},{1,5},{5,6},{9,7},{14,8},{2,9},{6,... | collective-permute-start | bytes 196616 | tf_op jit(solution)/shard_map/ppermute | solution.py:292
  41.2 0.0 copy-done
  41.2 5.2 %prefill.2.refs_2_ = f32[2,128,16,128]{3,2,1,0:T(8,128)} custom-call(s32[3]{0:T(128)S(1)} %get-tuple-element.29.marks, f32[2,128,16,128]{3,2,1,0:T(8,128)S(1)} %copy-done, f32[1,2,512,128]{3,2,1,0:T(8,128)S(1)} %bitcast.21, f32[1,2,512,128]{3,2,1,0:T(8,128)S(1)} %collective-permute-done.1.refs_1_.refs_5_), custom_call_target="tpu_custom_call" | custom-call | flops 2684354560 | bytes 3145728 | tf_op jit(solution)/shard_map/prefill/pallas_call | solution.py:115
  46.5 5.2 %prefill.3 = f32[2,128,16,128]{3,2,1,0:T(8,128)} custom-call(s32[3]{0:T(128)S(1)} %get-tuple-element.28.marks, f32[2,128,16,128]{3,2,1,0:T(8,128)S(1)} %copy-done, f32[1,2,512,128]{3,2,1,0:T(8,128)S(1)} %bitcast.24, f32[1,2,512,128]{3,2,1,0:T(8,128)S(1)} %collective-permute-done.refs_1_.refs_5_, ...), custom_call_target="tpu_custom_call", output_to_operand_aliasing={{}: (4, {})} | custom-call | flops 2684354560 | bytes 3145728 | tf_op jit(solution)/shard_map/prefill/pallas_call | solution.py:115
  51.7 0.0 collective-permute-done.6.refs_0_
  51.7 0.0 copy-start.2
  51.7 0.0 collective-permute-done.7.refs_1_
  51.7 0.0 copy-start.3
  51.7 0.0 collective-permute-done.8.refs_2_
  51.8 0.0 copy-start.4
  51.8 0.0 collective-permute-done.9.refs_3_
  51.8 0.6 %copy-done.2 = f32[2,1,64,128]{3,2,1,0:T(8,128)} copy-done((f32[2,1,64,128]{3,2,1,0:T(8,128)}, f32[2,1,64,128]{3,2,1,0:T(8,128)S(1)}, u32[]{:S(2)}) %copy-start.2) | copy-done | bytes 65560
  52.4 0.0 copy-done.3
  52.4 0.0 copy-done.4
  52.4 0.0 copy-start.5
  52.4 0.6 %copy-done.5 = f32[2,1,64,128]{3,2,1,0:T(8,128)} copy-done((f32[2,1,64,128]{3,2,1,0:T(8,128)}, f32[2,1,64,128]{3,2,1,0:T(8,128)S(1)}, u32[]{:S(2)}) %copy-start.5) | copy-done | bytes 65560
  53.0 1.7 %place.1 = f32[8,1,64,128]{3,2,1,0:T(8,128)} custom-call(s32[4]{0:T(128)} %pad_add_fusion.at, f32[2,1,64,128]{3,2,1,0:T(8,128)} %copy-done.2, f32[2,1,64,128]{3,2,1,0:T(8,128)} %copy-done.3, f32[2,1,64,128]{3,2,1,0:T(8,128)} %copy-done.4, f32[2,1,64,128]{3,2,1,0:T(8,128)} %copy-done.5), custom_call_target="tpu_custom_call" | custom-call | tf_op jit(solution)/shard_map/place/pallas_call | solution.py:236
  (3 shorter events, 0.1 us)
Async XLA Ops:
  0.6 4.5 %copy-start.8 = (s32[8,1]{0,1:T(1,128)S(1)}, s32[8,1]{0,1:T(1,128)}, u32[]{:S(2)}) copy-start(s32[8,1]{0,1:T(1,128)} %param.11) | copy-start | bytes 100
  0.6 4.5 %copy-start.6 = (f32[8,1,4,2,2,128]{5,4,3,2,1,0:T(2,128)S(1)}, f32[8,1,4,2,2,128]{5,4,3,2,1,0:T(2,128)}, u32[]{:S(2)}) copy-start(f32[8,1,4,2,2,128]{5,4,3,2,1,0:T(2,128)} %param.9) | copy-start | bytes 196612
  0.7 4.5 %copy-start.1 = (f32[8,1,4,16,128]{4,3,2,1,0:T(8,128)S(1)}, f32[8,1,4,16,128]{4,3,2,1,0:T(8,128)}, u32[]{:S(2)}) copy-start(f32[8,1,4,16,128]{4,3,2,1,0:T(8,128)} %param.8) | copy-start | bytes 786436
  0.7 9.3 %copy-start.7 = (s32[8]{0:T(128)S(1)}, s32[8]{0:T(128)}, u32[]{:S(2)}) copy-start(s32[8]{0:T(128)} %param.10) | copy-start | bytes 100
  2.0 28.2 %collective-permute-start = (f32[1,2,512,128]{3,2,1,0:T(8,128)S(1)}, f32[1,2,512,128]{3,2,1,0:T(8,128)S(1)}, u32[]{:S(2)}, u32[]{:S(2)}) collective-permute-start(f32[1,2,512,128]{3,2,1,0:T(8,128)S(1)} %bitcast.22), channel_id=1, source_target_pairs={{16,0},{0,16},{17,1},{1,17},{18,2},{2,18},{19,3},{3,19},{20,4},{4,... | collective-permute-start | bytes 1572872 | tf_op jit(solution)/shard_map/ppermute | solution.py:261
  5.0 23.2 %collective-permute-start.1 = (f32[1,2,512,128]{3,2,1,0:T(8,128)S(1)}, f32[1,2,512,128]{3,2,1,0:T(8,128)S(1)}, u32[]{:S(2)}, u32[]{:S(2)}) collective-permute-start(f32[1,2,512,128]{3,2,1,0:T(8,128)S(1)} %bitcast.19), channel_id=1, source_target_pairs={{16,0},{0,16},{17,1},{1,17},{18,2},{2,18},{19,3},{3,19},{20,4},{4,... | collective-permute-start | bytes 1572872 | tf_op jit(solution)/shard_map/ppermute | solution.py:261
  5.2 6.7 %collective-permute-start.5 = (f32[2,1,88,128]{3,2,1,0:T(8,128)S(1)}, f32[2,1,88,128]{3,2,1,0:T(8,128)S(1)}, u32[]{:S(2)}, u32[]{:S(2)}) collective-permute-start(f32[2,1,88,128]{3,2,1,0:T(8,128)S(1)} %get-tuple-element.22), channel_id=1, source_target_pairs={{0,12},{1,0},{2,4},{3,8},{4,13},{5,1},{6,5},{7,9},{8,14},{9,2},{10... | collective-permute-start | bytes 270344 | tf_op jit(solution)/shard_map/ppermute | solution.py:279
  6.2 13.3 %collective-permute-start.4 = (f32[2,1,88,128]{3,2,1,0:T(8,128)S(1)}, f32[2,1,88,128]{3,2,1,0:T(8,128)S(1)}, u32[]{:S(2)}, u32[]{:S(2)}) collective-permute-start(f32[2,1,88,128]{3,2,1,0:T(8,128)S(1)} %get-tuple-element.23), channel_id=1, source_target_pairs={{0,8},{1,12},{2,0},{3,4},{4,9},{5,13},{6,1},{7,5},{8,10},{9,14},{1... | collective-permute-start | bytes 270344 | tf_op jit(solution)/shard_map/ppermute | solution.py:279
  8.8 10.7 %collective-permute-start.3 = (f32[2,1,88,128]{3,2,1,0:T(8,128)S(1)}, f32[2,1,88,128]{3,2,1,0:T(8,128)S(1)}, u32[]{:S(2)}, u32[]{:S(2)}) collective-permute-start(f32[2,1,88,128]{3,2,1,0:T(8,128)S(1)} %get-tuple-element.24), channel_id=1, source_target_pairs={{0,4},{1,8},{2,12},{3,0},{4,5},{5,9},{6,13},{7,1},{8,6},{9,10},{10... | collective-permute-start | bytes 270344 | tf_op jit(solution)/shard_map/ppermute | solution.py:279
  11.8 29.4 %copy-start = (f32[2,128,16,128]{3,2,1,0:T(8,128)S(1)}, f32[2,128,16,128]{3,2,1,0:T(8,128)}, u32[]{:S(2)}) copy-start(f32[2,128,16,128]{3,2,1,0:T(8,128)} %q_ref.3) | copy-start | bytes 6291460
  11.9 7.5 %collective-permute-start.2 = (f32[2,1,88,128]{3,2,1,0:T(8,128)S(1)}, f32[2,1,88,128]{3,2,1,0:T(8,128)S(1)}, u32[]{:S(2)}, u32[]{:S(2)}) collective-permute-start(f32[2,1,88,128]{3,2,1,0:T(8,128)S(1)} %get-tuple-element.25), channel_id=1, source_target_pairs={{0,0},{1,4},{2,8},{3,12},{4,1},{5,5},{6,9},{7,13},{8,2},{9,6},{10,... | collective-permute-start | bytes 270344 | tf_op jit(solution)/shard_map/ppermute | solution.py:279
  32.3 19.4 %collective-permute-start.6 = (f32[2,1,64,128]{3,2,1,0:T(8,128)S(1)}, f32[2,1,64,128]{3,2,1,0:T(8,128)S(1)}, u32[]{:S(2)}, u32[]{:S(2)}) collective-permute-start(f32[2,1,64,128]{3,2,1,0:T(8,128)S(1)} %get-tuple-element.14), channel_id=1, source_target_pairs={{0,0},{4,1},{8,2},{12,3},{1,4},{5,5},{9,6},{13,7},{2,8},{6,9},{10,... | collective-permute-start | bytes 196616 | tf_op jit(solution)/shard_map/ppermute | solution.py:292
  33.0 18.8 %collective-permute-start.7 = (f32[2,1,64,128]{3,2,1,0:T(8,128)S(1)}, f32[2,1,64,128]{3,2,1,0:T(8,128)S(1)}, u32[]{:S(2)}, u32[]{:S(2)}) collective-permute-start(f32[2,1,64,128]{3,2,1,0:T(8,128)S(1)} %get-tuple-element.15), channel_id=1, source_target_pairs={{4,0},{8,1},{12,2},{0,3},{5,4},{9,5},{13,6},{1,7},{6,8},{10,9},{14... | collective-permute-start | bytes 196616 | tf_op jit(solution)/shard_map/ppermute | solution.py:292
  38.1 13.6 %collective-permute-start.8 = (f32[2,1,64,128]{3,2,1,0:T(8,128)S(1)}, f32[2,1,64,128]{3,2,1,0:T(8,128)S(1)}, u32[]{:S(2)}, u32[]{:S(2)}) collective-permute-start(f32[2,1,64,128]{3,2,1,0:T(8,128)S(1)} %get-tuple-element.16), channel_id=1, source_target_pairs={{8,0},{12,1},{0,2},{4,3},{9,4},{13,5},{1,6},{5,7},{10,8},{14,9},{2... | collective-permute-start | bytes 196616 | tf_op jit(solution)/shard_map/ppermute | solution.py:292
  39.7 12.1 %collective-permute-start.9 = (f32[2,1,64,128]{3,2,1,0:T(8,128)S(1)}, f32[2,1,64,128]{3,2,1,0:T(8,128)S(1)}, u32[]{:S(2)}, u32[]{:S(2)}) collective-permute-start(f32[2,1,64,128]{3,2,1,0:T(8,128)S(1)} %get-tuple-element.17), channel_id=1, source_target_pairs={{12,0},{0,1},{4,2},{8,3},{13,4},{1,5},{5,6},{9,7},{14,8},{2,9},{6,... | collective-permute-start | bytes 196616 | tf_op jit(solution)/shard_map/ppermute | solution.py:292
  51.7 0.6 %copy-start.2 = (f32[2,1,64,128]{3,2,1,0:T(8,128)}, f32[2,1,64,128]{3,2,1,0:T(8,128)S(1)}, u32[]{:S(2)}) copy-start(f32[2,1,64,128]{3,2,1,0:T(8,128)S(1)} %collective-permute-done.6.refs_0_) | copy-start | bytes 196612
  51.7 0.6 %copy-start.3 = (f32[2,1,64,128]{3,2,1,0:T(8,128)}, f32[2,1,64,128]{3,2,1,0:T(8,128)S(1)}, u32[]{:S(2)}) copy-start(f32[2,1,64,128]{3,2,1,0:T(8,128)S(1)} %collective-permute-done.7.refs_1_) | copy-start | bytes 196612
  51.8 0.7 %copy-start.4 = (f32[2,1,64,128]{3,2,1,0:T(8,128)}, f32[2,1,64,128]{3,2,1,0:T(8,128)S(1)}, u32[]{:S(2)}) copy-start(f32[2,1,64,128]{3,2,1,0:T(8,128)S(1)} %collective-permute-done.8.refs_2_) | copy-start | bytes 196612
  52.4 0.6 %copy-start.5 = (f32[2,1,64,128]{3,2,1,0:T(8,128)}, f32[2,1,64,128]{3,2,1,0:T(8,128)S(1)}, u32[]{:S(2)}) copy-start(f32[2,1,64,128]{3,2,1,0:T(8,128)S(1)} %collective-permute-done.9.refs_3_) | copy-start | bytes 196612

commit v2 on v1

--- a/solution.py
+++ b/solution.py
@@ -51,8 +51,7 @@
     return both[:, :half] + both[:, half:]
 
 
-def attend(q6, groups):
-    state = None
+def attend(q6, groups, state=None):
     for group in groups:
         parts = [jnp.where(mask(), scores_of(q6, k6), NEG_FILL) for k6, _, mask in group]
         top = functools.reduce(jnp.maximum, [jnp.max(s, axis=-1, keepdims=True) for s in parts])
@@ -66,7 +65,20 @@
             total = total + state[1] * factor
             acc = acc + state[2] * factor
         state = (top, total, acc)
-    return state[2] / state[1]
+    return state
+
+
+def put_state(state, acc_ref, stat_ref, at):
+    top, total, acc = state
+    acc_ref[at] = acc
+    lane = lax.broadcasted_iota(jnp.int32, acc.shape, 1)
+    stat_ref[at] = jnp.where(lane < acc.shape[1] // 2, top, total)
+
+
+def get_state(acc_ref, stat_ref, at):
+    stats = stat_ref[at]
+    half = stats.shape[1] // 2
+    return stats[:, 0:1], stats[:, half : half + 1], acc_ref[at]
 
 
 def in_pairs(blocks):
@@ -78,8 +90,11 @@
     return ref[0, which, pl.ds(head, rows, stride=heads), :]
 
 
-def prefill_kernel(blocks, heads, group, scale, marks, q_ref, *refs):
-    kv_refs, o_ref = refs[:blocks], refs[-1]
+def prefill_kernel(plan, heads, group, scale, marks, q_ref, *refs):
+    blocks, first_block, started, finish, unread = plan
+    kv_refs, refs = refs[:blocks], refs[blocks:]
+    state_in = refs[:2] if started else None
+    outs = refs[(2 if started else 0) + unread :]
     span = q_ref.shape[1]
     dim = q_ref.shape[3]
     head = pl.program_id(0)
@@ -89,72 +104,81 @@
     for first in range(0, span, chunk):
         q = q_ref[0, first : first + chunk].reshape(chunk * group, dim) * scale
         q6 = query_terms(q)
+        at = (0, pl.ds(first * group, chunk * group))
 
         def mask_of(b, first=first):
             shape = (chunk * group, keys[b].shape[0])
-            pos = marks[1 + b] + lax.broadcasted_iota(jnp.int32, shape, 1)
+            pos = marks[1 + first_block + b] + lax.broadcasted_iota(jnp.int32, shape, 1)
             row = lax.broadcasted_iota(jnp.int32, shape, 0) // group
             return pos <= row + (marks[0] + first)
 
         todo = [(keys[b], vals[b], functools.partial(mask_of, b)) for b in range(blocks)]
-        out = attend(q6, in_pairs(todo))
-        o_ref[0, first : first + chunk] = out.reshape(chunk, group, dim)
-
-
-def prefill_request(index, marks, prefill_q, kv_list, carried, heads, scale):
+        state = attend(q6, in_pairs(todo), get_state(*state_in, at) if started else None)
+        if finish:
+            outs[0][0, first : first + chunk] = (state[2] / state[1]).reshape(chunk, group, dim)
+        else:
+            put_state(state, outs[0], outs[1], at)
+    if finish:
+        outs[1][...] = jnp.zeros_like(outs[1])
+
+
+def prefill_request(index, marks, prefill_q, kv_list, first_block, heads, scale, state=None, finish=True, carried=None, after=()):
     nreq, span, q_heads, dim = prefill_q.shape
     group = q_heads // heads
     blocks = len(kv_list)
     q_spec = pl.BlockSpec((1, span, group, dim), lambda k, m: (index, 0, k, 0))
     kv_specs = [pl.BlockSpec(kv.shape, lambda k, m: (0, 0, 0, 0)) for kv in kv_list]
-    extra_specs, extra, alias = [], [], {}
-    if carried is not None:
-        extra_specs, extra = [pl.BlockSpec(memory_space=pl.ANY)], [carried]
-        alias = {2 + blocks: 0}
-    keys = sum(kv.shape[2] for kv in kv_list)
+    state_spec = pl.BlockSpec((1, span * group, dim), lambda k, m: (k, 0, 0))
+    state_shape = jax.ShapeDtypeStruct((heads, span * group, dim), F32)
+    started = state is not None
+    state = list(state) if started else []
+    unread = list(after) + ([carried] if carried is not None else [])
+    alias = {2 + blocks + len(state) + len(after): 0} if carried is not None else {}
+    keys = sum(kv.shape[2] for kv in kv_list) // heads
+    if finish:
+        out_specs = [q_spec, pl.BlockSpec((8, 128), lambda k, m: (0, 0))]
+        out_shape = [jax.ShapeDtypeStruct(prefill_q.shape, F32), jax.ShapeDtypeStruct((8, 128), F32)]
+    else:
+        out_specs = [state_spec, state_spec]
+        out_shape = [state_shape, state_shape]
     return pl.pallas_call(
-        functools.partial(prefill_kernel, blocks, heads, group, scale),
+        functools.partial(prefill_kernel, (blocks, first_block, started, finish, len(unread)), heads, group, scale),
         grid_spec=pltpu.PrefetchScalarGridSpec(
             num_scalar_prefetch=1,
             grid=(heads,),
-            in_specs=[q_spec] + kv_specs + extra_specs,
-            out_specs=q_spec,
-        ),
-        out_shape=jax.ShapeDtypeStruct(prefill_q.shape, F32),
+            in_specs=[q_spec] + kv_specs + [state_spec] * len(state) + [pl.BlockSpec(memory_space=pl.ANY)] * len(unread),
+            out_specs=out_specs,
+        ),
+        out_shape=out_shape,
         input_output_aliases=alias,
-        compiler_params=pltpu.CompilerParams(vmem_limit_bytes=40 * 2**20),
+        compiler_params=pltpu.CompilerParams(vmem_limit_bytes=32 * 2**20),
         cost_estimate=pl.CostEstimate(
-            flops=2 * 10 * span * group * keys * dim,
-            bytes_accessed=4 * (2 * span * q_heads * dim + 2 * keys * dim),
-            transcendentals=span * group * keys,
+            flops=span * q_heads * keys * dim,
+            bytes_accessed=4 * (2 * span * q_heads * dim + 2 * heads * keys * dim),
+            transcendentals=span * q_heads * keys,
         ),
         name="prefill",
-    )(marks, prefill_q, *kv_list, *extra)
-
-
-def decode_kernel(blocks, packets, heads, group, steps, scale, marks, *refs):
-    pk_refs = refs[:packets]
-    kv_refs = refs[packets : packets + blocks]
-    out_refs = refs[-packets:]
+    )(marks, prefill_q, *kv_list, *state, *unread)
+
+
+def decode_kernel(plan, heads, group, steps, scale, marks, *refs):
+    packets, blocks, first_block, started, finish, unread = plan
+    pk_refs, kv_refs, refs = refs[:packets], refs[packets : packets + blocks], refs[packets + blocks :]
+    state_in = refs[:2] if started else None
+    outs = refs[(2 if started else 0) + unread :]
     per = pk_refs[0].shape[1]
     dim = pk_refs[0].shape[3]
     q_rows = steps * heads * group
     rows = steps * group
     slots = [(ref, n) for ref in pk_refs for n in range(per)]
+    at_limit = q_rows + 2 * heads * steps
     limit = jnp.concatenate(
-        [
-            jnp.broadcast_to(ref[0, n, q_rows + 4 * steps : q_rows + 4 * steps + 1, 0:1], (rows, 1))
-            for ref, n in slots
-        ],
-        axis=0,
+        [jnp.broadcast_to(ref[0, n, at_limit : at_limit + 1, 0:1], (rows, 1)) for ref, n in slots], axis=0
     ).astype(jnp.int32)
     for head in range(heads):
+        own = slice(head * group, (head + 1) * group)
         q = jnp.concatenate(
-            [
-                ref[0, n, 0:q_rows].reshape(steps, heads * group, dim)[:, head * group : (head + 1) * group].reshape(rows, dim)
-                for ref, n in slots
-            ],
-            axis=0,
+            [ref[0, n, 0:q_rows].reshape(steps, heads * group, dim)[:, own].reshape(rows, dim) for ref, n in slots], axis=0
         )
         q6 = query_terms(q * scale)
         todo = []
@@ -163,64 +187,85 @@
             vv = value_terms(cache_head(ref, 1, head, heads))
 
             def visible(b=b, count=k6.shape[0]):
-                pos = marks[1 + b] + lax.broadcasted_iota(jnp.int32, (q.shape[0], count), 1)
+                pos = marks[1 + first_block + b] + lax.broadcasted_iota(jnp.int32, (q.shape[0], count), 1)
                 return pos < limit
 
             todo.append((k6, vv, visible))
-        drafts = [
-            jnp.concatenate(
-                [ref[0, n, pl.ds(q_rows + which * heads + head, steps, stride=2 * heads), :] for ref, n in slots], axis=0
-            )
-            for which in range(2)
-        ]
-
-        def causal(count=drafts[0].shape[0]):
-            row = lax.broadcasted_iota(jnp.int32, (q.shape[0], count), 0)
-            col = lax.broadcasted_iota(jnp.int32, (q.shape[0], count), 1)
-            return (row // rows == col // steps) & (col % steps <= row % rows // group)
-
         groups = in_pairs(todo)
-        groups[0] = groups[0] + [(key_terms(drafts[0]), value_terms(drafts[1]), causal)]
-        out = attend(q6, groups)
+        if not started:
+            drafts = [
+                jnp.concatenate(
+                    [ref[0, n, pl.ds(q_rows + which * heads + head, steps, stride=2 * heads), :] for ref, n in slots], axis=0
+                )
+                for which in range(2)
+            ]
+
+            def causal(count=drafts[0].shape[0]):
+                row = lax.broadcasted_iota(jnp.int32, (q.shape[0], count), 0)
+                col = lax.broadcasted_iota(jnp.int32, (q.shape[0], count), 1)
+                return (row // rows == col // steps) & (col % steps <= row % rows // group)
+
+            groups[0] = groups[0] + [(key_terms(drafts[0]), value_terms(drafts[1]), causal)]
+        state = attend(q6, groups, get_state(*state_in, head) if started else None)
+        if not finish:
+            put_state(state, outs[0], outs[1], head)
+            continue
+        out = state[2] / state[1]
         for i in range(packets):
             for n in range(per):
                 at = (i * per + n) * rows
                 for step in range(steps):
                     first = step * heads * group + head * group
-                    out_refs[i][0, n, first : first + group] = out[at + step * group : at + (step + 1) * group]
-
-
-def decode_request(index, marks, packets, kv_list, carried, heads, group, steps, scale):
+                    outs[i][0, n, first : first + group] = out[at + step * group : at + (step + 1) * group]
+
+
+def decode_request(
+    index, marks, packets, kv_list, first_block, heads, group, steps, scale, state=None, finish=True, carried=None, after=()
+):
     nreq, per, packet_rows, dim = packets[0].shape
     blocks = len(kv_list)
     count = len(packets)
     q_rows = steps * heads * group
+    all_rows = count * per * steps * group
     pk_spec = pl.BlockSpec((1, per, packet_rows, dim), lambda i, m: (index, 0, 0, 0))
     out_spec = pl.BlockSpec((1, per, q_rows, dim), lambda i, m: (index, 0, 0, 0))
     kv_specs = [pl.BlockSpec(kv.shape, lambda i, m: (0, 0, 0, 0)) for kv in kv_list]
-    extra_specs, extra, alias = [], [], {}
-    if carried is not None:
-        extra_specs, extra = [pl.BlockSpec(memory_space=pl.ANY)] * count, list(carried)
-        alias = {1 + count + blocks + i: i for i in range(count)}
-    keys = sum(kv.shape[2] for kv in kv_list)
+    state_spec = pl.BlockSpec((heads, all_rows, dim), lambda i, m: (0, 0, 0))
+    started = state is not None
+    state = list(state) if started else []
+    unread = list(after) + (list(carried) if carried is not None else [])
+    before = 1 + count + blocks + len(state) + len(after)
+    alias = {before + i: i for i in range(count)} if carried is not None else {}
+    if finish:
+        out_specs = [out_spec] * count
+        out_shape = [jax.ShapeDtypeStruct((nreq, per, q_rows, dim), F32)] * count
+    else:
+        out_specs = [state_spec] * 2
+        out_shape = [jax.ShapeDtypeStruct((heads, all_rows, dim), F32)] * 2
+    keys = sum(kv.shape[2] for kv in kv_list) // heads
     return pl.pallas_call(
-        functools.partial(decode_kernel, blocks, count, heads, group, steps, scale),
+        functools.partial(
+            decode_kernel, (count, blocks, first_block, started, finish, len(unread)), heads, group, steps, scale
+        ),
         grid_spec=pltpu.PrefetchScalarGridSpec(
             num_scalar_prefetch=1,
             grid=(1,),
-            in_specs=[pk_spec] * count + kv_specs + extra_specs,
-            out_specs=[out_spec] * count,
-        ),
-        out_shape=[jax.ShapeDtypeStruct((nreq, per, q_rows, dim), F32)] * count,
+            in_specs=[pk_spec] * count
+            + kv_specs
+            + [state_spec] * len(state)
+            + [pl.BlockSpec(memory_space=pl.ANY)] * len(unread),
+            out_specs=out_specs,
+        ),
+        out_shape=out_shape,
         input_output_aliases=alias,
-        compiler_params=pltpu.CompilerParams(vmem_limit_bytes=40 * 2**20),
+        compiler_params=pltpu.CompilerParams(vmem_limit_bytes=16 * 2**20),
         cost_estimate=pl.CostEstimate(
-            flops=2 * 10 * count * per * steps * group * keys * dim,
-            bytes_accessed=4 * (2 * count * per * packet_rows * dim + 2 * keys * dim),
-            transcendentals=count * per * steps * group * keys,
+            flops=all_rows * heads * keys * dim,
+            bytes_accessed=4 * (2 * count * per * packet_rows * dim + 2 * heads * keys * dim),
+            transcendentals=all_rows * heads * keys,
         ),
         name="decode",
-    )(marks, *packets, *kv_list, *extra)
+    )(marks, *packets, *kv_list, *state, *unread)
 
 
 def place_kernel(count, at, *refs):
@@ -238,6 +283,7 @@
         in_specs=[pl.BlockSpec(memory_space=pltpu.SMEM)] + [pl.BlockSpec(memory_space=pltpu.VMEM)] * count,
         out_specs=pl.BlockSpec(memory_space=pltpu.VMEM),
         out_shape=jax.ShapeDtypeStruct((count * nreq, per, rows, dim), F32),
+        compiler_params=pltpu.CompilerParams(vmem_limit_bytes=8 * 2**20),
         name="place",
     )(at, *pieces)
 
@@ -280,14 +326,27 @@
         for k in range(head_count)
     ]
 
-    results = None
-    prefill_out = None
-    for i in range(nreq):
+    def marks_of(i):
         length = lengths[head_index * nreq + i]
         first = length - span * ctx_count + ctx_index * span
-        marks = jnp.concatenate([first[None].astype(jnp.int32), starts])
-        results = decode_request(i, marks, packets, held[i], results, heads, group, steps, scale)
-        prefill_out = prefill_request(i, marks, prefill_q, held[i], prefill_out, heads, scale)
+        return jnp.concatenate([first[None].astype(jnp.int32), starts])
+
+    last = nreq - 1
+    last_marks = marks_of(last)
+    prefill_state = prefill_request(last, last_marks, prefill_q, held[last][:1], 0, heads, scale, finish=False)
+    results, prefill_out, token = None, None, None
+    for i in range(last):
+        marks = marks_of(i)
+        prefill_out, token = prefill_request(i, marks, prefill_q, held[i], 0, heads, scale, carried=prefill_out)
+        results = decode_request(i, marks, packets, held[i], 0, heads, group, steps, scale, carried=results)
+    decode_state = decode_request(last, last_marks, packets, held[last][:1], 0, heads, group, steps, scale, finish=False)
+    results = decode_request(
+        last, last_marks, packets, held[last][1:], 1, heads, group, steps, scale,
+        state=decode_state, carried=results, after=(token, prefill_state[0]),
+    )
+    prefill_out, _ = prefill_request(
+        last, last_marks, prefill_q, held[last][1:], 1, heads, scale, state=prefill_state, carried=prefill_out
+    )
     homes = [
         lax.ppermute(results[k], ("head", "rep"), [(b, a) for a, b in routes[k]]) for k in range(head_count)
     ]

time: 54.9 us -> 61.1 us (1.11)
  Pallas kernels: 16.3 us -> 28.9 us
  waiting for transfers between devices: 14.8 us -> 4.08 us
  starting transfers between devices: 17.5 us -> 22.6 us
    pallas_call x4 -> x6, Pallas kernels: 14.6 us -> 27.6 us  [the longest x3 20 us: prefill_request(): pl.pallas_call(functools.partial(prefill_kernel, (blocks, first_block, st...]
    ppermute x2, waiting for transfers between devices: 8.69 us -> 0.01 us  [on_device(): held[i].append(lax.ppermute(own[i], 'ctx', perm))]
    ppermute x4, starting transfers between devices: 5.47 us -> 9.01 us  [on_device(): lax.ppermute(lax.dynamic_slice_in_dim(packet, targets[k] * nreq, nreq, 0)...]
    ppermute x4, waiting for transfers between devices: 6.11 us -> 4.06 us  [on_device(): lax.ppermute(lax.dynamic_slice_in_dim(packet, targets[k] * nreq, nreq, 0)...]
    ppermute x4, starting transfers between devices: 8.93 us -> 10.5 us  [on_device(): lax.ppermute(results[k], ('head', 'rep'), [(b, a) for a, b in routes[k]])]
    unnamed x18 -> x10, local copies, waits for them, and re-layouts: 1.29 us -> 0.02 us
    dynamic_slice x1, local copies, waits for them, and re-layouts: 0.04 us -> 0.72 us  [on_device(): lax.dynamic_slice_in_dim(packet, targets[k] * nreq, nreq, 0)]
  transfers between devices with their start and end apart: 10 -> 10, of which waited for: 2 -> 2; matrix products, arithmetic and copies ran while one was open for 3% -> 3% of each run, Pallas kernels for 23% -> 41%
where the time goes in v2:
time: 61.1 us; the launch traced here: 60.7 us
  Pallas kernels  28.9 us (47%)
  starting transfers between devices  22.6 us (37%)
  waiting for transfers between devices  4.08 us (7%)
  local copies, waits for them, and re-layouts  2.9 us (5%)
  between operations  2.01 us (3%)
    pallas_call x3, Pallas kernels, prefill_request(): pl.pallas_call(functools.partial(prefill_kernel, (blocks, first_block, st...  20 us
    ppermute x4, starting transfers between devices, on_device(): lax.ppermute(results[k], ('head', 'rep'), [(b, a) for a, b in routes[k]])  10.5 us
    ppermute x4, starting transfers between devices, on_device(): lax.ppermute(lax.dynamic_slice_in_dim(packet, targets[k] * nreq, nreq, 0)...  9.01 us
    pallas_call x3, Pallas kernels, decode_request(): pl.pallas_call(functools.partial(decode_kernel, (count, blocks, first_blo...  7.58 us
    ppermute x4, waiting for transfers between devices, on_device(): lax.ppermute(lax.dynamic_slice_in_dim(packet, targets[k] * nreq, nreq, 0)...  4.06 us
    ppermute x2, starting transfers between devices, on_device(): held[i].append(lax.ppermute(own[i], 'ctx', perm))  3.08 us
    slice x1, local copies, waits for them, and re-layouts, on_device(): own = [flat[i:i + 1] for i in range(nreq)]  1.42 us
    pallas_call x1, Pallas kernels, place(): pl.pallas_call(functools.partial(place_kernel, count), in_specs=[pl.Block...  1.26 us
  transfers between devices with their start and end apart: 10, of which 2 were waited for; matrix products, arithmetic and copies ran while one was open for 3% of the time, Pallas kernels for 41%

profile of v2, /device:TPU:0, one launch (start us, length us, event | category | flops | bytes accessed | tf_op | source)
XLA Modules:
  0.0 60.7 jit_solution(11914852473775546807)
XLA Ops:
  0.6 0.0 copy-start.4
  0.6 0.0 copy-start.1
  0.7 0.0 copy-start.2
  0.7 0.0 copy-start.3
  0.7 0.0 copy-start
  0.7 1.4 %fusion = (f32[1,2,256,2,128]{4,3,2,1,0:T(2,128)S(1)}, f32[1,2,256,2,128]{4,3,2,1,0:T(2,128)S(1)}) fusion(f32[2,2,256,2,128]{4,3,2,1,0:T(2,128)} %param.6), kind=kLoop, calls=%fused_computation.9 | loop fusion | bytes 2097152 | tf_op jit(solution)/shard_map/slice | solution.py:301
  2.1 3.0 %collective-permute-start.1 = (f32[1,2,512,128]{3,2,1,0:T(8,128)S(1)}, f32[1,2,512,128]{3,2,1,0:T(8,128)}, u32[]{:S(2)}, u32[]{:S(2)}) collective-permute-start(f32[1,2,512,128]{3,2,1,0:T(8,128)S(1)} %bitcast.19), channel_id=1, source_target_pairs={{16,0},{0,16},{17,1},{1,17},{18,2},{2,18},{19,3},{3,19},{20,4},{4,... | collective-permute-start | bytes 1572872 | tf_op jit(solution)/shard_map/ppermute | solution.py:307
  5.1 0.1 collective-permute-start
  5.2 0.0 copy-done.4
  5.2 0.1 broadcast_in_dim.17
  5.3 0.0 copy-done.1
  5.3 0.0 copy-done.2
  5.3 0.7 %constant_dynamic-slice_fusion = (f32[2,1,88,128]{3,2,1,0:T(8,128)S(1)}, f32[2,1,88,128]{3,2,1,0:T(8,128)}, f32[2,1,88,128]{3,2,1,0:T(8,128)}, f32[2,1,88,128]{3,2,1,0:T(8,128)}) fusion(f32[8,1,88,128]{3,2,1,0:T(8,128)S(1)} %pad_maximum_fusion, s32[]{:T(128)S(6)} %select_n.56, s32[]{:T(128)S(6)} %select_n.55, s32[]{:T(128)S(6)} %select_n.54, s32[]{:T(128)S(6)} %select_n.53), kind=kLoop, calls=%fused_computation.1 | loop fusion | bytes 720912 | tf_op jit(solution)/shard_map/dynamic_slice | solution.py:325
  6.0 1.5 %collective-permute-start.2 = (f32[2,1,88,128]{3,2,1,0:T(8,128)}, f32[2,1,88,128]{3,2,1,0:T(8,128)S(1)}, u32[]{:S(2)}, u32[]{:S(2)}) collective-permute-start(f32[2,1,88,128]{3,2,1,0:T(8,128)} %get-tuple-element.39), channel_id=1, source_target_pairs={{0,0},{1,4},{2,8},{3,12},{4,1},{5,5},{6,9},{7,13},{8,2},{9,6},{10,... | collective-permute-start | bytes 270344 | tf_op jit(solution)/shard_map/ppermute | solution.py:325
  7.6 2.6 %collective-permute-start.3 = (f32[2,1,88,128]{3,2,1,0:T(8,128)}, f32[2,1,88,128]{3,2,1,0:T(8,128)S(1)}, u32[]{:S(2)}, u32[]{:S(2)}) collective-permute-start(f32[2,1,88,128]{3,2,1,0:T(8,128)} %get-tuple-element.38), channel_id=1, source_target_pairs={{0,4},{1,8},{2,12},{3,0},{4,5},{5,9},{6,13},{7,1},{8,6},{9,10},{10... | collective-permute-start | bytes 270344 | tf_op jit(solution)/shard_map/ppermute | solution.py:325
  10.1 3.5 %collective-permute-start.4 = (f32[2,1,88,128]{3,2,1,0:T(8,128)}, f32[2,1,88,128]{3,2,1,0:T(8,128)S(1)}, u32[]{:S(2)}, u32[]{:S(2)}) collective-permute-start(f32[2,1,88,128]{3,2,1,0:T(8,128)} %get-tuple-element.37), channel_id=1, source_target_pairs={{0,8},{1,12},{2,0},{3,4},{4,9},{5,13},{6,1},{7,5},{8,10},{9,14},{1... | collective-permute-start | bytes 270344 | tf_op jit(solution)/shard_map/ppermute | solution.py:325
  13.6 0.0 copy-done.3
  13.6 0.7 %fusion.1 = (s32[1]{0:T(128)}, s32[1]{0:T(128)}) fusion(s32[8]{0:T(128)S(1)} %copy-done.3, s32[]{:T(128)S(6)} %select_n.48, s32[]{:T(128)S(6)} %select_n.45), kind=kLoop, calls=%fused_computation.10 | loop fusion | bytes 24 | tf_op jit(solution)/shard_map/dynamic_slice | solution.py:330
  15.5 0.1 add_add_fusion.marks
  15.6 0.0 copy-done
  15.6 4.0 %prefill.3 = (f32[2,1024,128]{2,1,0:T(8,128)S(1)}, f32[2,1024,128]{2,1,0:T(8,128)S(1)}) custom-call(s32[3]{0:T(128)S(1)} %add_add_fusion.marks, f32[2,128,16,128]{3,2,1,0:T(8,128)S(1)} %copy-done, f32[1,2,512,128]{3,2,1,0:T(8,128)S(1)} %bitcast.23), custom_call_target="tpu_custom_call" | custom-call | flops 67108864 | bytes 2621440 | tf_op jit(solution)/shard_map/prefill/pallas_call | solution.py:144
  19.6 0.0 collective-permute-done.2.refs_0_
  19.7 1.4 %collective-permute-start.5 = (f32[2,1,88,128]{3,2,1,0:T(8,128)S(1)}, f32[2,1,88,128]{3,2,1,0:T(8,128)S(1)}, u32[]{:S(2)}, u32[]{:S(2)}) collective-permute-start(f32[2,1,88,128]{3,2,1,0:T(8,128)S(1)} %get-tuple-element.36), channel_id=1, source_target_pairs={{0,12},{1,0},{2,4},{3,8},{4,13},{5,1},{6,5},{7,9},{8,14},{9,2},{10... | collective-permute-start | bytes 270344 | tf_op jit(solution)/shard_map/ppermute | solution.py:325
  21.1 0.1 add_add_fusion.1.marks
  21.1 0.0 collective-permute-done.3.refs_1_
  21.1 3.8 %collective-permute-done.4.refs_2_ = f32[2,1,88,128]{3,2,1,0:T(8,128)S(1)} collective-permute-done((f32[2,1,88,128]{3,2,1,0:T(8,128)}, f32[2,1,88,128]{3,2,1,0:T(8,128)S(1)}, u32[]{:S(2)}, u32[]{:S(2)}) %collective-permute-start.4) | collective-permute-done | bytes 90144 | tf_op jit(solution)/shard_map/ppermute | solution.py:325
  24.9 0.3 collective-permute-done.5.refs_3_
  25.2 1.6 %decode.3 = (f32[2,128,128]{2,1,0:T(8,128)S(1)}, f32[2,128,128]{2,1,0:T(8,128)S(1)}) custom-call(s32[3]{0:T(128)S(1)} %add_add_fusion.marks, f32[2,1,88,128]{3,2,1,0:T(8,128)S(1)} %collective-permute-done.2.refs_0_, f32[2,1,88,128]{3,2,1,0:T(8,128)S(1)} %collective-permute-done.3.refs_1_, f32[2,1,88,128]{3,2,1,0:T(8,128)S(1)} %collective-permute-done.4.refs_2_, ...), custom_call_target="tpu_custom_call" | custom-call | flops 8388608 | bytes 884736 | tf_op jit(solution)/shard_map/decode/pallas_call | solution.py:246
  26.8 0.0 collective-permute-done.1.refs_1_.refs_5_
  26.9 3.1 %decode.4 = (f32[2,1,64,128]{3,2,1,0:T(8,128)S(1)}, f32[2,1,64,128]{3,2,1,0:T(8,128)S(1)}, f32[2,1,64,128]{3,2,1,0:T(8,128)S(1)}, f32[2,1,64,128]{3,2,1,0:T(8,128)S(1)}) custom-call(s32[3]{0:T(128)S(1)} %add_add_fusion.1.marks, f32[2,1,88,128]{3,2,1,0:T(8,128)S(1)} %collective-permute-done.2.refs_0_, f32[2,1,88,128]{3,2,1,0:T(8,128)S(1)} %collective-permute-done.3.refs_1_, ...), custom_call_target="tpu_custom_call" | custom-call | flops 16777216 | bytes 1409024 | tf_op jit(solution)/shard_map/decode/pallas_call | solution.py:246
  30.0 6.3 %prefill.4 = (f32[2,128,16,128]{3,2,1,0:T(8,128)}, f32[8,128]{1,0:T(8,128)S(1)}) custom-call(s32[3]{0:T(128)S(1)} %add_add_fusion.1.marks, f32[2,128,16,128]{3,2,1,0:T(8,128)S(1)} %copy-done, f32[1,2,512,128]{3,2,1,0:T(8,128)S(1)} %bitcast.21, f32[1,2,512,128]{3,2,1,0:T(8,128)} %collective-permute-done.1.refs_1_.refs_5_), custom_call_target="tpu_custom_call" | custom-call | flops 134217728 | bytes 3145728 | tf_op jit(solution)/shard_map/prefill/pallas_call | solution.py:144
  36.2 0.0 collective-permute-done.refs_0_.refs_4_
  36.2 2.9 %decode.5 = (f32[2,1,64,128]{3,2,1,0:T(8,128)S(1)}, f32[2,1,64,128]{3,2,1,0:T(8,128)S(1)}, f32[2,1,64,128]{3,2,1,0:T(8,128)S(1)}, f32[2,1,64,128]{3,2,1,0:T(8,128)S(1)}) custom-call(s32[3]{0:T(128)S(1)} %add_add_fusion.marks, ...), custom_call_target="tpu_custom_call", output_to_operand_aliasing={{0}: (10, {}), {1}: (11, {}), {2}: (12, {}), {3}: (13, {})} | custom-call | flops 8388608 | bytes 884736 | tf_op jit(solution)/shard_map/decode/pallas_call | solution.py:246
  39.1 0.7 %collective-permute-start.6 = (f32[2,1,64,128]{3,2,1,0:T(8,128)S(1)}, f32[2,1,64,128]{3,2,1,0:T(8,128)S(1)}, u32[]{:S(2)}, u32[]{:S(2)}) collective-permute-start(f32[2,1,64,128]{3,2,1,0:T(8,128)S(1)} %get-tuple-element.28), channel_id=1, source_target_pairs={{0,0},{4,1},{8,2},{12,3},{1,4},{5,5},{9,6},{13,7},{2,8},{6,9},{10,... | collective-permute-start | bytes 196616 | tf_op jit(solution)/shard_map/ppermute | solution.py:351
  39.8 7.0 %collective-permute-start.7 = (f32[2,1,64,128]{3,2,1,0:T(8,128)S(1)}, f32[2,1,64,128]{3,2,1,0:T(8,128)S(1)}, u32[]{:S(2)}, u32[]{:S(2)}) collective-permute-start(f32[2,1,64,128]{3,2,1,0:T(8,128)S(1)} %get-tuple-element.29), channel_id=1, source_target_pairs={{4,0},{8,1},{12,2},{0,3},{5,4},{9,5},{13,6},{1,7},{6,8},{10,9},{14... | collective-permute-start | bytes 196616 | tf_op jit(solution)/shard_map/ppermute | solution.py:351
  46.7 1.4 %collective-permute-start.8 = (f32[2,1,64,128]{3,2,1,0:T(8,128)S(1)}, f32[2,1,64,128]{3,2,1,0:T(8,128)S(1)}, u32[]{:S(2)}, u32[]{:S(2)}) collective-permute-start(f32[2,1,64,128]{3,2,1,0:T(8,128)S(1)} %get-tuple-element.30), channel_id=1, source_target_pairs={{8,0},{12,1},{0,2},{4,3},{9,4},{13,5},{1,6},{5,7},{10,8},{14,9},{2... | collective-permute-start | bytes 196616 | tf_op jit(solution)/shard_map/ppermute | solution.py:351
  48.2 1.4 %collective-permute-start.9 = (f32[2,1,64,128]{3,2,1,0:T(8,128)S(1)}, f32[2,1,64,128]{3,2,1,0:T(8,128)S(1)}, u32[]{:S(2)}, u32[]{:S(2)}) collective-permute-start(f32[2,1,64,128]{3,2,1,0:T(8,128)S(1)} %get-tuple-element.31), channel_id=1, source_target_pairs={{12,0},{0,1},{4,2},{8,3},{13,4},{1,5},{5,6},{9,7},{14,8},{2,9},{6,... | collective-permute-start | bytes 196616 | tf_op jit(solution)/shard_map/ppermute | solution.py:351
  49.6 0.1 pad_add_fusion.at
  49.6 9.8 %prefill.5 = (f32[2,128,16,128]{3,2,1,0:T(8,128)}, f32[8,128]{1,0:T(8,128)}) custom-call(s32[3]{0:T(128)S(1)} %add_add_fusion.marks, f32[2,128,16,128]{3,2,1,0:T(8,128)S(1)} %copy-done, f32[1,2,512,128]{3,2,1,0:T(8,128)} %collective-permute-done.refs_0_.refs_4_, ...), custom_call_target="tpu_custom_call", output_to_operand_aliasing={{0}: (5, {})} | custom-call | flops 67108864 | bytes 2621440 | tf_op jit(solution)/shard_map/prefill/pallas_call | solution.py:144
  59.4 0.0 collective-permute-done.6.refs_0_
  59.4 0.0 collective-permute-done.7.refs_1_
  59.4 0.0 collective-permute-done.8.refs_2_
  59.4 0.0 collective-permute-done.9.refs_3_
  59.4 1.3 %place.1 = f32[8,1,64,128]{3,2,1,0:T(8,128)} custom-call(s32[4]{0:T(128)S(1)} %pad_add_fusion.at, f32[2,1,64,128]{3,2,1,0:T(8,128)S(1)} %collective-permute-done.6.refs_0_, f32[2,1,64,128]{3,2,1,0:T(8,128)S(1)} %collective-permute-done.7.refs_1_, f32[2,1,64,128]{3,2,1,0:T(8,128)S(1)} %collective-permute-done.8.refs_2_, ...), custom_call_target="tpu_custom_call" | custom-call | tf_op jit(solution)/shard_map/place/pallas_call | solution.py:281
  (2 shorter events, 0.0 us)
Async XLA Ops:
  0.6 4.6 %copy-start.4 = (s32[8,1]{0,1:T(1,128)S(1)}, s32[8,1]{0,1:T(1,128)}, u32[]{:S(2)}) copy-start(s32[8,1]{0,1:T(1,128)} %param.11) | copy-start | bytes 100
  0.6 4.6 %copy-start.1 = (f32[8,1,4,16,128]{4,3,2,1,0:T(8,128)S(1)}, f32[8,1,4,16,128]{4,3,2,1,0:T(8,128)}, u32[]{:S(2)}) copy-start(f32[8,1,4,16,128]{4,3,2,1,0:T(8,128)} %param.8) | copy-start | bytes 786436
  0.7 4.6 %copy-start.2 = (f32[8,1,4,2,2,128]{5,4,3,2,1,0:T(2,128)S(1)}, f32[8,1,4,2,2,128]{5,4,3,2,1,0:T(2,128)}, u32[]{:S(2)}) copy-start(f32[8,1,4,2,2,128]{5,4,3,2,1,0:T(2,128)} %param.9) | copy-start | bytes 196612
  0.7 13.0 %copy-start.3 = (s32[8]{0:T(128)S(1)}, s32[8]{0:T(128)}, u32[]{:S(2)}) copy-start(s32[8]{0:T(128)} %param.10) | copy-start | bytes 100
  0.7 15.0 %copy-start = (f32[2,128,16,128]{3,2,1,0:T(8,128)S(1)}, f32[2,128,16,128]{3,2,1,0:T(8,128)}, u32[]{:S(2)}) copy-start(f32[2,128,16,128]{3,2,1,0:T(8,128)} %q_ref.5) | copy-start | bytes 6291460
  2.1 24.7 %collective-permute-start.1 = (f32[1,2,512,128]{3,2,1,0:T(8,128)S(1)}, f32[1,2,512,128]{3,2,1,0:T(8,128)}, u32[]{:S(2)}, u32[]{:S(2)}) collective-permute-start(f32[1,2,512,128]{3,2,1,0:T(8,128)S(1)} %bitcast.19), channel_id=1, source_target_pairs={{16,0},{0,16},{17,1},{1,17},{18,2},{2,18},{19,3},{3,19},{20,4},{4,... | collective-permute-start | bytes 1572872 | tf_op jit(solution)/shard_map/ppermute | solution.py:307
  5.1 31.1 %collective-permute-start = (f32[1,2,512,128]{3,2,1,0:T(8,128)S(1)}, f32[1,2,512,128]{3,2,1,0:T(8,128)}, u32[]{:S(2)}, u32[]{:S(2)}) collective-permute-start(f32[1,2,512,128]{3,2,1,0:T(8,128)S(1)} %bitcast.22), channel_id=1, source_target_pairs={{16,0},{0,16},{17,1},{1,17},{18,2},{2,18},{19,3},{3,19},{20,4},{4,... | collective-permute-start | bytes 1572872 | tf_op jit(solution)/shard_map/ppermute | solution.py:307
  6.0 13.6 %collective-permute-start.2 = (f32[2,1,88,128]{3,2,1,0:T(8,128)}, f32[2,1,88,128]{3,2,1,0:T(8,128)S(1)}, u32[]{:S(2)}, u32[]{:S(2)}) collective-permute-start(f32[2,1,88,128]{3,2,1,0:T(8,128)} %get-tuple-element.39), channel_id=1, source_target_pairs={{0,0},{1,4},{2,8},{3,12},{4,1},{5,5},{6,9},{7,13},{8,2},{9,6},{10,... | collective-permute-start | bytes 270344 | tf_op jit(solution)/shard_map/ppermute | solution.py:325
  7.6 13.6 %collective-permute-start.3 = (f32[2,1,88,128]{3,2,1,0:T(8,128)}, f32[2,1,88,128]{3,2,1,0:T(8,128)S(1)}, u32[]{:S(2)}, u32[]{:S(2)}) collective-permute-start(f32[2,1,88,128]{3,2,1,0:T(8,128)} %get-tuple-element.38), channel_id=1, source_target_pairs={{0,4},{1,8},{2,12},{3,0},{4,5},{5,9},{6,13},{7,1},{8,6},{9,10},{10... | collective-permute-start | bytes 270344 | tf_op jit(solution)/shard_map/ppermute | solution.py:325
  10.1 14.8 %collective-permute-start.4 = (f32[2,1,88,128]{3,2,1,0:T(8,128)}, f32[2,1,88,128]{3,2,1,0:T(8,128)S(1)}, u32[]{:S(2)}, u32[]{:S(2)}) collective-permute-start(f32[2,1,88,128]{3,2,1,0:T(8,128)} %get-tuple-element.37), channel_id=1, source_target_pairs={{0,8},{1,12},{2,0},{3,4},{4,9},{5,13},{6,1},{7,5},{8,10},{9,14},{1... | collective-permute-start | bytes 270344 | tf_op jit(solution)/shard_map/ppermute | solution.py:325
  19.7 5.6 %collective-permute-start.5 = (f32[2,1,88,128]{3,2,1,0:T(8,128)S(1)}, f32[2,1,88,128]{3,2,1,0:T(8,128)S(1)}, u32[]{:S(2)}, u32[]{:S(2)}) collective-permute-start(f32[2,1,88,128]{3,2,1,0:T(8,128)S(1)} %get-tuple-element.36), channel_id=1, source_target_pairs={{0,12},{1,0},{2,4},{3,8},{4,13},{5,1},{6,5},{7,9},{8,14},{9,2},{10... | collective-permute-start | bytes 270344 | tf_op jit(solution)/shard_map/ppermute | solution.py:325
  39.1 20.3 %collective-permute-start.6 = (f32[2,1,64,128]{3,2,1,0:T(8,128)S(1)}, f32[2,1,64,128]{3,2,1,0:T(8,128)S(1)}, u32[]{:S(2)}, u32[]{:S(2)}) collective-permute-start(f32[2,1,64,128]{3,2,1,0:T(8,128)S(1)} %get-tuple-element.28), channel_id=1, source_target_pairs={{0,0},{4,1},{8,2},{12,3},{1,4},{5,5},{9,6},{13,7},{2,8},{6,9},{10,... | collective-permute-start | bytes 196616 | tf_op jit(solution)/shard_map/ppermute | solution.py:351
  39.8 19.7 %collective-permute-start.7 = (f32[2,1,64,128]{3,2,1,0:T(8,128)S(1)}, f32[2,1,64,128]{3,2,1,0:T(8,128)S(1)}, u32[]{:S(2)}, u32[]{:S(2)}) collective-permute-start(f32[2,1,64,128]{3,2,1,0:T(8,128)S(1)} %get-tuple-element.29), channel_id=1, source_target_pairs={{4,0},{8,1},{12,2},{0,3},{5,4},{9,5},{13,6},{1,7},{6,8},{10,9},{14... | collective-permute-start | bytes 196616 | tf_op jit(solution)/shard_map/ppermute | solution.py:351
  46.7 12.7 %collective-permute-start.8 = (f32[2,1,64,128]{3,2,1,0:T(8,128)S(1)}, f32[2,1,64,128]{3,2,1,0:T(8,128)S(1)}, u32[]{:S(2)}, u32[]{:S(2)}) collective-permute-start(f32[2,1,64,128]{3,2,1,0:T(8,128)S(1)} %get-tuple-element.30), channel_id=1, source_target_pairs={{8,0},{12,1},{0,2},{4,3},{9,4},{13,5},{1,6},{5,7},{10,8},{14,9},{2... | collective-permute-start | bytes 196616 | tf_op jit(solution)/shard_map/ppermute | solution.py:351
  48.2 11.3 %collective-permute-start.9 = (f32[2,1,64,128]{3,2,1,0:T(8,128)S(1)}, f32[2,1,64,128]{3,2,1,0:T(8,128)S(1)}, u32[]{:S(2)}, u32[]{:S(2)}) collective-permute-start(f32[2,1,64,128]{3,2,1,0:T(8,128)S(1)} %get-tuple-element.31), channel_id=1, source_target_pairs={{12,0},{0,1},{4,2},{8,3},{13,4},{1,5},{5,6},{9,7},{14,8},{2,9},{6,... | collective-permute-start | bytes 196616 | tf_op jit(solution)/shard_map/ppermute | solution.py:351

commit v3 on v2

v3 whole, which is shorter than its diff:
```python
import functools
import math

import jax
import jax.numpy as jnp
from jax import lax
from jax.experimental import pallas as pl
from jax.experimental.pallas import tpu as pltpu
from jax.sharding import PartitionSpec as P

NEG_FILL = -1e30
LOG2E = math.log2(math.e)
F32 = jnp.float32
BF16 = jnp.bfloat16


def split_two(x):
    high = x.astype(BF16)
    return high, (x - high.astype(F32)).astype(BF16)


def split_three(x):
    high = x.astype(BF16)
    rest = x - high.astype(F32)
    mid = rest.astype(BF16)
    return high, mid, (rest - mid.astype(F32)).astype(BF16)


def query_terms(q):
    a, b, c = split_three(q)
    return jnp.concatenate([a, b, a, b, a, c], axis=-1)


def key_terms(k):
    a, b, c = split_three(k)
    return jnp.concatenate([a, a, b, b, c, a], axis=-1)


def value_terms(v):
    return jnp.concatenate(split_two(v.T), axis=0)


def score_block(k6, q6, limit, first_pos):
    s = lax.dot_general(k6, q6, (((1,), (1,)), ((), ())), preferred_element_type=F32)
    return jnp.where(lax.broadcasted_iota(jnp.int32, s.shape, 0) < limit - first_pos, s, NEG_FILL)


def weighted(vv, p):
    dim = vv.shape[0] // 2
    a, b = split_two(p)
    both = jnp.dot(vv, a, preferred_element_type=F32)
    return (both[:dim] + both[dim:]) + jnp.dot(vv[:dim], b, preferred_element_type=F32)


def fold(state, scores, values):
    top = functools.reduce(jnp.maximum, [jnp.max(s, axis=0, keepdims=True) for s in scores])
    if state is not None:
        top = jnp.maximum(top, state[0])
    weights = [jnp.exp2(s - top) for s in scores]
    total = functools.reduce(jnp.add, [jnp.sum(w, axis=0, keepdims=True) for w in weights])
    acc = functools.reduce(jnp.add, [weighted(vv, w) for vv, w in zip(values, weights)])
    if state is not None:
        factor = jnp.exp2(state[0] - top)
        total = total + state[1] * factor
        acc = acc + state[2] * factor
    return top, total, acc


def in_pairs(blocks):
    return [blocks[i : i + 2] for i in range(0, len(blocks), 2)]


def cache_head(ref, which, head, heads):
    return ref[0, which, pl.ds(head, ref.shape[2] // heads, stride=heads), :]


def put_state(state, acc_ref, stat_ref, head, cols):
    acc_ref[head, :, cols] = state[2]
    stat_ref[head, 0:1, cols] = state[0]
    stat_ref[head, 1:2, cols] = state[1]


def get_state(acc_ref, stat_ref, head, cols):
    return stat_ref[head, 0:1, cols], stat_ref[head, 1:2, cols], acc_ref[head, :, cols]


def state_shapes(heads, dim, rows):
    return [jax.ShapeDtypeStruct((heads, dim, rows), F32), jax.ShapeDtypeStruct((heads, 8, rows), F32)]


def block_starts(count, first, block_len):
    here, total = lax.axis_index("ctx"), lax.axis_size("ctx")
    return [lax.rem(here + (first + b), total) * block_len for b in range(count)]


def prefill_kernel(plan, heads, scale, lengths, q_ref, *refs):
    index, blocks, first_block, started, finish, unread = plan
    kv_refs, refs = refs[:blocks], refs[blocks:]
    state_in = refs[:2] if started else None
    outs = refs[(2 if started else 0) + unread :]
    _, span, q_heads, dim = q_ref.shape
    group = q_heads // heads
    chunk = min(span, CHUNK)
    total = lax.axis_size("ctx") * span
    begin = lengths[lax.axis_index("head") * q_ref.shape[0] + index] - total + lax.axis_index("ctx") * span
    at_pos = block_starts(blocks, first_block, kv_refs[0].shape[2] // heads)
    keys = [[key_terms(cache_head(ref, 0, h, heads)) for ref in kv_refs] for h in range(heads)]
    vals = [[value_terms(cache_head(ref, 1, h, heads)) for ref in kv_refs] for h in range(heads)]
    items = [(first, h) for first in range(0, span, chunk) for h in range(heads)]
    groups = in_pairs(list(range(blocks)))

    def scores(item):
        first, h = item
        q = q_ref[index, first : first + chunk, h * group : (h + 1) * group].reshape(chunk * group, dim) * scale
        q6 = query_terms(q)
        limit = begin + first + 1 + lax.broadcasted_iota(jnp.int32, (1, chunk * group), 1) // group
        return [
            functools.partial(
                lambda g: [score_block(keys[h][b], q6, limit, at_pos[b]) for b in g], g
            )
            for g in groups
        ]

    steps = [(n, g, make) for n, item in enumerate(items) for g, make in zip(groups, scores(item))]
    ahead = steps[0][2]()
    state = None
    copies = []
    for at, (n, g, _) in enumerate(steps):
        now, ahead = ahead, steps[at + 1][2]() if at + 1 < len(steps) else None
        first, h = items[n]
        cols = pl.ds(first * group, chunk * group)
        if g is groups[0]:
            state = get_state(*state_in, h, cols) if started else None
        state = fold(state, now, [vals[h][b] for b in g])
        if g is not groups[-1]:
            continue
        if not finish:
            put_state(state, outs[0], outs[1], h, cols)
            continue
        out_ref, hold, sems = outs[0], outs[-2], outs[-1]
        hold[n] = (state[2] * (1.0 / state[1])).T.reshape(chunk, group, dim)
        copy = pltpu.make_async_copy(
            hold.at[n], out_ref.at[index, pl.ds(first, chunk), pl.ds(h * group, group)], sems.at[n]
        )
        copy.start()
        copies.append(copy)
    if finish:
        outs[1][...] = jnp.zeros_like(outs[1])
    for copy in copies:
        copy.wait()


CHUNK = 64
SMEM_SPEC = pl.BlockSpec(memory_space=pltpu.SMEM)
VMEM_SPEC = pl.BlockSpec(memory_space=pltpu.VMEM)
ANY_SPEC = pl.BlockSpec(memory_space=pl.ANY)


def prefill_request(index, lengths, prefill_q, kv_list, first_block, heads, scale, state=None, finish=True, carried=None, after=()):
    nreq, span, q_heads, dim = prefill_q.shape
    group = q_heads // heads
    blocks = len(kv_list)
    started = state is not None
    state = list(state) if started else []
    unread = list(after) + ([carried] if carried is not None else [])
    alias = {2 + blocks + len(state) + len(after): 0} if carried is not None else {}
    keys = sum(kv.shape[2] for kv in kv_list) // heads
    scratch = []
    if finish:
        out_specs = [ANY_SPEC, VMEM_SPEC]
        out_shape = [jax.ShapeDtypeStruct(prefill_q.shape, F32), jax.ShapeDtypeStruct((8, 128), F32)]
        chunk = min(span, CHUNK)
        items = span // chunk * heads
        scratch = [pltpu.VMEM((items, chunk, group, dim), F32), pltpu.SemaphoreType.DMA((items,))]
    else:
        out_specs = [VMEM_SPEC, VMEM_SPEC]
        out_shape = state_shapes(heads, dim, span * group)
    return pl.pallas_call(
        functools.partial(prefill_kernel, (index, blocks, first_block, started, finish, len(unread)), heads, scale),
        in_specs=[SMEM_SPEC] + [VMEM_SPEC] * (1 + blocks + len(state)) + [ANY_SPEC] * len(unread),
        out_specs=out_specs,
        out_shape=out_shape,
        scratch_shapes=scratch,
        input_output_aliases=alias,
        compiler_params=pltpu.CompilerParams(vmem_limit_bytes=16 * 2**20),
        cost_estimate=pl.CostEstimate(
            flops=span * q_heads * keys * dim,
            bytes_accessed=4 * (2 * span * q_heads * dim + 2 * heads * keys * dim),
            transcendentals=span * q_heads * keys,
        ),
        name="prefill",
    )(lengths, prefill_q, *kv_list, *state, *unread)


def decode_kernel(plan, heads, group, steps, scale, *refs):
    index, near, blocks, first_block, started, finish, ready, unread = plan
    near_refs, far_ref, refs = refs[:near], refs[near], refs[near + 1 :]
    kv_refs, refs = refs[:blocks], refs[blocks:]
    state_in = refs[:2] if started else None
    refs = refs[2 if started else 0 :]
    ready_refs, outs = refs[:ready], refs[ready + unread :]
    side = lax.rem(lax.axis_index("head"), 2)
    at_pos = block_starts(blocks, first_block, kv_refs[0].shape[2] // heads)
    _, nreq, per, _, dim = far_ref.shape
    q_rows = steps * heads * group
    rows = steps * group
    slots = [(ref, side, n) for ref in near_refs for n in range(per)]
    slots += [(far_ref, j, n) for j in range(near) for n in range(per)]
    every = pl.ds(0, len(slots) * rows)
    at_limit = q_rows + 2 * heads * steps
    lane = lax.broadcasted_iota(jnp.int32, (1, len(slots) * rows), 1)
    limit = jnp.zeros(lane.shape, F32)
    for i, (ref, lead, n) in enumerate(slots):
        wide = jnp.broadcast_to(ref[lead, index, n, at_limit : at_limit + 1, 0:1], lane.shape)
        limit = jnp.where(lane // rows == i, wide, limit)
    limit = limit.astype(jnp.int32)
    if finish:
        for i in range(ready):
            first = i // 2
            outs[i % 2][:, first : first + 1] = ready_refs[i][...]
    for head in range(heads):
        own = slice(head * group, (head + 1) * group)
        q = jnp.concatenate(
            [
                ref[lead, index, n, 0:q_rows].reshape(steps, heads * group, dim)[:, own].reshape(rows, dim)
                for ref, lead, n in slots
            ],
            axis=0,
        )
        q6 = query_terms(q * scale)
        state = get_state(*state_in, head, every) if started else None
        for g, group_blocks in enumerate(in_pairs(list(range(blocks)))):
            parts = [
                score_block(key_terms(cache_head(kv_refs[b], 0, head, heads)), q6, limit, at_pos[b])
                for b in group_blocks
            ]
            vals = [value_terms(cache_head(kv_refs[b], 1, head, heads)) for b in group_blocks]
            if g == 0 and not started:
                drafts = [
                    jnp.concatenate(
                        [
                            ref[lead, index, n, pl.ds(q_rows + which * heads + head, steps, stride=2 * heads), :]
                            for ref, lead, n in slots
                        ],
                        axis=0,
                    )
                    for which in range(2)
                ]
                s = lax.dot_general(
                    key_terms(drafts[0]), q6, (((1,), (1,)), ((), ())), preferred_element_type=F32
                )
                key = lax.broadcasted_iota(jnp.int32, s.shape, 0)
                row = lax.broadcasted_iota(jnp.int32, s.shape, 1)
                seen = (row // rows == key // steps) & (key % steps <= row % rows // group)
                parts.append(jnp.where(seen, s, NEG_FILL))
                vals.append(value_terms(drafts[1]))
            state = fold(state, parts, vals)
        if not finish:
            put_state(state, outs[0], outs[1], head, every)
            continue
        out = (state[2] * (1.0 / state[1])).T
        for i in range(len(slots)):
            dst, j, n = outs[i // (near * per)], i // per % near, i % per
            for step in range(steps):
                first = step * heads * group + head * group
                at = i * rows + step * group
                dst[j, dst.shape[1] - 1, n, first : first + group] = out[at : at + group]


def decode_request(
    index, near, far, kv_list, first_block, heads, group, steps, scale, state=None, finish=True, ready=(), after=()
):
    count, _, per, packet_rows, dim = far.shape
    blocks = len(kv_list)
    q_rows = steps * heads * group
    all_rows = 2 * count * per * steps * group
    started = state is not None
    state = list(state) if started else []
    ready_flat = [a for one in ready for a in one]
    if finish:
        out_shape = [jax.ShapeDtypeStruct((count, len(ready) + 1, per, q_rows, dim), F32)] * 2
    else:
        out_shape = state_shapes(heads, dim, all_rows)
    keys = sum(kv.shape[2] for kv in kv_list) // heads
    plan = (index, count, blocks, first_block, started, finish, len(ready_flat), len(after))
    operands = count + 1 + blocks + len(state) + len(ready_flat)
    return pl.pallas_call(
        functools.partial(decode_kernel, plan, heads, group, steps, scale),
        in_specs=[VMEM_SPEC] * operands + [ANY_SPEC] * len(after),
        out_specs=[VMEM_SPEC] * len(out_shape),
        out_shape=out_shape,
        compiler_params=pltpu.CompilerParams(vmem_limit_bytes=12 * 2**20),
        cost_estimate=pl.CostEstimate(
            flops=all_rows * heads * keys * dim,
            bytes_accessed=4 * (4 * count * per * packet_rows * dim + 2 * heads * keys * dim),
            transcendentals=all_rows * heads * keys,
        ),
        name="decode",
    )(*near, far, *kv_list, *state, *ready_flat, *after)


def take_kernel(index, src, dst, sem):
    copy = pltpu.make_async_copy(src.at[pl.ds(index, 1)], dst, sem)
    copy.start()
    copy.wait()


def take(index, array):
    return pl.pallas_call(
        functools.partial(take_kernel, index),
        in_specs=[pl.BlockSpec(memory_space=pltpu.HBM)],
        out_specs=VMEM_SPEC,
        out_shape=jax.ShapeDtypeStruct((1,) + array.shape[1:], array.dtype),
        scratch_shapes=[pltpu.SemaphoreType.DMA],
        compiler_params=pltpu.CompilerParams(vmem_limit_bytes=4 * 2**20),
        name="take",
    )(array)


def pack_kernel(unread, lengths, q_ref, kv_ref, *refs):
    outs = refs[unread:]
    half = len(outs)
    _, nreq, per, rows, dim = outs[0].shape
    q_rows, kv_rows = q_ref.shape[2], kv_ref.shape[2]
    for j, out in enumerate(outs):
        pair = lax.rem(lax.axis_index("rep") + j, half)
        for c in range(2):
            for i in range(nreq):
                request = (pair * 2 + c) * nreq + i
                for n in range(per):
                    out[c, i, n, 0:q_rows] = q_ref[request, n]
                    out[c, i, n, q_rows : q_rows + kv_rows] = kv_ref[request, n]
                    reads = jnp.full((rows - q_rows - kv_rows, dim), lengths[request, n], jnp.int32)
                    out[c, i, n, q_rows + kv_rows :] = reads.astype(F32)


def pack(lengths, q, kv, half, nreq, after):
    requests, per, q_rows, dim = q.shape
    shape = jax.ShapeDtypeStruct((2, nreq, per, q_rows + kv.shape[2] + 8, dim), F32)
    return pl.pallas_call(
        functools.partial(pack_kernel, len(after)),
        in_specs=[SMEM_SPEC, VMEM_SPEC, VMEM_SPEC] + [ANY_SPEC] * len(after),
        out_specs=[VMEM_SPEC] * half,
        out_shape=[shape] * half,
        compiler_params=pltpu.CompilerParams(vmem_limit_bytes=4 * 2**20),
        cost_estimate=pl.CostEstimate(flops=10**11, bytes_accessed=10**6, transcendentals=0),
        name="pack",
    )(lengths, q, kv, *after)


def other_kernel(count, *refs):
    out = refs[-1]
    for j, ref in enumerate(refs[:count]):
        out[j] = ref[1 - lax.rem(lax.axis_index("head"), 2)]


def other_side(near, after):
    return pl.pallas_call(
        functools.partial(other_kernel, len(near)),
        in_specs=[VMEM_SPEC] * len(near) + [ANY_SPEC] * len(after),
        out_specs=VMEM_SPEC,
        out_shape=jax.ShapeDtypeStruct((len(near),) + near[0].shape[1:], F32),
        compiler_params=pltpu.CompilerParams(vmem_limit_bytes=4 * 2**20),
        name="other_side",
    )(*near, *after)


def join_kernel(kept, back, *outs):
    side = lax.rem(lax.axis_index("head"), 2)
    for j, out in enumerate(outs):
        out[side] = kept[j]
        out[1 - side] = back[j]


def join(kept, back):
    count = kept.shape[0]
    return pl.pallas_call(
        join_kernel,
        in_specs=[VMEM_SPEC] * 2,
        out_specs=[VMEM_SPEC] * count,
        out_shape=[jax.ShapeDtypeStruct((2,) + kept.shape[1:], F32)] * count,
        compiler_params=pltpu.CompilerParams(vmem_limit_bytes=4 * 2**20),
        name="join",
    )(kept, back)


def place_kernel(*refs):
    o_ref, count = refs[-1], len(refs) - 1
    size = refs[0].shape[0]
    for j in range(count):
        o_ref[pl.ds(lax.rem(lax.axis_index("rep") + j, count) * size, size)] = refs[j][...]


def place(pieces):
    size, per, rows, dim = pieces[0].shape
    count = len(pieces)
    return pl.pallas_call(
        place_kernel,
        in_specs=[VMEM_SPEC] * count,
        out_specs=VMEM_SPEC,
        out_shape=jax.ShapeDtypeStruct((count * size, per, rows, dim), F32),
        compiler_params=pltpu.CompilerParams(vmem_limit_bytes=4 * 2**20),
        name="place",
    )(*pieces)


def on_device(kv_cache, prefill_q, decode_q, decode_kv, lengths, row_length):
    ctx_count, head_count, rep_count = lax.axis_size("ctx"), lax.axis_size("head"), lax.axis_size("rep")
    nreq, _, block_len, heads, dim = kv_cache.shape
    group = prefill_q.shape[2] // heads
    requests, per, steps, q_heads, _ = decode_q.shape
    scale = LOG2E / math.sqrt(dim)
    half = head_count // 2

    flat = kv_cache.reshape(nreq, 2, block_len * heads, dim)
    own = [take(i, flat) for i in range(nreq)]
    held = [[own[i]] for i in range(nreq)]
    for shift in range(1, ctx_count):
        perm = [((i + shift) % ctx_count, i) for i in range(ctx_count)]
        for i in range(nreq):
            held[i].append(lax.ppermute(own[i], "ctx", perm))

    routes = [
        [
            (s * rep_count + t, ((t + j) % half * 2 + t // half) * rep_count + s)
            for s in range(head_count)
            for t in range(rep_count)
        ]
        for j in range(half)
    ]
    swap = [(i, i ^ 1) for i in range(head_count)]
    packets = pack(
        row_length,
        decode_q.reshape(requests, per, steps * q_heads, dim),
        decode_kv.reshape(requests, per, steps * 2 * heads, dim),
        half,
        nreq,
        own,
    )
    near = [lax.ppermute(packets[j], ("head", "rep"), routes[j]) for j in range(half)]
    last = nreq - 1
    prefill_state = prefill_request(last, lengths, prefill_q, held[last][:1], 0, heads, scale, finish=False, after=packets[:1])
    prefill_out, token = None, prefill_state[1]
    for i in range(last):
        prefill_out, token = prefill_request(i, lengths, prefill_q, held[i], 0, heads, scale, carried=prefill_out, after=(token,))
    far = lax.ppermute(other_side(near, (token,)), "head", swap)
    ready = [decode_request(i, near, far, held[i], 0, heads, group, steps, scale) for i in range(last)]
    decode_state = decode_request(last, near, far, held[last][:1], 0, heads, group, steps, scale, finish=False)
    kept, sent = decode_request(
        last, near, far, held[last][1:], 1, heads, group, steps, scale, state=decode_state, ready=ready
    )
    prefill_out, _ = prefill_request(
        last, lengths, prefill_q, held[last][1:], 1, heads, scale, state=prefill_state, carried=prefill_out
    )
    joined = join(kept, lax.ppermute(sent, "head", swap))
    homes = [lax.ppermute(joined[j], ("head", "rep"), [(b, a) for a, b in routes[j]]) for j in range(half)]
    decode_out = place([a.reshape((2 * nreq,) + a.shape[2:]) for a in homes]).reshape(decode_q.shape)
    return (prefill_out, decode_out)


def solution(mesh):
    in_specs = (
        P("head", None, "ctx", "rep", None),
        P("head", "ctx", "rep", None),
        P(None, ("ctx", "rep"), None, "head", None),
        P(None, ("ctx", "rep"), None, None, "head", None),
        P(),
        P(None, ("ctx", "rep")),
    )
    out_specs = (P("head", "ctx", "rep", None), P(None, ("ctx", "rep"), None, "head", None))
    return jax.shard_map(on_device, mesh=mesh, in_specs=in_specs, out_specs=out_specs, check_vma=False)
```

time: 61.1 us -> 46.3 us (0.76)
  the two profiles are of different devices: /device:TPU:0 before, /device:TPU:7 now
where the time goes in v3:
time: 46.3 us; the launch traced here: 46 us
  Pallas kernels  16.6 us (36%)
  starting transfers between devices  15.7 us (34%)
  waiting for transfers between devices  11.6 us (25%)
  local copies, waits for them, and re-layouts  1.32 us (3%)
  between operations  0.78 us (2%)
    pallas_call x3, Pallas kernels, prefill_request(): pl.pallas_call(functools.partial(prefill_kernel, (index, blocks, first_bl...  11.4 us
    ppermute x2, starting transfers between devices, on_device(): lax.ppermute(joined[j], ('head', 'rep'), [(b, a) for a, b in routes[j]])  7.39 us
    ppermute x2, starting transfers between devices, on_device(): lax.ppermute(packets[j], ('head', 'rep'), routes[j])  6.42 us
    ppermute x2, waiting for transfers between devices, on_device(): lax.ppermute(packets[j], ('head', 'rep'), routes[j])  5.28 us
    pallas_call x3, Pallas kernels, decode_request(): pl.pallas_call(functools.partial(decode_kernel, plan, heads, group, steps...  3.67 us
    ppermute x2, waiting for transfers between devices, on_device(): lax.ppermute(joined[j], ('head', 'rep'), [(b, a) for a, b in routes[j]])  2.21 us
    ppermute x2, starting transfers between devices, on_device(): held[i].append(lax.ppermute(own[i], 'ctx', perm))  1.6 us
    ppermute x2, waiting for transfers between devices, on_device(): held[i].append(lax.ppermute(own[i], 'ctx', perm))  1.52 us
  transfers between devices with their start and end apart: 8, of which 5 were waited for; matrix products, arithmetic and copies ran while one was open for 0% of the time, Pallas kernels for 32%

profile of v3, /device:TPU:7, one launch (start us, length us, event | category | flops | bytes accessed | tf_op | source)
XLA Modules:
  0.0 46.0 jit_solution(2435412023700126685)
XLA Ops:
  0.6 0.0 copy-start.5
  0.6 0.0 copy-start.1
  0.7 1.2 %copy-done.1 = f32[2,2,256,2,128]{4,3,2,1,0:T(2,128)S(1)} copy-done((f32[2,2,256,2,128]{4,3,2,1,0:T(2,128)S(1)}, f32[2,2,256,2,128]{4,3,2,1,0:T(2,128)}, u32[]{:S(2)}) %copy-start.1) | copy-done | bytes 1048600
  1.9 0.0 copy-start.3
  1.9 0.0 copy-start.4
  1.9 0.3 collective-permute-start.1
  2.3 1.3 %collective-permute-start = (f32[1,2,512,128]{3,2,1,0:T(8,128)S(1)}, f32[1,2,512,128]{3,2,1,0:T(8,128)S(1)}, u32[]{:S(2)}, u32[]{:S(2)}) collective-permute-start(f32[1,2,512,128]{3,2,1,0:T(8,128)S(1)} %take.2.refs_1_.refs_0_.refs_3_), channel_id=1, source_target_pairs={{16,0},{0,16},{17,1},{1,17},{18,2},{2,18},{19,3},{3,19},{20,4},{4,... | collective-permute-start | bytes 1572872 | tf_op jit(solution)/shard_map/ppermute | solution.py:421
  3.6 0.0 copy-done.5
  3.6 0.1 copy.9.lengths
  3.7 0.0 copy-done.3
  3.7 0.0 copy-done.4
  3.7 0.0 copy-start
  3.7 0.0 copy-start.2
  3.7 0.6 %pack.1 = (f32[2,2,1,88,128]{4,3,2,1,0:T(8,128)S(1)}, f32[2,2,1,88,128]{4,3,2,1,0:T(8,128)S(1)}) custom-call(s32[8,1]{1,0:T(8,128)S(1)} %copy.9.lengths, f32[8,1,64,128]{3,2,1,0:T(8,128)S(1)} %bitcast.12, f32[8,1,16,128]{3,2,1,0:T(8,128)S(1)} %bitcast.13, f32[1,2,512,128]{3,2,1,0:T(8,128)S(1)} %take.3.refs_0_.refs_3_, ...), custom_call_target="tpu_custom_call" | custom-call | flops 99999997952 | bytes 1000000 | tf_op jit(solution)/shard_map/pack/pallas_call | solution.py:340
  4.3 6.3 %collective-permute-start.2 = (f32[2,2,1,88,128]{4,3,2,1,0:T(8,128)S(1)}, f32[2,2,1,88,128]{4,3,2,1,0:T(8,128)S(1)}, u32[]{:S(2)}, u32[]{:S(2)}) collective-permute-start(f32[2,2,1,88,128]{4,3,2,1,0:T(8,128)S(1)} %get-tuple-element.17.refs_1_), channel_id=1, source_target_pairs={{0,0},{1,8},{2,4},{3,12},{4,1},{5,9},{6,5},{7,13},{8,2},{9,10},{10... | collective-permute-start | bytes 540680 | tf_op jit(solution)/shard_map/ppermute | solution.py:440
  10.6 0.1 collective-permute-start.3
  10.8 0.0 copy-done
  10.8 0.0 copy-done.2
  10.8 2.5 %prefill.3 = (f32[2,128,1024]{2,1,0:T(8,128)S(1)}, f32[2,8,1024]{2,1,0:T(8,128)S(1)}) custom-call(s32[8]{0:T(128)S(1)} %copy-done.2, f32[2,128,16,128]{3,2,1,0:T(8,128)S(1)} %copy-done, f32[1,2,512,128]{3,2,1,0:T(8,128)S(1)} %take.2.refs_1_.refs_0_.refs_3_, f32[2,2,1,88,128]{4,3,2,1,0:T(8,128)S(1)} %get-tuple-element.17.refs_1_), custom_call_target="tpu_custom_call" | custom-call | flops 67108864 | bytes 2621440 | tf_op jit(solution)/shard_map/prefill/pallas_call | solution.py:178
  13.3 1.5 %collective-permute-done.1.refs_1_.refs_4_ = f32[1,2,512,128]{3,2,1,0:T(8,128)S(1)} collective-permute-done((f32[1,2,512,128]{3,2,1,0:T(8,128)S(1)}, f32[1,2,512,128]{3,2,1,0:T(8,128)S(1)}, u32[]{:S(2)}, u32[]{:S(2)}) %collective-permute-start.1) | collective-permute-done | bytes 524320 | tf_op jit(solution)/shard_map/ppermute | solution.py:421
  14.8 5.0 %prefill.4 = (f32[2,128,16,128]{3,2,1,0:T(8,128)}, f32[8,128]{1,0:T(8,128)S(1)}) custom-call(s32[8]{0:T(128)S(1)} %copy-done.2, f32[2,128,16,128]{3,2,1,0:T(8,128)S(1)} %copy-done, f32[1,2,512,128]{3,2,1,0:T(8,128)S(1)} %take.3.refs_0_.refs_3_, f32[1,2,512,128]{3,2,1,0:T(8,128)S(1)} %collective-permute-done.1.refs_1_.refs_4_, ...), custom_call_target="tpu_custom_call" | custom-call | flops 134217728 | bytes 3145728 | tf_op jit(solution)/shard_map/prefill/pallas_call | solution.py:178
  19.8 0.0 collective-permute-done.2.refs_0_
  19.8 5.3 %collective-permute-done.3.refs_1_ = f32[2,2,1,88,128]{4,3,2,1,0:T(8,128)S(1)} collective-permute-done((f32[2,2,1,88,128]{4,3,2,1,0:T(8,128)S(1)}, f32[2,2,1,88,128]{4,3,2,1,0:T(8,128)S(1)}, u32[]{:S(2)}, u32[]{:S(2)}) %collective-permute-start.3) | collective-permute-done | bytes 180256 | tf_op jit(solution)/shard_map/ppermute | solution.py:440
  25.1 0.1 collective-permute-start.4
  25.1 1.4 %collective-permute-done.4.refs_2_ = f32[2,2,1,88,128]{4,3,2,1,0:T(8,128)S(1)} collective-permute-done((f32[2,2,1,88,128]{4,3,2,1,0:T(8,128)S(1)}, f32[2,2,1,88,128]{4,3,2,1,0:T(8,128)S(1)}, u32[]{:S(2)}, u32[]{:S(2)}) %collective-permute-start.4) | collective-permute-done | bytes 180256 | tf_op jit(solution)/shard_map/ppermute | solution.py:446
  26.5 1.0 %decode.3 = (f32[2,128,128]{2,1,0:T(8,128)S(1)}, f32[2,8,128]{2,1,0:T(8,128)S(1)}) custom-call(f32[2,2,1,88,128]{4,3,2,1,0:T(8,128)S(1)} %collective-permute-done.2.refs_0_, f32[2,2,1,88,128]{4,3,2,1,0:T(8,128)S(1)} %collective-permute-done.3.refs_1_, f32[2,2,1,88,128]{4,3,2,1,0:T(8,128)S(1)} %collective-permute-done.4.refs_2_, ...), custom_call_target="tpu_custom_call" | custom-call | flops 8388608 | bytes 884736 | tf_op jit(solution)/shard_map/decode/pallas_call | solution.py:287
  27.6 1.5 %decode.4 = (f32[2,1,1,64,128]{4,3,2,1,0:T(8,128)S(1)}, f32[2,1,1,64,128]{4,3,2,1,0:T(8,128)S(1)}) custom-call(f32[2,2,1,88,128]{4,3,2,1,0:T(8,128)S(1)} %collective-permute-done.2.refs_0_, f32[2,2,1,88,128]{4,3,2,1,0:T(8,128)S(1)} %collective-permute-done.3.refs_1_, f32[2,2,1,88,128]{4,3,2,1,0:T(8,128)S(1)} %collective-permute-done.4.refs_2_, ...), custom_call_target="tpu_custom_call" | custom-call | flops 16777216 | bytes 1409024 | tf_op jit(solution)/shard_map/decode/pallas_call | solution.py:287
  29.1 0.0 collective-permute-done.refs_0_.refs_3_
  29.1 1.2 %decode.5 = (f32[2,2,1,64,128]{4,3,2,1,0:T(8,128)S(1)}, f32[2,2,1,64,128]{4,3,2,1,0:T(8,128)S(1)}) custom-call(f32[2,2,1,88,128]{4,3,2,1,0:T(8,128)S(1)} %collective-permute-done.2.refs_0_, f32[2,2,1,88,128]{4,3,2,1,0:T(8,128)S(1)} %collective-permute-done.3.refs_1_, f32[2,2,1,88,128]{4,3,2,1,0:T(8,128)S(1)} %collective-permute-done.4.refs_2_, ...), custom_call_target="tpu_custom_call" | custom-call | flops 8388608 | bytes 884736 | tf_op jit(solution)/shard_map/decode/pallas_call | solution.py:287
  30.2 0.2 collective-permute-start.5
  30.4 1.2 %collective-permute-done.5.back = f32[2,2,1,64,128]{4,3,2,1,0:T(8,128)S(1)} collective-permute-done((f32[2,2,1,64,128]{4,3,2,1,0:T(8,128)S(1)}, f32[2,2,1,64,128]{4,3,2,1,0:T(8,128)S(1)}, u32[]{:S(2)}, u32[]{:S(2)}) %collective-permute-start.5) | collective-permute-done | bytes 131104 | tf_op jit(solution)/shard_map/ppermute | solution.py:455
  31.7 7.3 %collective-permute-start.6 = (f32[2,2,1,64,128]{4,3,2,1,0:T(8,128)S(1)}, f32[2,2,1,64,128]{4,3,2,1,0:T(8,128)S(1)}, u32[]{:S(2)}, u32[]{:S(2)}) collective-permute-start(f32[2,2,1,64,128]{4,3,2,1,0:T(8,128)S(1)} %get-tuple-element.30), channel_id=1, source_target_pairs={{0,0},{8,1},{4,2},{12,3},{1,4},{9,5},{5,6},{13,7},{2,8},{10,9},{6,... | collective-permute-start | bytes 393224 | tf_op jit(solution)/shard_map/ppermute | solution.py:456
  39.0 0.1 collective-permute-start.7
  39.1 3.9 %prefill.5 = (f32[2,128,16,128]{3,2,1,0:T(8,128)}, f32[8,128]{1,0:T(8,128)}) custom-call(s32[8]{0:T(128)S(1)} %copy-done.2, f32[2,128,16,128]{3,2,1,0:T(8,128)S(1)} %copy-done, f32[1,2,512,128]{3,2,1,0:T(8,128)S(1)} %collective-permute-done.refs_0_.refs_3_, f32[2,128,1024]{2,1,0:T(8,128)S(1)} %get-tuple-element.18.refs_1_, ...), custom_call_target="tpu_custom_call", output_to_operand_aliasing={{0}: (5, {})} | custom-call | flops 67108864 | bytes 2621440 | tf_op jit(solution)/shard_map/prefill/pallas_call | solution.py:178
  43.0 0.0 collective-permute-done.6
  43.0 2.2 %collective-permute-done.7 = f32[2,2,1,64,128]{4,3,2,1,0:T(8,128)S(1)} collective-permute-done((f32[2,2,1,64,128]{4,3,2,1,0:T(8,128)S(1)}, f32[2,2,1,64,128]{4,3,2,1,0:T(8,128)S(1)}, u32[]{:S(2)}, u32[]{:S(2)}) %collective-permute-start.7) | collective-permute-done | bytes 131104 | tf_op jit(solution)/shard_map/ppermute | solution.py:456
  45.3 0.7 %place.1 = f32[8,1,64,128]{3,2,1,0:T(8,128)} custom-call(f32[4,1,64,128]{3,2,1,0:T(8,128)S(1)} %bitcast.10, f32[4,1,64,128]{3,2,1,0:T(8,128)S(1)} %bitcast.11), custom_call_target="tpu_custom_call" | custom-call | tf_op jit(solution)/shard_map/place/pallas_call | solution.py:397
  (4 shorter events, 0.1 us)
Async XLA Ops:
  0.6 3.0 %copy-start.5 = (s32[8,1]{0,1:T(1,128)S(1)}, s32[8,1]{0,1:T(1,128)}, u32[]{:S(2)}) copy-start(s32[8,1]{0,1:T(1,128)} %param.11) | copy-start | bytes 100
  0.6 1.2 %copy-start.1 = (f32[2,2,256,2,128]{4,3,2,1,0:T(2,128)S(1)}, f32[2,2,256,2,128]{4,3,2,1,0:T(2,128)}, u32[]{:S(2)}) copy-start(f32[2,2,256,2,128]{4,3,2,1,0:T(2,128)} %param.6) | copy-start | bytes 3145732
  1.9 1.8 %copy-start.3 = (f32[8,1,4,16,128]{4,3,2,1,0:T(8,128)S(1)}, f32[8,1,4,16,128]{4,3,2,1,0:T(8,128)}, u32[]{:S(2)}) copy-start(f32[8,1,4,16,128]{4,3,2,1,0:T(8,128)} %param.8) | copy-start | bytes 786436
  1.9 1.8 %copy-start.4 = (f32[8,1,4,2,2,128]{5,4,3,2,1,0:T(2,128)S(1)}, f32[8,1,4,2,2,128]{5,4,3,2,1,0:T(2,128)}, u32[]{:S(2)}) copy-start(f32[8,1,4,2,2,128]{5,4,3,2,1,0:T(2,128)} %param.9) | copy-start | bytes 196612
  1.9 12.9 %collective-permute-start.1 = (f32[1,2,512,128]{3,2,1,0:T(8,128)S(1)}, f32[1,2,512,128]{3,2,1,0:T(8,128)S(1)}, u32[]{:S(2)}, u32[]{:S(2)}) collective-permute-start(f32[1,2,512,128]{3,2,1,0:T(8,128)S(1)} %take.3.refs_0_.refs_3_), channel_id=1, source_target_pairs={{16,0},{0,16},{17,1},{1,17},{18,2},{2,18},{19,3},{3,19},{20,4},{4,... | collective-permute-start | bytes 1572872 | tf_op jit(solution)/shard_map/ppermute | solution.py:421
  2.3 26.7 %collective-permute-start = (f32[1,2,512,128]{3,2,1,0:T(8,128)S(1)}, f32[1,2,512,128]{3,2,1,0:T(8,128)S(1)}, u32[]{:S(2)}, u32[]{:S(2)}) collective-permute-start(f32[1,2,512,128]{3,2,1,0:T(8,128)S(1)} %take.2.refs_1_.refs_0_.refs_3_), channel_id=1, source_target_pairs={{16,0},{0,16},{17,1},{1,17},{18,2},{2,18},{19,3},{3,19},{20,4},{4,... | collective-permute-start | bytes 1572872 | tf_op jit(solution)/shard_map/ppermute | solution.py:421
  3.7 7.1 %copy-start = (f32[2,128,16,128]{3,2,1,0:T(8,128)S(1)}, f32[2,128,16,128]{3,2,1,0:T(8,128)}, u32[]{:S(2)}) copy-start(f32[2,128,16,128]{3,2,1,0:T(8,128)} %q_ref.5) | copy-start | bytes 6291460
  3.7 7.1 %copy-start.2 = (s32[8]{0:T(128)S(1)}, s32[8]{0:T(128)}, u32[]{:S(2)}) copy-start(s32[8]{0:T(128)} %lengths.6) | copy-start | bytes 100
  4.3 15.4 %collective-permute-start.2 = (f32[2,2,1,88,128]{4,3,2,1,0:T(8,128)S(1)}, f32[2,2,1,88,128]{4,3,2,1,0:T(8,128)S(1)}, u32[]{:S(2)}, u32[]{:S(2)}) collective-permute-start(f32[2,2,1,88,128]{4,3,2,1,0:T(8,128)S(1)} %get-tuple-element.17.refs_1_), channel_id=1, source_target_pairs={{0,0},{1,8},{2,4},{3,12},{4,1},{5,9},{6,5},{7,13},{8,2},{9,10},{10... | collective-permute-start | bytes 540680 | tf_op jit(solution)/shard_map/ppermute | solution.py:440
  10.6 14.4 %collective-permute-start.3 = (f32[2,2,1,88,128]{4,3,2,1,0:T(8,128)S(1)}, f32[2,2,1,88,128]{4,3,2,1,0:T(8,128)S(1)}, u32[]{:S(2)}, u32[]{:S(2)}) collective-permute-start(f32[2,2,1,88,128]{4,3,2,1,0:T(8,128)S(1)} %get-tuple-element.22), channel_id=1, source_target_pairs={{0,8},{1,0},{2,12},{3,4},{4,9},{5,1},{6,13},{7,5},{8,10},{9,2},{10... | collective-permute-start | bytes 540680 | tf_op jit(solution)/shard_map/ppermute | solution.py:440
  25.1 1.5 %collective-permute-start.4 = (f32[2,2,1,88,128]{4,3,2,1,0:T(8,128)S(1)}, f32[2,2,1,88,128]{4,3,2,1,0:T(8,128)S(1)}, u32[]{:S(2)}, u32[]{:S(2)}) collective-permute-start(f32[2,2,1,88,128]{4,3,2,1,0:T(8,128)S(1)} %other_side.1), channel_id=1, source_target_pairs={{0,4},{4,0},{8,12},{12,8},{1,5},{5,1},{9,13},{13,9},{2,6},{6,2},{1... | collective-permute-start | bytes 540680 | tf_op jit(solution)/shard_map/ppermute | solution.py:446
  30.2 1.4 %collective-permute-start.5 = (f32[2,2,1,64,128]{4,3,2,1,0:T(8,128)S(1)}, f32[2,2,1,64,128]{4,3,2,1,0:T(8,128)S(1)}, u32[]{:S(2)}, u32[]{:S(2)}) collective-permute-start(f32[2,2,1,64,128]{4,3,2,1,0:T(8,128)S(1)} %get-tuple-element.29), channel_id=1, source_target_pairs={{0,4},{4,0},{8,12},{12,8},{1,5},{5,1},{9,13},{13,9},{2,6},{6,2},{1... | collective-permute-start | bytes 393224 | tf_op jit(solution)/shard_map/ppermute | solution.py:455
  31.7 11.4 %collective-permute-start.6 = (f32[2,2,1,64,128]{4,3,2,1,0:T(8,128)S(1)}, f32[2,2,1,64,128]{4,3,2,1,0:T(8,128)S(1)}, u32[]{:S(2)}, u32[]{:S(2)}) collective-permute-start(f32[2,2,1,64,128]{4,3,2,1,0:T(8,128)S(1)} %get-tuple-element.30), channel_id=1, source_target_pairs={{0,0},{8,1},{4,2},{12,3},{1,4},{9,5},{5,6},{13,7},{2,8},{10,9},{6,... | collective-permute-start | bytes 393224 | tf_op jit(solution)/shard_map/ppermute | solution.py:456
  39.0 6.2 %collective-permute-start.7 = (f32[2,2,1,64,128]{4,3,2,1,0:T(8,128)S(1)}, f32[2,2,1,64,128]{4,3,2,1,0:T(8,128)S(1)}, u32[]{:S(2)}, u32[]{:S(2)}) collective-permute-start(f32[2,2,1,64,128]{4,3,2,1,0:T(8,128)S(1)} %get-tuple-element.31), channel_id=1, source_target_pairs={{8,0},{0,1},{12,2},{4,3},{9,4},{1,5},{13,6},{5,7},{10,8},{2,9},{14... | collective-permute-start | bytes 393224 | tf_op jit(solution)/shard_map/ppermute | solution.py:456

commit v4 on v3

--- a/solution.py
+++ b/solution.py
@@ -323,7 +323,7 @@
     _, nreq, per, rows, dim = outs[0].shape
     q_rows, kv_rows = q_ref.shape[2], kv_ref.shape[2]
     for j, out in enumerate(outs):
-        pair = lax.rem(lax.axis_index("rep") + j, half)
+        pair = lax.rem(lax.axis_index("rep") + (j + 1), half)
         for c in range(2):
             for i in range(nreq):
                 request = (pair * 2 + c) * nreq + i
@@ -388,7 +388,7 @@
     o_ref, count = refs[-1], len(refs) - 1
     size = refs[0].shape[0]
     for j in range(count):
-        o_ref[pl.ds(lax.rem(lax.axis_index("rep") + j, count) * size, size)] = refs[j][...]
+        o_ref[pl.ds(lax.rem(lax.axis_index("rep") + (j + 1), count) * size, size)] = refs[j][...]
 
 
 def place(pieces):
@@ -422,7 +422,7 @@
 
     routes = [
         [
-            (s * rep_count + t, ((t + j) % half * 2 + t // half) * rep_count + s)
+            (s * rep_count + t, ((t + j + 1) % half * 2 + t // half) * rep_count + s)
             for s in range(head_count)
             for t in range(rep_count)
         ]

time: 46.3 us -> 44.1 us (0.952)
  the two profiles are of different devices: /device:TPU:7 before, /device:TPU:1 now
where the time goes in v4:
time: 44.1 us; the launch traced here: 43.9 us
  Pallas kernels  16.6 us (38%)
  starting transfers between devices  13 us (29%)
  waiting for transfers between devices  12.2 us (28%)
  local copies, waits for them, and re-layouts  1.32 us (3%)
  between operations  0.79 us (2%)
    pallas_call x3, Pallas kernels, prefill_request(): pl.pallas_call(functools.partial(prefill_kernel, (index, blocks, first_bl...  11.4 us
    ppermute x2, starting transfers between devices, on_device(): lax.ppermute(packets[j], ('head', 'rep'), routes[j])  5.57 us
    ppermute x2, starting transfers between devices, on_device(): lax.ppermute(joined[j], ('head', 'rep'), [(b, a) for a, b in routes[j]])  4.93 us
    ppermute x2, waiting for transfers between devices, on_device(): lax.ppermute(packets[j], ('head', 'rep'), routes[j])  4.32 us
    pallas_call x3, Pallas kernels, decode_request(): pl.pallas_call(functools.partial(decode_kernel, plan, heads, group, steps...  3.67 us
    ppermute x2, waiting for transfers between devices, on_device(): held[i].append(lax.ppermute(own[i], 'ctx', perm))  2.65 us
    ppermute x2, waiting for transfers between devices, on_device(): lax.ppermute(joined[j], ('head', 'rep'), [(b, a) for a, b in routes[j]])  2.62 us
    ppermute x2, starting transfers between devices, on_device(): held[i].append(lax.ppermute(own[i], 'ctx', perm))  2.19 us
  transfers between devices with their start and end apart: 8, of which 5 were waited for; matrix products, arithmetic and copies ran while one was open for 0% of the time, Pallas kernels for 33%

profile of v4, /device:TPU:1, one launch (start us, length us, event | category | flops | bytes accessed | tf_op | source)
XLA Modules:
  0.0 43.9 jit_solution(637035121648862015)
XLA Ops:
  0.6 0.0 copy-start.5
  0.6 0.0 copy-start.1
  0.7 1.2 %copy-done.1 = f32[2,2,256,2,128]{4,3,2,1,0:T(2,128)S(1)} copy-done((f32[2,2,256,2,128]{4,3,2,1,0:T(2,128)S(1)}, f32[2,2,256,2,128]{4,3,2,1,0:T(2,128)}, u32[]{:S(2)}) %copy-start.1) | copy-done | bytes 1048600
  1.9 0.0 copy-start.3
  1.9 0.0 copy-start.4
  1.9 2.1 %collective-permute-start.1 = (f32[1,2,512,128]{3,2,1,0:T(8,128)S(1)}, f32[1,2,512,128]{3,2,1,0:T(8,128)S(1)}, u32[]{:S(2)}, u32[]{:S(2)}) collective-permute-start(f32[1,2,512,128]{3,2,1,0:T(8,128)S(1)} %take.3.refs_0_.refs_3_), channel_id=1, source_target_pairs={{16,0},{0,16},{17,1},{1,17},{18,2},{2,18},{19,3},{3,19},{20,4},{4,... | collective-permute-start | bytes 1572872 | tf_op jit(solution)/shard_map/ppermute | solution.py:421
  4.1 0.1 collective-permute-start
  4.2 0.0 copy-done.5
  4.2 0.1 copy.9.lengths
  4.3 0.0 copy-done.3
  4.3 0.0 copy-done.4
  4.3 0.0 copy-start
  4.3 0.0 copy-start.2
  4.3 0.6 %pack.1 = (f32[2,2,1,88,128]{4,3,2,1,0:T(8,128)S(1)}, f32[2,2,1,88,128]{4,3,2,1,0:T(8,128)S(1)}) custom-call(s32[8,1]{1,0:T(8,128)S(1)} %copy.9.lengths, f32[8,1,64,128]{3,2,1,0:T(8,128)S(1)} %bitcast.12, f32[8,1,16,128]{3,2,1,0:T(8,128)S(1)} %bitcast.13, f32[1,2,512,128]{3,2,1,0:T(8,128)S(1)} %take.3.refs_0_.refs_3_, ...), custom_call_target="tpu_custom_call" | custom-call | flops 99999997952 | bytes 1000000 | tf_op jit(solution)/shard_map/pack/pallas_call | solution.py:340
  4.9 3.7 %collective-permute-start.2 = (f32[2,2,1,88,128]{4,3,2,1,0:T(8,128)S(1)}, f32[2,2,1,88,128]{4,3,2,1,0:T(8,128)S(1)}, u32[]{:S(2)}, u32[]{:S(2)}) collective-permute-start(f32[2,2,1,88,128]{4,3,2,1,0:T(8,128)S(1)} %get-tuple-element.17.refs_1_), channel_id=1, source_target_pairs={{0,8},{1,0},{2,12},{3,4},{4,9},{5,1},{6,13},{7,5},{8,10},{9,2},{10... | collective-permute-start | bytes 540680 | tf_op jit(solution)/shard_map/ppermute | solution.py:440
  8.6 1.9 %collective-permute-start.3 = (f32[2,2,1,88,128]{4,3,2,1,0:T(8,128)S(1)}, f32[2,2,1,88,128]{4,3,2,1,0:T(8,128)S(1)}, u32[]{:S(2)}, u32[]{:S(2)}) collective-permute-start(f32[2,2,1,88,128]{4,3,2,1,0:T(8,128)S(1)} %get-tuple-element.22), channel_id=1, source_target_pairs={{0,0},{1,8},{2,4},{3,12},{4,1},{5,9},{6,5},{7,13},{8,2},{9,10},{10... | collective-permute-start | bytes 540680 | tf_op jit(solution)/shard_map/ppermute | solution.py:440
  10.5 0.0 copy-done
  10.5 0.0 copy-done.2
  10.5 2.5 %prefill.3 = (f32[2,128,1024]{2,1,0:T(8,128)S(1)}, f32[2,8,1024]{2,1,0:T(8,128)S(1)}) custom-call(s32[8]{0:T(128)S(1)} %copy-done.2, f32[2,128,16,128]{3,2,1,0:T(8,128)S(1)} %copy-done, f32[1,2,512,128]{3,2,1,0:T(8,128)S(1)} %take.2.refs_1_.refs_0_.refs_3_, f32[2,2,1,88,128]{4,3,2,1,0:T(8,128)S(1)} %get-tuple-element.17.refs_1_), custom_call_target="tpu_custom_call" | custom-call | flops 67108864 | bytes 2621440 | tf_op jit(solution)/shard_map/prefill/pallas_call | solution.py:178
  13.0 2.6 %collective-permute-done.1.refs_1_.refs_4_ = f32[1,2,512,128]{3,2,1,0:T(8,128)S(1)} collective-permute-done((f32[1,2,512,128]{3,2,1,0:T(8,128)S(1)}, f32[1,2,512,128]{3,2,1,0:T(8,128)S(1)}, u32[]{:S(2)}, u32[]{:S(2)}) %collective-permute-start.1) | collective-permute-done | bytes 524320 | tf_op jit(solution)/shard_map/ppermute | solution.py:421
  15.7 5.0 %prefill.4 = (f32[2,128,16,128]{3,2,1,0:T(8,128)}, f32[8,128]{1,0:T(8,128)S(1)}) custom-call(s32[8]{0:T(128)S(1)} %copy-done.2, f32[2,128,16,128]{3,2,1,0:T(8,128)S(1)} %copy-done, f32[1,2,512,128]{3,2,1,0:T(8,128)S(1)} %take.3.refs_0_.refs_3_, f32[1,2,512,128]{3,2,1,0:T(8,128)S(1)} %collective-permute-done.1.refs_1_.refs_4_, ...), custom_call_target="tpu_custom_call" | custom-call | flops 134217728 | bytes 3145728 | tf_op jit(solution)/shard_map/prefill/pallas_call | solution.py:178
  20.7 0.0 collective-permute-done.2.refs_0_
  20.7 4.3 %collective-permute-done.3.refs_1_ = f32[2,2,1,88,128]{4,3,2,1,0:T(8,128)S(1)} collective-permute-done((f32[2,2,1,88,128]{4,3,2,1,0:T(8,128)S(1)}, f32[2,2,1,88,128]{4,3,2,1,0:T(8,128)S(1)}, u32[]{:S(2)}, u32[]{:S(2)}) %collective-permute-start.3) | collective-permute-done | bytes 180256 | tf_op jit(solution)/shard_map/ppermute | solution.py:440
  25.0 0.1 collective-permute-start.4
  25.1 1.4 %collective-permute-done.4.refs_2_ = f32[2,2,1,88,128]{4,3,2,1,0:T(8,128)S(1)} collective-permute-done((f32[2,2,1,88,128]{4,3,2,1,0:T(8,128)S(1)}, f32[2,2,1,88,128]{4,3,2,1,0:T(8,128)S(1)}, u32[]{:S(2)}, u32[]{:S(2)}) %collective-permute-start.4) | collective-permute-done | bytes 180256 | tf_op jit(solution)/shard_map/ppermute | solution.py:446
  26.5 1.0 %decode.3 = (f32[2,128,128]{2,1,0:T(8,128)S(1)}, f32[2,8,128]{2,1,0:T(8,128)S(1)}) custom-call(f32[2,2,1,88,128]{4,3,2,1,0:T(8,128)S(1)} %collective-permute-done.2.refs_0_, f32[2,2,1,88,128]{4,3,2,1,0:T(8,128)S(1)} %collective-permute-done.3.refs_1_, f32[2,2,1,88,128]{4,3,2,1,0:T(8,128)S(1)} %collective-permute-done.4.refs_2_, ...), custom_call_target="tpu_custom_call" | custom-call | flops 8388608 | bytes 884736 | tf_op jit(solution)/shard_map/decode/pallas_call | solution.py:287
  27.5 1.5 %decode.4 = (f32[2,1,1,64,128]{4,3,2,1,0:T(8,128)S(1)}, f32[2,1,1,64,128]{4,3,2,1,0:T(8,128)S(1)}) custom-call(f32[2,2,1,88,128]{4,3,2,1,0:T(8,128)S(1)} %collective-permute-done.2.refs_0_, f32[2,2,1,88,128]{4,3,2,1,0:T(8,128)S(1)} %collective-permute-done.3.refs_1_, f32[2,2,1,88,128]{4,3,2,1,0:T(8,128)S(1)} %collective-permute-done.4.refs_2_, ...), custom_call_target="tpu_custom_call" | custom-call | flops 16777216 | bytes 1409024 | tf_op jit(solution)/shard_map/decode/pallas_call | solution.py:287
  29.0 0.0 collective-permute-done.refs_0_.refs_3_
  29.0 1.2 %decode.5 = (f32[2,2,1,64,128]{4,3,2,1,0:T(8,128)S(1)}, f32[2,2,1,64,128]{4,3,2,1,0:T(8,128)S(1)}) custom-call(f32[2,2,1,88,128]{4,3,2,1,0:T(8,128)S(1)} %collective-permute-done.2.refs_0_, f32[2,2,1,88,128]{4,3,2,1,0:T(8,128)S(1)} %collective-permute-done.3.refs_1_, f32[2,2,1,88,128]{4,3,2,1,0:T(8,128)S(1)} %collective-permute-done.4.refs_2_, ...), custom_call_target="tpu_custom_call" | custom-call | flops 8388608 | bytes 884736 | tf_op jit(solution)/shard_map/decode/pallas_call | solution.py:287
  30.2 0.2 collective-permute-start.5
  30.4 1.2 %collective-permute-done.5.back = f32[2,2,1,64,128]{4,3,2,1,0:T(8,128)S(1)} collective-permute-done((f32[2,2,1,64,128]{4,3,2,1,0:T(8,128)S(1)}, f32[2,2,1,64,128]{4,3,2,1,0:T(8,128)S(1)}, u32[]{:S(2)}, u32[]{:S(2)}) %collective-permute-start.5) | collective-permute-done | bytes 131104 | tf_op jit(solution)/shard_map/ppermute | solution.py:455
  31.6 2.6 %collective-permute-start.6 = (f32[2,2,1,64,128]{4,3,2,1,0:T(8,128)S(1)}, f32[2,2,1,64,128]{4,3,2,1,0:T(8,128)S(1)}, u32[]{:S(2)}, u32[]{:S(2)}) collective-permute-start(f32[2,2,1,64,128]{4,3,2,1,0:T(8,128)S(1)} %get-tuple-element.30), channel_id=1, source_target_pairs={{8,0},{0,1},{12,2},{4,3},{9,4},{1,5},{13,6},{5,7},{10,8},{2,9},{14... | collective-permute-start | bytes 393224 | tf_op jit(solution)/shard_map/ppermute | solution.py:456
  34.3 2.3 %collective-permute-start.7 = (f32[2,2,1,64,128]{4,3,2,1,0:T(8,128)S(1)}, f32[2,2,1,64,128]{4,3,2,1,0:T(8,128)S(1)}, u32[]{:S(2)}, u32[]{:S(2)}) collective-permute-start(f32[2,2,1,64,128]{4,3,2,1,0:T(8,128)S(1)} %get-tuple-element.31), channel_id=1, source_target_pairs={{0,0},{8,1},{4,2},{12,3},{1,4},{9,5},{5,6},{13,7},{2,8},{10,9},{6,... | collective-permute-start | bytes 393224 | tf_op jit(solution)/shard_map/ppermute | solution.py:456
  36.6 4.0 %prefill.5 = (f32[2,128,16,128]{3,2,1,0:T(8,128)}, f32[8,128]{1,0:T(8,128)}) custom-call(s32[8]{0:T(128)S(1)} %copy-done.2, f32[2,128,16,128]{3,2,1,0:T(8,128)S(1)} %copy-done, f32[1,2,512,128]{3,2,1,0:T(8,128)S(1)} %collective-permute-done.refs_0_.refs_3_, f32[2,128,1024]{2,1,0:T(8,128)S(1)} %get-tuple-element.18.refs_1_, ...), custom_call_target="tpu_custom_call", output_to_operand_aliasing={{0}: (5, {})} | custom-call | flops 67108864 | bytes 2621440 | tf_op jit(solution)/shard_map/prefill/pallas_call | solution.py:178
  40.5 0.0 collective-permute-done.6
  40.5 2.6 %collective-permute-done.7 = f32[2,2,1,64,128]{4,3,2,1,0:T(8,128)S(1)} collective-permute-done((f32[2,2,1,64,128]{4,3,2,1,0:T(8,128)S(1)}, f32[2,2,1,64,128]{4,3,2,1,0:T(8,128)S(1)}, u32[]{:S(2)}, u32[]{:S(2)}) %collective-permute-start.7) | collective-permute-done | bytes 131104 | tf_op jit(solution)/shard_map/ppermute | solution.py:456
  43.2 0.7 %place.1 = f32[8,1,64,128]{3,2,1,0:T(8,128)} custom-call(f32[4,1,64,128]{3,2,1,0:T(8,128)S(1)} %bitcast.10, f32[4,1,64,128]{3,2,1,0:T(8,128)S(1)} %bitcast.11), custom_call_target="tpu_custom_call" | custom-call | tf_op jit(solution)/shard_map/place/pallas_call | solution.py:397
  (4 shorter events, 0.1 us)
Async XLA Ops:
  0.6 3.5 %copy-start.5 = (s32[8,1]{0,1:T(1,128)S(1)}, s32[8,1]{0,1:T(1,128)}, u32[]{:S(2)}) copy-start(s32[8,1]{0,1:T(1,128)} %param.11) | copy-start | bytes 100
  0.6 1.2 %copy-start.1 = (f32[2,2,256,2,128]{4,3,2,1,0:T(2,128)S(1)}, f32[2,2,256,2,128]{4,3,2,1,0:T(2,128)}, u32[]{:S(2)}) copy-start(f32[2,2,256,2,128]{4,3,2,1,0:T(2,128)} %param.6) | copy-start | bytes 3145732
  1.9 2.4 %copy-start.3 = (f32[8,1,4,16,128]{4,3,2,1,0:T(8,128)S(1)}, f32[8,1,4,16,128]{4,3,2,1,0:T(8,128)}, u32[]{:S(2)}) copy-start(f32[8,1,4,16,128]{4,3,2,1,0:T(8,128)} %param.8) | copy-start | bytes 786436
  1.9 2.4 %copy-start.4 = (f32[8,1,4,2,2,128]{5,4,3,2,1,0:T(2,128)S(1)}, f32[8,1,4,2,2,128]{5,4,3,2,1,0:T(2,128)}, u32[]{:S(2)}) copy-start(f32[8,1,4,2,2,128]{5,4,3,2,1,0:T(2,128)} %param.9) | copy-start | bytes 196612
  1.9 13.8 %collective-permute-start.1 = (f32[1,2,512,128]{3,2,1,0:T(8,128)S(1)}, f32[1,2,512,128]{3,2,1,0:T(8,128)S(1)}, u32[]{:S(2)}, u32[]{:S(2)}) collective-permute-start(f32[1,2,512,128]{3,2,1,0:T(8,128)S(1)} %take.3.refs_0_.refs_3_), channel_id=1, source_target_pairs={{16,0},{0,16},{17,1},{1,17},{18,2},{2,18},{19,3},{3,19},{20,4},{4,... | collective-permute-start | bytes 1572872 | tf_op jit(solution)/shard_map/ppermute | solution.py:421
  4.1 24.9 %collective-permute-start = (f32[1,2,512,128]{3,2,1,0:T(8,128)S(1)}, f32[1,2,512,128]{3,2,1,0:T(8,128)S(1)}, u32[]{:S(2)}, u32[]{:S(2)}) collective-permute-start(f32[1,2,512,128]{3,2,1,0:T(8,128)S(1)} %take.2.refs_1_.refs_0_.refs_3_), channel_id=1, source_target_pairs={{16,0},{0,16},{17,1},{1,17},{18,2},{2,18},{19,3},{3,19},{20,4},{4,... | collective-permute-start | bytes 1572872 | tf_op jit(solution)/shard_map/ppermute | solution.py:421
  4.3 6.2 %copy-start = (f32[2,128,16,128]{3,2,1,0:T(8,128)S(1)}, f32[2,128,16,128]{3,2,1,0:T(8,128)}, u32[]{:S(2)}) copy-start(f32[2,128,16,128]{3,2,1,0:T(8,128)} %q_ref.5) | copy-start | bytes 6291460
  4.3 6.2 %copy-start.2 = (s32[8]{0:T(128)S(1)}, s32[8]{0:T(128)}, u32[]{:S(2)}) copy-start(s32[8]{0:T(128)} %lengths.6) | copy-start | bytes 100
  4.9 15.7 %collective-permute-start.2 = (f32[2,2,1,88,128]{4,3,2,1,0:T(8,128)S(1)}, f32[2,2,1,88,128]{4,3,2,1,0:T(8,128)S(1)}, u32[]{:S(2)}, u32[]{:S(2)}) collective-permute-start(f32[2,2,1,88,128]{4,3,2,1,0:T(8,128)S(1)} %get-tuple-element.17.refs_1_), channel_id=1, source_target_pairs={{0,8},{1,0},{2,12},{3,4},{4,9},{5,1},{6,13},{7,5},{8,10},{9,2},{10... | collective-permute-start | bytes 540680 | tf_op jit(solution)/shard_map/ppermute | solution.py:440
  8.6 16.4 %collective-permute-start.3 = (f32[2,2,1,88,128]{4,3,2,1,0:T(8,128)S(1)}, f32[2,2,1,88,128]{4,3,2,1,0:T(8,128)S(1)}, u32[]{:S(2)}, u32[]{:S(2)}) collective-permute-start(f32[2,2,1,88,128]{4,3,2,1,0:T(8,128)S(1)} %get-tuple-element.22), channel_id=1, source_target_pairs={{0,0},{1,8},{2,4},{3,12},{4,1},{5,9},{6,5},{7,13},{8,2},{9,10},{10... | collective-permute-start | bytes 540680 | tf_op jit(solution)/shard_map/ppermute | solution.py:440
  25.0 1.5 %collective-permute-start.4 = (f32[2,2,1,88,128]{4,3,2,1,0:T(8,128)S(1)}, f32[2,2,1,88,128]{4,3,2,1,0:T(8,128)S(1)}, u32[]{:S(2)}, u32[]{:S(2)}) collective-permute-start(f32[2,2,1,88,128]{4,3,2,1,0:T(8,128)S(1)} %other_side.1), channel_id=1, source_target_pairs={{0,4},{4,0},{8,12},{12,8},{1,5},{5,1},{9,13},{13,9},{2,6},{6,2},{1... | collective-permute-start | bytes 540680 | tf_op jit(solution)/shard_map/ppermute | solution.py:446
  30.2 1.4 %collective-permute-start.5 = (f32[2,2,1,64,128]{4,3,2,1,0:T(8,128)S(1)}, f32[2,2,1,64,128]{4,3,2,1,0:T(8,128)S(1)}, u32[]{:S(2)}, u32[]{:S(2)}) collective-permute-start(f32[2,2,1,64,128]{4,3,2,1,0:T(8,128)S(1)} %get-tuple-element.29), channel_id=1, source_target_pairs={{0,4},{4,0},{8,12},{12,8},{1,5},{5,1},{9,13},{13,9},{2,6},{6,2},{1... | collective-permute-start | bytes 393224 | tf_op jit(solution)/shard_map/ppermute | solution.py:455
  31.6 8.9 %collective-permute-start.6 = (f32[2,2,1,64,128]{4,3,2,1,0:T(8,128)S(1)}, f32[2,2,1,64,128]{4,3,2,1,0:T(8,128)S(1)}, u32[]{:S(2)}, u32[]{:S(2)}) collective-permute-start(f32[2,2,1,64,128]{4,3,2,1,0:T(8,128)S(1)} %get-tuple-element.30), channel_id=1, source_target_pairs={{8,0},{0,1},{12,2},{4,3},{9,4},{1,5},{13,6},{5,7},{10,8},{2,9},{14... | collective-permute-start | bytes 393224 | tf_op jit(solution)/shard_map/ppermute | solution.py:456
  34.3 8.9 %collective-permute-start.7 = (f32[2,2,1,64,128]{4,3,2,1,0:T(8,128)S(1)}, f32[2,2,1,64,128]{4,3,2,1,0:T(8,128)S(1)}, u32[]{:S(2)}, u32[]{:S(2)}) collective-permute-start(f32[2,2,1,64,128]{4,3,2,1,0:T(8,128)S(1)} %get-tuple-element.31), channel_id=1, source_target_pairs={{0,0},{8,1},{4,2},{12,3},{1,4},{9,5},{5,6},{13,7},{2,8},{10,9},{6,... | collective-permute-start | bytes 393224 | tf_op jit(solution)/shard_map/ppermute | solution.py:456

commit v5 on v4

--- a/solution.py
+++ b/solution.py
@@ -86,6 +86,14 @@
 
 def state_shapes(heads, dim, rows):
     return [jax.ShapeDtypeStruct((heads, dim, rows), F32), jax.ShapeDtypeStruct((heads, 8, rows), F32)]
+
+
+def pair_of(t, j, half):
+    return (t // 2 + j + 1) % half
+
+
+def core_of(t, half):
+    return (t + t // 2) % 2
 
 
 def block_starts(count, first, block_len):
@@ -323,7 +331,7 @@
     _, nreq, per, rows, dim = outs[0].shape
     q_rows, kv_rows = q_ref.shape[2], kv_ref.shape[2]
     for j, out in enumerate(outs):
-        pair = lax.rem(lax.axis_index("rep") + (j + 1), half)
+        pair = pair_of(lax.axis_index("rep"), j, half)
         for c in range(2):
             for i in range(nreq):
                 request = (pair * 2 + c) * nreq + i
@@ -388,7 +396,7 @@
     o_ref, count = refs[-1], len(refs) - 1
     size = refs[0].shape[0]
     for j in range(count):
-        o_ref[pl.ds(lax.rem(lax.axis_index("rep") + (j + 1), count) * size, size)] = refs[j][...]
+        o_ref[pl.ds(pair_of(lax.axis_index("rep"), j, count) * size, size)] = refs[j][...]
 
 
 def place(pieces):
@@ -422,7 +430,7 @@
 
     routes = [
         [
-            (s * rep_count + t, ((t + j + 1) % half * 2 + t // half) * rep_count + s)
+            (s * rep_count + t, (pair_of(t, j, half) * 2 + core_of(t, half)) * rep_count + s)
             for s in range(head_count)
             for t in range(rep_count)
         ]
@@ -445,9 +453,8 @@
         prefill_out, token = prefill_request(i, lengths, prefill_q, held[i], 0, heads, scale, carried=prefill_out, after=(token,))
     far = lax.ppermute(other_side(near, (token,)), "head", swap)
     ready = [decode_request(i, near, far, held[i], 0, heads, group, steps, scale) for i in range(last)]
-    decode_state = decode_request(last, near, far, held[last][:1], 0, heads, group, steps, scale, finish=False)
     kept, sent = decode_request(
-        last, near, far, held[last][1:], 1, heads, group, steps, scale, state=decode_state, ready=ready
+        last, near, far, held[last], 0, heads, group, steps, scale, ready=ready, after=(prefill_state[0],)
     )
     prefill_out, _ = prefill_request(
         last, lengths, prefill_q, held[last][1:], 1, heads, scale, state=prefill_state, carried=prefill_out

time: 44.1 us -> 43.3 us (0.982)
  the two profiles are of different devices: /device:TPU:1 before, /device:TPU:6 now
where the time goes in v5:
time: 43.3 us; the launch traced here: 43.1 us
  Pallas kernels  15.9 us (37%)
  starting transfers between devices  14.8 us (34%)
  waiting for transfers between devices  10.3 us (24%)
  local copies, waits for them, and re-layouts  1.32 us (3%)
  between operations  0.79 us (2%)
    pallas_call x3, Pallas kernels, prefill_request(): pl.pallas_call(functools.partial(prefill_kernel, (index, blocks, first_bl...  11.4 us
    ppermute x2, starting transfers between devices, on_device(): lax.ppermute(joined[j], ('head', 'rep'), [(b, a) for a, b in routes[j]])  6.76 us
    ppermute x2, waiting for transfers between devices, on_device(): held[i].append(lax.ppermute(own[i], 'ctx', perm))  6.07 us
    ppermute x2, starting transfers between devices, on_device(): lax.ppermute(packets[j], ('head', 'rep'), routes[j])  4.56 us
    pallas_call x2, Pallas kernels, decode_request(): pl.pallas_call(functools.partial(decode_kernel, plan, heads, group, steps...  2.91 us
    ppermute x2, starting transfers between devices, on_device(): held[i].append(lax.ppermute(own[i], 'ctx', perm))  2.16 us
    ppermute x2, waiting for transfers between devices, on_device(): lax.ppermute(joined[j], ('head', 'rep'), [(b, a) for a, b in routes[j]])  1.84 us
    ppermute x1, waiting for transfers between devices, on_device(): joined = join(kept, lax.ppermute(sent, 'head', swap))  1.33 us
  transfers between devices with their start and end apart: 8, of which 5 were waited for; matrix products, arithmetic and copies ran while one was open for 0% of the time, Pallas kernels for 32%

profile of v5, /device:TPU:6, one launch (start us, length us, event | category | flops | bytes accessed | tf_op | source)
XLA Modules:
  0.0 43.1 jit_solution(13170696650946523769)
XLA Ops:
  0.6 0.0 copy-start.5
  0.6 0.0 copy-start.1
  0.7 1.2 %copy-done.1 = f32[2,2,256,2,128]{4,3,2,1,0:T(2,128)S(1)} copy-done((f32[2,2,256,2,128]{4,3,2,1,0:T(2,128)S(1)}, f32[2,2,256,2,128]{4,3,2,1,0:T(2,128)}, u32[]{:S(2)}) %copy-start.1) | copy-done | bytes 1048600
  1.9 0.0 copy-start.3
  1.9 0.0 copy-start.4
  1.9 0.6 %collective-permute-start.1 = (f32[1,2,512,128]{3,2,1,0:T(8,128)S(1)}, f32[1,2,512,128]{3,2,1,0:T(8,128)S(1)}, u32[]{:S(2)}, u32[]{:S(2)}) collective-permute-start(f32[1,2,512,128]{3,2,1,0:T(8,128)S(1)} %take.3.refs_0_.refs_3_), channel_id=1, source_target_pairs={{16,0},{0,16},{17,1},{1,17},{18,2},{2,18},{19,3},{3,19},{20,4},{4,... | collective-permute-start | bytes 1572872 | tf_op jit(solution)/shard_map/ppermute | solution.py:429
  2.6 1.6 %collective-permute-start = (f32[1,2,512,128]{3,2,1,0:T(8,128)S(1)}, f32[1,2,512,128]{3,2,1,0:T(8,128)S(1)}, u32[]{:S(2)}, u32[]{:S(2)}) collective-permute-start(f32[1,2,512,128]{3,2,1,0:T(8,128)S(1)} %take.2.refs_1_.refs_0_.refs_3_), channel_id=1, source_target_pairs={{16,0},{0,16},{17,1},{1,17},{18,2},{2,18},{19,3},{3,19},{20,4},{4,... | collective-permute-start | bytes 1572872 | tf_op jit(solution)/shard_map/ppermute | solution.py:429
  4.1 0.0 copy-done.5
  4.1 0.1 copy.9.lengths
  4.2 0.0 copy-done.3
  4.2 0.0 copy-done.4
  4.2 0.0 copy-start
  4.2 0.0 copy-start.2
  4.2 0.6 %pack.1 = (f32[2,2,1,88,128]{4,3,2,1,0:T(8,128)S(1)}, f32[2,2,1,88,128]{4,3,2,1,0:T(8,128)S(1)}) custom-call(s32[8,1]{1,0:T(8,128)S(1)} %copy.9.lengths, f32[8,1,64,128]{3,2,1,0:T(8,128)S(1)} %bitcast.12, f32[8,1,16,128]{3,2,1,0:T(8,128)S(1)} %bitcast.13, f32[1,2,512,128]{3,2,1,0:T(8,128)S(1)} %take.3.refs_0_.refs_3_, ...), custom_call_target="tpu_custom_call" | custom-call | flops 99999997952 | bytes 1000000 | tf_op jit(solution)/shard_map/pack/pallas_call | solution.py:348
  4.9 2.7 %collective-permute-start.2 = (f32[2,2,1,88,128]{4,3,2,1,0:T(8,128)S(1)}, f32[2,2,1,88,128]{4,3,2,1,0:T(8,128)S(1)}, u32[]{:S(2)}, u32[]{:S(2)}) collective-permute-start(f32[2,2,1,88,128]{4,3,2,1,0:T(8,128)S(1)} %get-tuple-element.15.refs_1_), channel_id=1, source_target_pairs={{0,8},{1,12},{2,4},{3,0},{4,9},{5,13},{6,5},{7,1},{8,10},{9,14},{1... | collective-permute-start | bytes 540680 | tf_op jit(solution)/shard_map/ppermute | solution.py:448
  7.5 1.9 %collective-permute-start.3 = (f32[2,2,1,88,128]{4,3,2,1,0:T(8,128)S(1)}, f32[2,2,1,88,128]{4,3,2,1,0:T(8,128)S(1)}, u32[]{:S(2)}, u32[]{:S(2)}) collective-permute-start(f32[2,2,1,88,128]{4,3,2,1,0:T(8,128)S(1)} %get-tuple-element.20), channel_id=1, source_target_pairs={{0,0},{1,4},{2,12},{3,8},{4,1},{5,5},{6,13},{7,9},{8,2},{9,6},{10,... | collective-permute-start | bytes 540680 | tf_op jit(solution)/shard_map/ppermute | solution.py:448
  9.5 0.0 copy-done
  9.5 0.0 copy-done.2
  9.5 2.5 %prefill.3 = (f32[2,128,1024]{2,1,0:T(8,128)S(1)}, f32[2,8,1024]{2,1,0:T(8,128)S(1)}) custom-call(s32[8]{0:T(128)S(1)} %copy-done.2, f32[2,128,16,128]{3,2,1,0:T(8,128)S(1)} %copy-done, f32[1,2,512,128]{3,2,1,0:T(8,128)S(1)} %take.2.refs_1_.refs_0_.refs_3_, f32[2,2,1,88,128]{4,3,2,1,0:T(8,128)S(1)} %get-tuple-element.15.refs_1_), custom_call_target="tpu_custom_call" | custom-call | flops 67108864 | bytes 2621440 | tf_op jit(solution)/shard_map/prefill/pallas_call | solution.py:186
  12.0 4.8 %collective-permute-done.1.refs_1_.refs_4_ = f32[1,2,512,128]{3,2,1,0:T(8,128)S(1)} collective-permute-done((f32[1,2,512,128]{3,2,1,0:T(8,128)S(1)}, f32[1,2,512,128]{3,2,1,0:T(8,128)S(1)}, u32[]{:S(2)}, u32[]{:S(2)}) %collective-permute-start.1) | collective-permute-done | bytes 524320 | tf_op jit(solution)/shard_map/ppermute | solution.py:429
  16.8 5.0 %prefill.4 = (f32[2,128,16,128]{3,2,1,0:T(8,128)}, f32[8,128]{1,0:T(8,128)S(1)}) custom-call(s32[8]{0:T(128)S(1)} %copy-done.2, f32[2,128,16,128]{3,2,1,0:T(8,128)S(1)} %copy-done, f32[1,2,512,128]{3,2,1,0:T(8,128)S(1)} %take.3.refs_0_.refs_3_, f32[1,2,512,128]{3,2,1,0:T(8,128)S(1)} %collective-permute-done.1.refs_1_.refs_4_, ...), custom_call_target="tpu_custom_call" | custom-call | flops 134217728 | bytes 3145728 | tf_op jit(solution)/shard_map/prefill/pallas_call | solution.py:186
  21.8 0.0 collective-permute-done.2.refs_0_
  21.8 0.0 collective-permute-done.3.refs_1_
  21.8 1.3 %collective-permute-start.4 = (f32[2,2,1,88,128]{4,3,2,1,0:T(8,128)S(1)}, f32[2,2,1,88,128]{4,3,2,1,0:T(8,128)S(1)}, u32[]{:S(2)}, u32[]{:S(2)}) collective-permute-start(f32[2,2,1,88,128]{4,3,2,1,0:T(8,128)S(1)} %other_side.1), channel_id=1, source_target_pairs={{0,4},{4,0},{8,12},{12,8},{1,5},{5,1},{9,13},{13,9},{2,6},{6,2},{1... | collective-permute-start | bytes 540680 | tf_op jit(solution)/shard_map/ppermute | solution.py:454
  23.1 1.0 %collective-permute-done.4.refs_2_ = f32[2,2,1,88,128]{4,3,2,1,0:T(8,128)S(1)} collective-permute-done((f32[2,2,1,88,128]{4,3,2,1,0:T(8,128)S(1)}, f32[2,2,1,88,128]{4,3,2,1,0:T(8,128)S(1)}, u32[]{:S(2)}, u32[]{:S(2)}) %collective-permute-start.4) | collective-permute-done | bytes 180256 | tf_op jit(solution)/shard_map/ppermute | solution.py:454
  24.2 1.5 %decode.2 = (f32[2,1,1,64,128]{4,3,2,1,0:T(8,128)S(1)}, f32[2,1,1,64,128]{4,3,2,1,0:T(8,128)S(1)}) custom-call(f32[2,2,1,88,128]{4,3,2,1,0:T(8,128)S(1)} %collective-permute-done.2.refs_0_, f32[2,2,1,88,128]{4,3,2,1,0:T(8,128)S(1)} %collective-permute-done.3.refs_1_, f32[2,2,1,88,128]{4,3,2,1,0:T(8,128)S(1)} %collective-permute-done.4.refs_2_, ...), custom_call_target="tpu_custom_call" | custom-call | flops 16777216 | bytes 1409024 | tf_op jit(solution)/shard_map/decode/pallas_call | solution.py:295
  25.6 1.3 %collective-permute-done.refs_0_.refs_4_ = f32[1,2,512,128]{3,2,1,0:T(8,128)S(1)} collective-permute-done((f32[1,2,512,128]{3,2,1,0:T(8,128)S(1)}, f32[1,2,512,128]{3,2,1,0:T(8,128)S(1)}, u32[]{:S(2)}, u32[]{:S(2)}) %collective-permute-start) | collective-permute-done | bytes 524320 | tf_op jit(solution)/shard_map/ppermute | solution.py:429
  26.9 1.5 %decode.3 = (f32[2,2,1,64,128]{4,3,2,1,0:T(8,128)S(1)}, f32[2,2,1,64,128]{4,3,2,1,0:T(8,128)S(1)}) custom-call(f32[2,2,1,88,128]{4,3,2,1,0:T(8,128)S(1)} %collective-permute-done.2.refs_0_, f32[2,2,1,88,128]{4,3,2,1,0:T(8,128)S(1)} %collective-permute-done.3.refs_1_, f32[2,2,1,88,128]{4,3,2,1,0:T(8,128)S(1)} %collective-permute-done.4.refs_2_, ...), custom_call_target="tpu_custom_call" | custom-call | flops 16777216 | bytes 1409024 | tf_op jit(solution)/shard_map/decode/pallas_call | solution.py:295
  28.4 0.1 collective-permute-start.5
  28.4 1.3 %collective-permute-done.5.back = f32[2,2,1,64,128]{4,3,2,1,0:T(8,128)S(1)} collective-permute-done((f32[2,2,1,64,128]{4,3,2,1,0:T(8,128)S(1)}, f32[2,2,1,64,128]{4,3,2,1,0:T(8,128)S(1)}, u32[]{:S(2)}, u32[]{:S(2)}) %collective-permute-start.5) | collective-permute-done | bytes 131104 | tf_op jit(solution)/shard_map/ppermute | solution.py:462
  29.8 0.5 %collective-permute-start.6 = (f32[2,2,1,64,128]{4,3,2,1,0:T(8,128)S(1)}, f32[2,2,1,64,128]{4,3,2,1,0:T(8,128)S(1)}, u32[]{:S(2)}, u32[]{:S(2)}) collective-permute-start(f32[2,2,1,64,128]{4,3,2,1,0:T(8,128)S(1)} %get-tuple-element.26), channel_id=1, source_target_pairs={{8,0},{12,1},{4,2},{0,3},{9,4},{13,5},{5,6},{1,7},{10,8},{14,9},{6... | collective-permute-start | bytes 393224 | tf_op jit(solution)/shard_map/ppermute | solution.py:463
  30.4 6.2 %collective-permute-start.7 = (f32[2,2,1,64,128]{4,3,2,1,0:T(8,128)S(1)}, f32[2,2,1,64,128]{4,3,2,1,0:T(8,128)S(1)}, u32[]{:S(2)}, u32[]{:S(2)}) collective-permute-start(f32[2,2,1,64,128]{4,3,2,1,0:T(8,128)S(1)} %get-tuple-element.27), channel_id=1, source_target_pairs={{0,0},{4,1},{12,2},{8,3},{1,4},{5,5},{13,6},{9,7},{2,8},{6,9},{14,... | collective-permute-start | bytes 393224 | tf_op jit(solution)/shard_map/ppermute | solution.py:463
  36.6 4.0 %prefill.5 = (f32[2,128,16,128]{3,2,1,0:T(8,128)}, f32[8,128]{1,0:T(8,128)}) custom-call(s32[8]{0:T(128)S(1)} %copy-done.2, f32[2,128,16,128]{3,2,1,0:T(8,128)S(1)} %copy-done, f32[1,2,512,128]{3,2,1,0:T(8,128)S(1)} %collective-permute-done.refs_0_.refs_4_, f32[2,128,1024]{2,1,0:T(8,128)S(1)} %get-tuple-element.16.refs_1_.refs_7_, ...), custom_call_target="tpu_custom_call", output_to_operand_aliasing={{0}: (5, {})} | custom-call | flops 67108864 | bytes 2621440 | tf_op jit(solution)/shard_map/prefill/pallas_call | solution.py:186
  40.5 0.0 collective-permute-done.6
  40.6 1.8 %collective-permute-done.7 = f32[2,2,1,64,128]{4,3,2,1,0:T(8,128)S(1)} collective-permute-done((f32[2,2,1,64,128]{4,3,2,1,0:T(8,128)S(1)}, f32[2,2,1,64,128]{4,3,2,1,0:T(8,128)S(1)}, u32[]{:S(2)}, u32[]{:S(2)}) %collective-permute-start.7) | collective-permute-done | bytes 131104 | tf_op jit(solution)/shard_map/ppermute | solution.py:463
  42.4 0.7 %place.1 = f32[8,1,64,128]{3,2,1,0:T(8,128)} custom-call(f32[4,1,64,128]{3,2,1,0:T(8,128)S(1)} %bitcast.10, f32[4,1,64,128]{3,2,1,0:T(8,128)S(1)} %bitcast.11), custom_call_target="tpu_custom_call" | custom-call | tf_op jit(solution)/shard_map/place/pallas_call | solution.py:405
  (4 shorter events, 0.1 us)
Async XLA Ops:
  0.6 3.5 %copy-start.5 = (s32[8,1]{0,1:T(1,128)S(1)}, s32[8,1]{0,1:T(1,128)}, u32[]{:S(2)}) copy-start(s32[8,1]{0,1:T(1,128)} %param.11) | copy-start | bytes 100
  0.6 1.2 %copy-start.1 = (f32[2,2,256,2,128]{4,3,2,1,0:T(2,128)S(1)}, f32[2,2,256,2,128]{4,3,2,1,0:T(2,128)}, u32[]{:S(2)}) copy-start(f32[2,2,256,2,128]{4,3,2,1,0:T(2,128)} %param.6) | copy-start | bytes 3145732
  1.9 2.4 %copy-start.3 = (f32[8,1,4,16,128]{4,3,2,1,0:T(8,128)S(1)}, f32[8,1,4,16,128]{4,3,2,1,0:T(8,128)}, u32[]{:S(2)}) copy-start(f32[8,1,4,16,128]{4,3,2,1,0:T(8,128)} %param.8) | copy-start | bytes 786436
  1.9 2.4 %copy-start.4 = (f32[8,1,4,2,2,128]{5,4,3,2,1,0:T(2,128)S(1)}, f32[8,1,4,2,2,128]{5,4,3,2,1,0:T(2,128)}, u32[]{:S(2)}) copy-start(f32[8,1,4,2,2,128]{5,4,3,2,1,0:T(2,128)} %param.9) | copy-start | bytes 196612
  1.9 14.9 %collective-permute-start.1 = (f32[1,2,512,128]{3,2,1,0:T(8,128)S(1)}, f32[1,2,512,128]{3,2,1,0:T(8,128)S(1)}, u32[]{:S(2)}, u32[]{:S(2)}) collective-permute-start(f32[1,2,512,128]{3,2,1,0:T(8,128)S(1)} %take.3.refs_0_.refs_3_), channel_id=1, source_target_pairs={{16,0},{0,16},{17,1},{1,17},{18,2},{2,18},{19,3},{3,19},{20,4},{4,... | collective-permute-start | bytes 1572872 | tf_op jit(solution)/shard_map/ppermute | solution.py:429
  2.6 24.3 %collective-permute-start = (f32[1,2,512,128]{3,2,1,0:T(8,128)S(1)}, f32[1,2,512,128]{3,2,1,0:T(8,128)S(1)}, u32[]{:S(2)}, u32[]{:S(2)}) collective-permute-start(f32[1,2,512,128]{3,2,1,0:T(8,128)S(1)} %take.2.refs_1_.refs_0_.refs_3_), channel_id=1, source_target_pairs={{16,0},{0,16},{17,1},{1,17},{18,2},{2,18},{19,3},{3,19},{20,4},{4,... | collective-permute-start | bytes 1572872 | tf_op jit(solution)/shard_map/ppermute | solution.py:429
  4.2 5.2 %copy-start = (f32[2,128,16,128]{3,2,1,0:T(8,128)S(1)}, f32[2,128,16,128]{3,2,1,0:T(8,128)}, u32[]{:S(2)}) copy-start(f32[2,128,16,128]{3,2,1,0:T(8,128)} %q_ref.5) | copy-start | bytes 6291460
  4.2 5.2 %copy-start.2 = (s32[8]{0:T(128)S(1)}, s32[8]{0:T(128)}, u32[]{:S(2)}) copy-start(s32[8]{0:T(128)} %lengths.6) | copy-start | bytes 100
  4.9 16.9 %collective-permute-start.2 = (f32[2,2,1,88,128]{4,3,2,1,0:T(8,128)S(1)}, f32[2,2,1,88,128]{4,3,2,1,0:T(8,128)S(1)}, u32[]{:S(2)}, u32[]{:S(2)}) collective-permute-start(f32[2,2,1,88,128]{4,3,2,1,0:T(8,128)S(1)} %get-tuple-element.15.refs_1_), channel_id=1, source_target_pairs={{0,8},{1,12},{2,4},{3,0},{4,9},{5,13},{6,5},{7,1},{8,10},{9,14},{1... | collective-permute-start | bytes 540680 | tf_op jit(solution)/shard_map/ppermute | solution.py:448
  7.5 14.2 %collective-permute-start.3 = (f32[2,2,1,88,128]{4,3,2,1,0:T(8,128)S(1)}, f32[2,2,1,88,128]{4,3,2,1,0:T(8,128)S(1)}, u32[]{:S(2)}, u32[]{:S(2)}) collective-permute-start(f32[2,2,1,88,128]{4,3,2,1,0:T(8,128)S(1)} %get-tuple-element.20), channel_id=1, source_target_pairs={{0,0},{1,4},{2,12},{3,8},{4,1},{5,5},{6,13},{7,9},{8,2},{9,6},{10,... | collective-permute-start | bytes 540680 | tf_op jit(solution)/shard_map/ppermute | solution.py:448
  21.8 2.3 %collective-permute-start.4 = (f32[2,2,1,88,128]{4,3,2,1,0:T(8,128)S(1)}, f32[2,2,1,88,128]{4,3,2,1,0:T(8,128)S(1)}, u32[]{:S(2)}, u32[]{:S(2)}) collective-permute-start(f32[2,2,1,88,128]{4,3,2,1,0:T(8,128)S(1)} %other_side.1), channel_id=1, source_target_pairs={{0,4},{4,0},{8,12},{12,8},{1,5},{5,1},{9,13},{13,9},{2,6},{6,2},{1... | collective-permute-start | bytes 540680 | tf_op jit(solution)/shard_map/ppermute | solution.py:454
  28.4 1.4 %collective-permute-start.5 = (f32[2,2,1,64,128]{4,3,2,1,0:T(8,128)S(1)}, f32[2,2,1,64,128]{4,3,2,1,0:T(8,128)S(1)}, u32[]{:S(2)}, u32[]{:S(2)}) collective-permute-start(f32[2,2,1,64,128]{4,3,2,1,0:T(8,128)S(1)} %get-tuple-element.25), channel_id=1, source_target_pairs={{0,4},{4,0},{8,12},{12,8},{1,5},{5,1},{9,13},{13,9},{2,6},{6,2},{1... | collective-permute-start | bytes 393224 | tf_op jit(solution)/shard_map/ppermute | solution.py:462
  29.8 10.7 %collective-permute-start.6 = (f32[2,2,1,64,128]{4,3,2,1,0:T(8,128)S(1)}, f32[2,2,1,64,128]{4,3,2,1,0:T(8,128)S(1)}, u32[]{:S(2)}, u32[]{:S(2)}) collective-permute-start(f32[2,2,1,64,128]{4,3,2,1,0:T(8,128)S(1)} %get-tuple-element.26), channel_id=1, source_target_pairs={{8,0},{12,1},{4,2},{0,3},{9,4},{13,5},{5,6},{1,7},{10,8},{14,9},{6... | collective-permute-start | bytes 393224 | tf_op jit(solution)/shard_map/ppermute | solution.py:463
  30.4 12.0 %collective-permute-start.7 = (f32[2,2,1,64,128]{4,3,2,1,0:T(8,128)S(1)}, f32[2,2,1,64,128]{4,3,2,1,0:T(8,128)S(1)}, u32[]{:S(2)}, u32[]{:S(2)}) collective-permute-start(f32[2,2,1,64,128]{4,3,2,1,0:T(8,128)S(1)} %get-tuple-element.27), channel_id=1, source_target_pairs={{0,0},{4,1},{12,2},{8,3},{1,4},{5,5},{13,6},{9,7},{2,8},{6,9},{14,... | collective-permute-start | bytes 393224 | tf_op jit(solution)/shard_map/ppermute | solution.py:463

commit v6 on v4

--- a/solution.py
+++ b/solution.py
@@ -86,6 +86,14 @@
 
 def state_shapes(heads, dim, rows):
     return [jax.ShapeDtypeStruct((heads, dim, rows), F32), jax.ShapeDtypeStruct((heads, 8, rows), F32)]
+
+
+def pair_of(s, t, j, half):
+    return (t // 2 + j + 1 + core_of(t) + s // half + s % 2) % half
+
+
+def core_of(t):
+    return (t + t // 2) % 2
 
 
 def block_starts(count, first, block_len):
@@ -323,7 +331,7 @@
     _, nreq, per, rows, dim = outs[0].shape
     q_rows, kv_rows = q_ref.shape[2], kv_ref.shape[2]
     for j, out in enumerate(outs):
-        pair = lax.rem(lax.axis_index("rep") + (j + 1), half)
+        pair = pair_of(lax.axis_index("head"), lax.axis_index("rep"), j, half)
         for c in range(2):
             for i in range(nreq):
                 request = (pair * 2 + c) * nreq + i
@@ -388,7 +396,7 @@
     o_ref, count = refs[-1], len(refs) - 1
     size = refs[0].shape[0]
     for j in range(count):
-        o_ref[pl.ds(lax.rem(lax.axis_index("rep") + (j + 1), count) * size, size)] = refs[j][...]
+        o_ref[pl.ds(pair_of(lax.axis_index("head"), lax.axis_index("rep"), j, count) * size, size)] = refs[j][...]
 
 
 def place(pieces):
@@ -422,7 +430,7 @@
 
     routes = [
         [
-            (s * rep_count + t, ((t + j + 1) % half * 2 + t // half) * rep_count + s)
+            (s * rep_count + t, (pair_of(s, t, j, half) * 2 + core_of(t)) * rep_count + s)
             for s in range(head_count)
             for t in range(rep_count)
         ]
@@ -445,7 +453,9 @@
         prefill_out, token = prefill_request(i, lengths, prefill_q, held[i], 0, heads, scale, carried=prefill_out, after=(token,))
     far = lax.ppermute(other_side(near, (token,)), "head", swap)
     ready = [decode_request(i, near, far, held[i], 0, heads, group, steps, scale) for i in range(last)]
-    decode_state = decode_request(last, near, far, held[last][:1], 0, heads, group, steps, scale, finish=False)
+    decode_state = decode_request(
+        last, near, far, held[last][:1], 0, heads, group, steps, scale, finish=False, after=ready[-1][:1]
+    )
     kept, sent = decode_request(
         last, near, far, held[last][1:], 1, heads, group, steps, scale, state=decode_state, ready=ready
     )

time: 44.1 us -> 42.4 us (0.961)
  the two profiles are of different devices: /device:TPU:1 before, /device:TPU:7 now
where the time goes in v6:
time: 42.4 us; the launch traced here: 42.2 us
  Pallas kernels  16.6 us (39%)
  starting transfers between devices  16.2 us (38%)
  waiting for transfers between devices  7.33 us (17%)
  local copies, waits for them, and re-layouts  1.32 us (3%)
  between operations  0.77 us (2%)
    pallas_call x3, Pallas kernels, prefill_request(): pl.pallas_call(functools.partial(prefill_kernel, (index, blocks, first_bl...  11.4 us
    ppermute x2, starting transfers between devices, on_device(): lax.ppermute(packets[j], ('head', 'rep'), routes[j])  6.56 us
    ppermute x2, starting transfers between devices, on_device(): lax.ppermute(joined[j], ('head', 'rep'), [(b, a) for a, b in routes[j]])  4.58 us
    pallas_call x3, Pallas kernels, decode_request(): pl.pallas_call(functools.partial(decode_kernel, plan, heads, group, steps...  3.67 us
    ppermute x2, waiting for transfers between devices, on_device(): lax.ppermute(joined[j], ('head', 'rep'), [(b, a) for a, b in routes[j]])  3.09 us
    ppermute x1, starting transfers between devices, on_device(): far = lax.ppermute(other_side(near, (token,)), 'head', swap)  1.94 us
    ppermute x2, starting transfers between devices, on_device(): held[i].append(lax.ppermute(own[i], 'ctx', perm))  1.6 us
    ppermute x1, starting transfers between devices, on_device(): joined = join(kept, lax.ppermute(sent, 'head', swap))  1.48 us
  transfers between devices with their start and end apart: 8, of which 5 were waited for; matrix products, arithmetic and copies ran while one was open for 0% of the time, Pallas kernels for 35%

profile of v6, /device:TPU:7, one launch (start us, length us, event | category | flops | bytes accessed | tf_op | source)
XLA Modules:
  0.0 42.2 jit_solution(896454565756245822)
XLA Ops:
  0.6 0.0 copy-start.5
  0.6 0.0 copy-start.1
  0.7 1.2 %copy-done.1 = f32[2,2,256,2,128]{4,3,2,1,0:T(2,128)S(1)} copy-done((f32[2,2,256,2,128]{4,3,2,1,0:T(2,128)S(1)}, f32[2,2,256,2,128]{4,3,2,1,0:T(2,128)}, u32[]{:S(2)}) %copy-start.1) | copy-done | bytes 1048600
  1.9 0.0 copy-start.3
  1.9 0.0 copy-start.4
  1.9 0.3 collective-permute-start.1
  2.3 1.3 %collective-permute-start = (f32[1,2,512,128]{3,2,1,0:T(8,128)S(1)}, f32[1,2,512,128]{3,2,1,0:T(8,128)S(1)}, u32[]{:S(2)}, u32[]{:S(2)}) collective-permute-start(f32[1,2,512,128]{3,2,1,0:T(8,128)S(1)} %take.2.refs_1_.refs_0_.refs_3_), channel_id=1, source_target_pairs={{16,0},{0,16},{17,1},{1,17},{18,2},{2,18},{19,3},{3,19},{20,4},{4,... | collective-permute-start | bytes 1572872 | tf_op jit(solution)/shard_map/ppermute | solution.py:429
  3.6 0.0 copy-done.5
  3.6 0.1 copy.9.lengths
  3.7 0.0 copy-done.3
  3.7 0.0 copy-done.4
  3.7 0.0 copy-start
  3.7 0.0 copy-start.2
  3.7 0.7 %pack.1 = (f32[2,2,1,88,128]{4,3,2,1,0:T(8,128)S(1)}, f32[2,2,1,88,128]{4,3,2,1,0:T(8,128)S(1)}) custom-call(s32[8,1]{1,0:T(8,128)S(1)} %copy.9.lengths, f32[8,1,64,128]{3,2,1,0:T(8,128)S(1)} %bitcast.12, f32[8,1,16,128]{3,2,1,0:T(8,128)S(1)} %bitcast.13, f32[1,2,512,128]{3,2,1,0:T(8,128)S(1)} %take.3.refs_0_.refs_3_, ...), custom_call_target="tpu_custom_call" | custom-call | flops 99999997952 | bytes 1000000 | tf_op jit(solution)/shard_map/pack/pallas_call | solution.py:348
  4.3 4.5 %collective-permute-start.2 = (f32[2,2,1,88,128]{4,3,2,1,0:T(8,128)S(1)}, f32[2,2,1,88,128]{4,3,2,1,0:T(8,128)S(1)}, u32[]{:S(2)}, u32[]{:S(2)}) collective-permute-start(f32[2,2,1,88,128]{4,3,2,1,0:T(8,128)S(1)} %get-tuple-element.17.refs_1_), channel_id=1, source_target_pairs={{0,8},{1,4},{2,12},{3,0},{4,1},{5,13},{6,5},{7,9},{8,2},{9,14},{10... | collective-permute-start | bytes 540680 | tf_op jit(solution)/shard_map/ppermute | solution.py:448
  8.8 2.1 %collective-permute-start.3 = (f32[2,2,1,88,128]{4,3,2,1,0:T(8,128)S(1)}, f32[2,2,1,88,128]{4,3,2,1,0:T(8,128)S(1)}, u32[]{:S(2)}, u32[]{:S(2)}) collective-permute-start(f32[2,2,1,88,128]{4,3,2,1,0:T(8,128)S(1)} %get-tuple-element.22), channel_id=1, source_target_pairs={{0,0},{1,12},{2,4},{3,8},{4,9},{5,5},{6,13},{7,1},{8,10},{9,6},{10... | collective-permute-start | bytes 540680 | tf_op jit(solution)/shard_map/ppermute | solution.py:448
  10.9 0.0 copy-done
  10.9 0.0 copy-done.2
  10.9 2.5 %prefill.3 = (f32[2,128,1024]{2,1,0:T(8,128)S(1)}, f32[2,8,1024]{2,1,0:T(8,128)S(1)}) custom-call(s32[8]{0:T(128)S(1)} %copy-done.2, f32[2,128,16,128]{3,2,1,0:T(8,128)S(1)} %copy-done, f32[1,2,512,128]{3,2,1,0:T(8,128)S(1)} %take.2.refs_1_.refs_0_.refs_3_, f32[2,2,1,88,128]{4,3,2,1,0:T(8,128)S(1)} %get-tuple-element.17.refs_1_), custom_call_target="tpu_custom_call" | custom-call | flops 67108864 | bytes 2621440 | tf_op jit(solution)/shard_map/prefill/pallas_call | solution.py:186
  13.4 1.3 %collective-permute-done.1.refs_1_.refs_4_ = f32[1,2,512,128]{3,2,1,0:T(8,128)S(1)} collective-permute-done((f32[1,2,512,128]{3,2,1,0:T(8,128)S(1)}, f32[1,2,512,128]{3,2,1,0:T(8,128)S(1)}, u32[]{:S(2)}, u32[]{:S(2)}) %collective-permute-start.1) | collective-permute-done | bytes 524320 | tf_op jit(solution)/shard_map/ppermute | solution.py:429
  14.8 5.0 %prefill.4 = (f32[2,128,16,128]{3,2,1,0:T(8,128)}, f32[8,128]{1,0:T(8,128)S(1)}) custom-call(s32[8]{0:T(128)S(1)} %copy-done.2, f32[2,128,16,128]{3,2,1,0:T(8,128)S(1)} %copy-done, f32[1,2,512,128]{3,2,1,0:T(8,128)S(1)} %take.3.refs_0_.refs_3_, f32[1,2,512,128]{3,2,1,0:T(8,128)S(1)} %collective-permute-done.1.refs_1_.refs_4_, ...), custom_call_target="tpu_custom_call" | custom-call | flops 134217728 | bytes 3145728 | tf_op jit(solution)/shard_map/prefill/pallas_call | solution.py:186
  19.8 0.9 %collective-permute-done.2.refs_0_ = f32[2,2,1,88,128]{4,3,2,1,0:T(8,128)S(1)} collective-permute-done((f32[2,2,1,88,128]{4,3,2,1,0:T(8,128)S(1)}, f32[2,2,1,88,128]{4,3,2,1,0:T(8,128)S(1)}, u32[]{:S(2)}, u32[]{:S(2)}) %collective-permute-start.2) | collective-permute-done | bytes 180256 | tf_op jit(solution)/shard_map/ppermute | solution.py:448
  20.6 0.0 collective-permute-done.3.refs_1_
  20.6 1.9 %collective-permute-start.4 = (f32[2,2,1,88,128]{4,3,2,1,0:T(8,128)S(1)}, f32[2,2,1,88,128]{4,3,2,1,0:T(8,128)S(1)}, u32[]{:S(2)}, u32[]{:S(2)}) collective-permute-start(f32[2,2,1,88,128]{4,3,2,1,0:T(8,128)S(1)} %other_side.1), channel_id=1, source_target_pairs={{0,4},{4,0},{8,12},{12,8},{1,5},{5,1},{9,13},{13,9},{2,6},{6,2},{1... | collective-permute-start | bytes 540680 | tf_op jit(solution)/shard_map/ppermute | solution.py:454
  22.6 1.0 %collective-permute-done.4.refs_2_ = f32[2,2,1,88,128]{4,3,2,1,0:T(8,128)S(1)} collective-permute-done((f32[2,2,1,88,128]{4,3,2,1,0:T(8,128)S(1)}, f32[2,2,1,88,128]{4,3,2,1,0:T(8,128)S(1)}, u32[]{:S(2)}, u32[]{:S(2)}) %collective-permute-start.4) | collective-permute-done | bytes 180256 | tf_op jit(solution)/shard_map/ppermute | solution.py:454
  23.6 1.4 %decode.3 = (f32[2,1,1,64,128]{4,3,2,1,0:T(8,128)S(1)}, f32[2,1,1,64,128]{4,3,2,1,0:T(8,128)S(1)}) custom-call(f32[2,2,1,88,128]{4,3,2,1,0:T(8,128)S(1)} %collective-permute-done.2.refs_0_, f32[2,2,1,88,128]{4,3,2,1,0:T(8,128)S(1)} %collective-permute-done.3.refs_1_, f32[2,2,1,88,128]{4,3,2,1,0:T(8,128)S(1)} %collective-permute-done.4.refs_2_, ...), custom_call_target="tpu_custom_call" | custom-call | flops 16777216 | bytes 1409024 | tf_op jit(solution)/shard_map/decode/pallas_call | solution.py:295
  25.1 1.1 %decode.4 = (f32[2,128,128]{2,1,0:T(8,128)S(1)}, f32[2,8,128]{2,1,0:T(8,128)S(1)}) custom-call(f32[2,2,1,88,128]{4,3,2,1,0:T(8,128)S(1)} %collective-permute-done.2.refs_0_, f32[2,2,1,88,128]{4,3,2,1,0:T(8,128)S(1)} %collective-permute-done.3.refs_1_, f32[2,2,1,88,128]{4,3,2,1,0:T(8,128)S(1)} %collective-permute-done.4.refs_2_, ...), custom_call_target="tpu_custom_call" | custom-call | flops 8388608 | bytes 884736 | tf_op jit(solution)/shard_map/decode/pallas_call | solution.py:295
  26.1 0.0 collective-permute-done.refs_0_.refs_3_
  26.1 1.2 %decode.5 = (f32[2,2,1,64,128]{4,3,2,1,0:T(8,128)S(1)}, f32[2,2,1,64,128]{4,3,2,1,0:T(8,128)S(1)}) custom-call(f32[2,2,1,88,128]{4,3,2,1,0:T(8,128)S(1)} %collective-permute-done.2.refs_0_, f32[2,2,1,88,128]{4,3,2,1,0:T(8,128)S(1)} %collective-permute-done.3.refs_1_, f32[2,2,1,88,128]{4,3,2,1,0:T(8,128)S(1)} %collective-permute-done.4.refs_2_, ...), custom_call_target="tpu_custom_call" | custom-call | flops 8388608 | bytes 884736 | tf_op jit(solution)/shard_map/decode/pallas_call | solution.py:295
  27.3 1.5 %collective-permute-start.5 = (f32[2,2,1,64,128]{4,3,2,1,0:T(8,128)S(1)}, f32[2,2,1,64,128]{4,3,2,1,0:T(8,128)S(1)}, u32[]{:S(2)}, u32[]{:S(2)}) collective-permute-start(f32[2,2,1,64,128]{4,3,2,1,0:T(8,128)S(1)} %get-tuple-element.29), channel_id=1, source_target_pairs={{0,4},{4,0},{8,12},{12,8},{1,5},{5,1},{9,13},{13,9},{2,6},{6,2},{1... | collective-permute-start | bytes 393224 | tf_op jit(solution)/shard_map/ppermute | solution.py:465
  28.8 1.0 %collective-permute-done.5.back = f32[2,2,1,64,128]{4,3,2,1,0:T(8,128)S(1)} collective-permute-done((f32[2,2,1,64,128]{4,3,2,1,0:T(8,128)S(1)}, f32[2,2,1,64,128]{4,3,2,1,0:T(8,128)S(1)}, u32[]{:S(2)}, u32[]{:S(2)}) %collective-permute-start.5) | collective-permute-done | bytes 131104 | tf_op jit(solution)/shard_map/ppermute | solution.py:465
  29.8 2.7 %collective-permute-start.6 = (f32[2,2,1,64,128]{4,3,2,1,0:T(8,128)S(1)}, f32[2,2,1,64,128]{4,3,2,1,0:T(8,128)S(1)}, u32[]{:S(2)}, u32[]{:S(2)}) collective-permute-start(f32[2,2,1,64,128]{4,3,2,1,0:T(8,128)S(1)} %get-tuple-element.30), channel_id=1, source_target_pairs={{8,0},{4,1},{12,2},{0,3},{1,4},{13,5},{5,6},{9,7},{2,8},{14,9},{6,... | collective-permute-start | bytes 393224 | tf_op jit(solution)/shard_map/ppermute | solution.py:466
  32.5 1.9 %collective-permute-start.7 = (f32[2,2,1,64,128]{4,3,2,1,0:T(8,128)S(1)}, f32[2,2,1,64,128]{4,3,2,1,0:T(8,128)S(1)}, u32[]{:S(2)}, u32[]{:S(2)}) collective-permute-start(f32[2,2,1,64,128]{4,3,2,1,0:T(8,128)S(1)} %get-tuple-element.31), channel_id=1, source_target_pairs={{0,0},{12,1},{4,2},{8,3},{9,4},{5,5},{13,6},{1,7},{10,8},{6,9},{14... | collective-permute-start | bytes 393224 | tf_op jit(solution)/shard_map/ppermute | solution.py:466
  34.4 3.9 %prefill.5 = (f32[2,128,16,128]{3,2,1,0:T(8,128)}, f32[8,128]{1,0:T(8,128)}) custom-call(s32[8]{0:T(128)S(1)} %copy-done.2, f32[2,128,16,128]{3,2,1,0:T(8,128)S(1)} %copy-done, f32[1,2,512,128]{3,2,1,0:T(8,128)S(1)} %collective-permute-done.refs_0_.refs_3_, f32[2,128,1024]{2,1,0:T(8,128)S(1)} %get-tuple-element.18.refs_1_, ...), custom_call_target="tpu_custom_call", output_to_operand_aliasing={{0}: (5, {})} | custom-call | flops 67108864 | bytes 2621440 | tf_op jit(solution)/shard_map/prefill/pallas_call | solution.py:186
  38.4 0.0 collective-permute-done.6
  38.4 3.1 %collective-permute-done.7 = f32[2,2,1,64,128]{4,3,2,1,0:T(8,128)S(1)} collective-permute-done((f32[2,2,1,64,128]{4,3,2,1,0:T(8,128)S(1)}, f32[2,2,1,64,128]{4,3,2,1,0:T(8,128)S(1)}, u32[]{:S(2)}, u32[]{:S(2)}) %collective-permute-start.7) | collective-permute-done | bytes 131104 | tf_op jit(solution)/shard_map/ppermute | solution.py:466
  41.5 0.7 %place.1 = f32[8,1,64,128]{3,2,1,0:T(8,128)} custom-call(f32[4,1,64,128]{3,2,1,0:T(8,128)S(1)} %bitcast.10, f32[4,1,64,128]{3,2,1,0:T(8,128)S(1)} %bitcast.11), custom_call_target="tpu_custom_call" | custom-call | tf_op jit(solution)/shard_map/place/pallas_call | solution.py:405
  (4 shorter events, 0.1 us)
Async XLA Ops:
  0.6 3.0 %copy-start.5 = (s32[8,1]{0,1:T(1,128)S(1)}, s32[8,1]{0,1:T(1,128)}, u32[]{:S(2)}) copy-start(s32[8,1]{0,1:T(1,128)} %param.11) | copy-start | bytes 100
  0.6 1.2 %copy-start.1 = (f32[2,2,256,2,128]{4,3,2,1,0:T(2,128)S(1)}, f32[2,2,256,2,128]{4,3,2,1,0:T(2,128)}, u32[]{:S(2)}) copy-start(f32[2,2,256,2,128]{4,3,2,1,0:T(2,128)} %param.6) | copy-start | bytes 3145732
  1.9 1.8 %copy-start.3 = (f32[8,1,4,16,128]{4,3,2,1,0:T(8,128)S(1)}, f32[8,1,4,16,128]{4,3,2,1,0:T(8,128)}, u32[]{:S(2)}) copy-start(f32[8,1,4,16,128]{4,3,2,1,0:T(8,128)} %param.8) | copy-start | bytes 786436
  1.9 1.8 %copy-start.4 = (f32[8,1,4,2,2,128]{5,4,3,2,1,0:T(2,128)S(1)}, f32[8,1,4,2,2,128]{5,4,3,2,1,0:T(2,128)}, u32[]{:S(2)}) copy-start(f32[8,1,4,2,2,128]{5,4,3,2,1,0:T(2,128)} %param.9) | copy-start | bytes 196612
  1.9 12.9 %collective-permute-start.1 = (f32[1,2,512,128]{3,2,1,0:T(8,128)S(1)}, f32[1,2,512,128]{3,2,1,0:T(8,128)S(1)}, u32[]{:S(2)}, u32[]{:S(2)}) collective-permute-start(f32[1,2,512,128]{3,2,1,0:T(8,128)S(1)} %take.3.refs_0_.refs_3_), channel_id=1, source_target_pairs={{16,0},{0,16},{17,1},{1,17},{18,2},{2,18},{19,3},{3,19},{20,4},{4,... | collective-permute-start | bytes 1572872 | tf_op jit(solution)/shard_map/ppermute | solution.py:429
  2.3 23.8 %collective-permute-start = (f32[1,2,512,128]{3,2,1,0:T(8,128)S(1)}, f32[1,2,512,128]{3,2,1,0:T(8,128)S(1)}, u32[]{:S(2)}, u32[]{:S(2)}) collective-permute-start(f32[1,2,512,128]{3,2,1,0:T(8,128)S(1)} %take.2.refs_1_.refs_0_.refs_3_), channel_id=1, source_target_pairs={{16,0},{0,16},{17,1},{1,17},{18,2},{2,18},{19,3},{3,19},{20,4},{4,... | collective-permute-start | bytes 1572872 | tf_op jit(solution)/shard_map/ppermute | solution.py:429
  3.7 7.2 %copy-start = (f32[2,128,16,128]{3,2,1,0:T(8,128)S(1)}, f32[2,128,16,128]{3,2,1,0:T(8,128)}, u32[]{:S(2)}) copy-start(f32[2,128,16,128]{3,2,1,0:T(8,128)} %q_ref.5) | copy-start | bytes 6291460
  3.7 7.2 %copy-start.2 = (s32[8]{0:T(128)S(1)}, s32[8]{0:T(128)}, u32[]{:S(2)}) copy-start(s32[8]{0:T(128)} %lengths.6) | copy-start | bytes 100
  4.3 16.3 %collective-permute-start.2 = (f32[2,2,1,88,128]{4,3,2,1,0:T(8,128)S(1)}, f32[2,2,1,88,128]{4,3,2,1,0:T(8,128)S(1)}, u32[]{:S(2)}, u32[]{:S(2)}) collective-permute-start(f32[2,2,1,88,128]{4,3,2,1,0:T(8,128)S(1)} %get-tuple-element.17.refs_1_), channel_id=1, source_target_pairs={{0,8},{1,4},{2,12},{3,0},{4,1},{5,13},{6,5},{7,9},{8,2},{9,14},{10... | collective-permute-start | bytes 540680 | tf_op jit(solution)/shard_map/ppermute | solution.py:448
  8.8 11.8 %collective-permute-start.3 = (f32[2,2,1,88,128]{4,3,2,1,0:T(8,128)S(1)}, f32[2,2,1,88,128]{4,3,2,1,0:T(8,128)S(1)}, u32[]{:S(2)}, u32[]{:S(2)}) collective-permute-start(f32[2,2,1,88,128]{4,3,2,1,0:T(8,128)S(1)} %get-tuple-element.22), channel_id=1, source_target_pairs={{0,0},{1,12},{2,4},{3,8},{4,9},{5,5},{6,13},{7,1},{8,10},{9,6},{10... | collective-permute-start | bytes 540680 | tf_op jit(solution)/shard_map/ppermute | solution.py:448
  20.6 3.0 %collective-permute-start.4 = (f32[2,2,1,88,128]{4,3,2,1,0:T(8,128)S(1)}, f32[2,2,1,88,128]{4,3,2,1,0:T(8,128)S(1)}, u32[]{:S(2)}, u32[]{:S(2)}) collective-permute-start(f32[2,2,1,88,128]{4,3,2,1,0:T(8,128)S(1)} %other_side.1), channel_id=1, source_target_pairs={{0,4},{4,0},{8,12},{12,8},{1,5},{5,1},{9,13},{13,9},{2,6},{6,2},{1... | collective-permute-start | bytes 540680 | tf_op jit(solution)/shard_map/ppermute | solution.py:454
  27.3 2.5 %collective-permute-start.5 = (f32[2,2,1,64,128]{4,3,2,1,0:T(8,128)S(1)}, f32[2,2,1,64,128]{4,3,2,1,0:T(8,128)S(1)}, u32[]{:S(2)}, u32[]{:S(2)}) collective-permute-start(f32[2,2,1,64,128]{4,3,2,1,0:T(8,128)S(1)} %get-tuple-element.29), channel_id=1, source_target_pairs={{0,4},{4,0},{8,12},{12,8},{1,5},{5,1},{9,13},{13,9},{2,6},{6,2},{1... | collective-permute-start | bytes 393224 | tf_op jit(solution)/shard_map/ppermute | solution.py:465
  29.8 8.5 %collective-permute-start.6 = (f32[2,2,1,64,128]{4,3,2,1,0:T(8,128)S(1)}, f32[2,2,1,64,128]{4,3,2,1,0:T(8,128)S(1)}, u32[]{:S(2)}, u32[]{:S(2)}) collective-permute-start(f32[2,2,1,64,128]{4,3,2,1,0:T(8,128)S(1)} %get-tuple-element.30), channel_id=1, source_target_pairs={{8,0},{4,1},{12,2},{0,3},{1,4},{13,5},{5,6},{9,7},{2,8},{14,9},{6,... | collective-permute-start | bytes 393224 | tf_op jit(solution)/shard_map/ppermute | solution.py:466
  32.5 9.0 %collective-permute-start.7 = (f32[2,2,1,64,128]{4,3,2,1,0:T(8,128)S(1)}, f32[2,2,1,64,128]{4,3,2,1,0:T(8,128)S(1)}, u32[]{:S(2)}, u32[]{:S(2)}) collective-permute-start(f32[2,2,1,64,128]{4,3,2,1,0:T(8,128)S(1)} %get-tuple-element.31), channel_id=1, source_target_pairs={{0,0},{12,1},{4,2},{8,3},{9,4},{5,5},{13,6},{1,7},{10,8},{6,9},{14... | collective-permute-start | bytes 393224 | tf_op jit(solution)/shard_map/ppermute | solution.py:466

commit v7 on v6

--- a/solution.py
+++ b/solution.py
@@ -201,7 +201,7 @@
 
 
 def decode_kernel(plan, heads, group, steps, scale, *refs):
-    index, near, blocks, first_block, started, finish, ready, unread = plan
+    index, nreq, per, near, blocks, first_block, started, finish, ready, unread = plan
     near_refs, far_ref, refs = refs[:near], refs[near], refs[near + 1 :]
     kv_refs, refs = refs[:blocks], refs[blocks:]
     state_in = refs[:2] if started else None
@@ -209,17 +209,18 @@
     ready_refs, outs = refs[:ready], refs[ready + unread :]
     side = lax.rem(lax.axis_index("head"), 2)
     at_pos = block_starts(blocks, first_block, kv_refs[0].shape[2] // heads)
-    _, nreq, per, _, dim = far_ref.shape
+    dim = far_ref.shape[2]
     q_rows = steps * heads * group
     rows = steps * group
     slots = [(ref, side, n) for ref in near_refs for n in range(per)]
     slots += [(far_ref, j, n) for j in range(near) for n in range(per)]
     every = pl.ds(0, len(slots) * rows)
-    at_limit = q_rows + 2 * heads * steps
+    each = q_rows + 2 * heads * steps
+    at_limit = nreq * per * each + index * per
     lane = lax.broadcasted_iota(jnp.int32, (1, len(slots) * rows), 1)
     limit = jnp.zeros(lane.shape, F32)
     for i, (ref, lead, n) in enumerate(slots):
-        wide = jnp.broadcast_to(ref[lead, index, n, at_limit : at_limit + 1, 0:1], lane.shape)
+        wide = jnp.broadcast_to(ref[lead, at_limit + n : at_limit + n + 1, 0:1], lane.shape)
         limit = jnp.where(lane // rows == i, wide, limit)
     limit = limit.astype(jnp.int32)
     if finish:
@@ -230,7 +231,7 @@
         own = slice(head * group, (head + 1) * group)
         q = jnp.concatenate(
             [
-                ref[lead, index, n, 0:q_rows].reshape(steps, heads * group, dim)[:, own].reshape(rows, dim)
+                ref[lead, (index * per + n) * each : (index * per + n) * each + q_rows].reshape(steps, heads * group, dim)[:, own].reshape(rows, dim)
                 for ref, lead, n in slots
             ],
             axis=0,
@@ -247,7 +248,7 @@
                 drafts = [
                     jnp.concatenate(
                         [
-                            ref[lead, index, n, pl.ds(q_rows + which * heads + head, steps, stride=2 * heads), :]
+                            ref[lead, pl.ds((index * per + n) * each + q_rows + which * heads + head, steps, stride=2 * heads), :]
                             for ref, lead, n in slots
                         ],
                         axis=0,
@@ -276,9 +277,10 @@
 
 
 def decode_request(
-    index, near, far, kv_list, first_block, heads, group, steps, scale, state=None, finish=True, ready=(), after=()
+    index, sizes, near, far, kv_list, first_block, heads, group, steps, scale, state=None, finish=True, ready=(), after=()
 ):
-    count, _, per, packet_rows, dim = far.shape
+    nreq, per = sizes
+    count, packet_rows, dim = far.shape
     blocks = len(kv_list)
     q_rows = steps * heads * group
     all_rows = 2 * count * per * steps * group
@@ -290,7 +292,7 @@
     else:
         out_shape = state_shapes(heads, dim, all_rows)
     keys = sum(kv.shape[2] for kv in kv_list) // heads
-    plan = (index, count, blocks, first_block, started, finish, len(ready_flat), len(after))
+    plan = (index, nreq, per, count, blocks, first_block, started, finish, len(ready_flat), len(after))
     operands = count + 1 + blocks + len(state) + len(ready_flat)
     return pl.pallas_call(
         functools.partial(decode_kernel, plan, heads, group, steps, scale),
@@ -300,7 +302,7 @@
         compiler_params=pltpu.CompilerParams(vmem_limit_bytes=12 * 2**20),
         cost_estimate=pl.CostEstimate(
             flops=all_rows * heads * keys * dim,
-            bytes_accessed=4 * (4 * count * per * packet_rows * dim + 2 * heads * keys * dim),
+            bytes_accessed=4 * (4 * count * packet_rows * dim + 2 * heads * keys * dim),
             transcendentals=all_rows * heads * keys,
         ),
         name="decode",
@@ -325,28 +327,33 @@
     )(array)
 
 
-def pack_kernel(unread, lengths, q_ref, kv_ref, *refs):
+def pack_kernel(nreq, unread, lengths, q_ref, kv_ref, *refs):
     outs = refs[unread:]
     half = len(outs)
-    _, nreq, per, rows, dim = outs[0].shape
-    q_rows, kv_rows = q_ref.shape[2], kv_ref.shape[2]
+    per, q_rows, dim = q_ref.shape[1:]
+    kv_rows = kv_ref.shape[2]
+    rows = q_rows + kv_rows
     for j, out in enumerate(outs):
         pair = pair_of(lax.axis_index("head"), lax.axis_index("rep"), j, half)
         for c in range(2):
+            tail = nreq * per * rows
+            out[c, tail:] = jnp.zeros((out.shape[1] - tail, dim), F32)
             for i in range(nreq):
                 request = (pair * 2 + c) * nreq + i
                 for n in range(per):
-                    out[c, i, n, 0:q_rows] = q_ref[request, n]
-                    out[c, i, n, q_rows : q_rows + kv_rows] = kv_ref[request, n]
-                    reads = jnp.full((rows - q_rows - kv_rows, dim), lengths[request, n], jnp.int32)
-                    out[c, i, n, q_rows + kv_rows :] = reads.astype(F32)
+                    at = i * per + n
+                    out[c, at * rows : at * rows + q_rows] = q_ref[request, n]
+                    out[c, at * rows + q_rows : (at + 1) * rows] = kv_ref[request, n]
+                    reads = jnp.full((1, dim), lengths[request, n], jnp.int32)
+                    out[c, tail + at : tail + at + 1] = reads.astype(F32)
 
 
 def pack(lengths, q, kv, half, nreq, after):
     requests, per, q_rows, dim = q.shape
-    shape = jax.ShapeDtypeStruct((2, nreq, per, q_rows + kv.shape[2] + 8, dim), F32)
-    return pl.pallas_call(
-        functools.partial(pack_kernel, len(after)),
+    each = nreq * per
+    shape = jax.ShapeDtypeStruct((2, each * (q_rows + kv.shape[2]) + -(-each // 8) * 8, dim), F32)
+    return pl.pallas_call(
+        functools.partial(pack_kernel, nreq, len(after)),
         in_specs=[SMEM_SPEC, VMEM_SPEC, VMEM_SPEC] + [ANY_SPEC] * len(after),
         out_specs=[VMEM_SPEC] * half,
         out_shape=[shape] * half,
@@ -449,15 +456,21 @@
     last = nreq - 1
     prefill_state = prefill_request(last, lengths, prefill_q, held[last][:1], 0, heads, scale, finish=False, after=packets[:1])
     prefill_out, token = None, prefill_state[1]
+    early = []
     for i in range(last):
-        prefill_out, token = prefill_request(i, lengths, prefill_q, held[i], 0, heads, scale, carried=prefill_out, after=(token,))
+        early.append(prefill_request(i, lengths, prefill_q, held[i][:1], 0, heads, scale, finish=False, after=(token,)))
+        token = early[i][1]
+    for i in range(last):
+        prefill_out, token = prefill_request(
+            i, lengths, prefill_q, held[i][1:], 1, heads, scale, state=early[i], carried=prefill_out, after=(token,)
+        )
     far = lax.ppermute(other_side(near, (token,)), "head", swap)
-    ready = [decode_request(i, near, far, held[i], 0, heads, group, steps, scale) for i in range(last)]
+    ready = [decode_request(i, (nreq, per), near, far, held[i], 0, heads, group, steps, scale) for i in range(last)]
     decode_state = decode_request(
-        last, near, far, held[last][:1], 0, heads, group, steps, scale, finish=False, after=ready[-1][:1]
+        last, (nreq, per), near, far, held[last][:1], 0, heads, group, steps, scale, finish=False, after=ready[-1][:1]
     )
     kept, sent = decode_request(
-        last, near, far, held[last][1:], 1, heads, group, steps, scale, state=decode_state, ready=ready
+        last, (nreq, per), near, far, held[last][1:], 1, heads, group, steps, scale, state=decode_state, ready=ready
     )
     prefill_out, _ = prefill_request(
         last, lengths, prefill_q, held[last][1:], 1, heads, scale, state=prefill_state, carried=prefill_out

time: 42.4 us -> 42.3 us (level)
  Pallas kernels: 16.6 us -> 17.6 us
  starting transfers between devices: 16.2 us -> 15.3 us
    pallas_call x3 -> x4, Pallas kernels: 11.4 us -> 12.4 us  [prefill_request(): pl.pallas_call(functools.partial(prefill_kernel, (index, blocks, first_bl...]
    ppermute x1, starting transfers between devices: 1.94 us -> 1.08 us  [on_device(): far = lax.ppermute(other_side(near, (token,)), 'head', swap)]
  transfers between devices with their start and end apart: 8 -> 8, of which waited for: 5 -> 5; matrix products, arithmetic and copies ran while one was open for 0% -> 0% of each run, Pallas kernels for 35% -> 37%
where the time goes in v7:
time: 42.3 us; the launch traced here: 42.2 us
  Pallas kernels  17.6 us (42%)
  starting transfers between devices  15.3 us (36%)
  waiting for transfers between devices  7.17 us (17%)
  local copies, waits for them, and re-layouts  1.32 us (3%)
  between operations  0.77 us (2%)
    pallas_call x4, Pallas kernels, prefill_request(): pl.pallas_call(functools.partial(prefill_kernel, (index, blocks, first_bl...  12.4 us
    ppermute x2, starting transfers between devices, on_device(): lax.ppermute(packets[j], ('head', 'rep'), routes[j])  6.56 us
    ppermute x2, starting transfers between devices, on_device(): lax.ppermute(joined[j], ('head', 'rep'), [(b, a) for a, b in routes[j]])  4.47 us
    pallas_call x3, Pallas kernels, decode_request(): pl.pallas_call(functools.partial(decode_kernel, plan, heads, group, steps...  3.67 us
    ppermute x2, waiting for transfers between devices, on_device(): lax.ppermute(joined[j], ('head', 'rep'), [(b, a) for a, b in routes[j]])  3.16 us
    ppermute x1, starting transfers between devices, on_device(): joined = join(kept, lax.ppermute(sent, 'head', swap))  1.61 us
    ppermute x2, starting transfers between devices, on_device(): held[i].append(lax.ppermute(own[i], 'ctx', perm))  1.6 us
    ppermute x2, waiting for transfers between devices, on_device(): held[i].append(lax.ppermute(own[i], 'ctx', perm))  1.46 us
  transfers between devices with their start and end apart: 8, of which 5 were waited for; matrix products, arithmetic and copies ran while one was open for 0% of the time, Pallas kernels for 37%

profile of v7, /device:TPU:7, one launch (start us, length us, event | category | flops | bytes accessed | tf_op | source)
XLA Modules:
  0.0 42.2 jit_solution(17705177435138355610)
XLA Ops:
  0.6 0.0 copy-start.5
  0.6 0.0 copy-start.1
  0.7 1.2 %copy-done.1 = f32[2,2,256,2,128]{4,3,2,1,0:T(2,128)S(1)} copy-done((f32[2,2,256,2,128]{4,3,2,1,0:T(2,128)S(1)}, f32[2,2,256,2,128]{4,3,2,1,0:T(2,128)}, u32[]{:S(2)}) %copy-start.1) | copy-done | bytes 1048600
  1.9 0.0 copy-start.3
  1.9 0.0 copy-start.4
  1.9 0.3 collective-permute-start.1
  2.3 1.3 %collective-permute-start = (f32[1,2,512,128]{3,2,1,0:T(8,128)S(1)}, f32[1,2,512,128]{3,2,1,0:T(8,128)S(1)}, u32[]{:S(2)}, u32[]{:S(2)}) collective-permute-start(f32[1,2,512,128]{3,2,1,0:T(8,128)S(1)} %take.2.refs_1_.refs_0_.refs_3_), channel_id=1, source_target_pairs={{16,0},{0,16},{17,1},{1,17},{18,2},{2,18},{19,3},{3,19},{20,4},{4,... | collective-permute-start | bytes 1572872 | tf_op jit(solution)/shard_map/ppermute | solution.py:436
  3.6 0.0 copy-done.5
  3.6 0.1 copy.9.lengths
  3.7 0.0 copy-done.3
  3.7 0.0 copy-done.4
  3.7 0.0 copy-start
  3.7 0.0 copy-start.2
  3.7 0.7 %pack.1 = (f32[2,168,128]{2,1,0:T(8,128)S(1)}, f32[2,168,128]{2,1,0:T(8,128)S(1)}) custom-call(s32[8,1]{1,0:T(8,128)S(1)} %copy.9.lengths, f32[8,1,64,128]{3,2,1,0:T(8,128)S(1)} %bitcast.12, f32[8,1,16,128]{3,2,1,0:T(8,128)S(1)} %bitcast.13, f32[1,2,512,128]{3,2,1,0:T(8,128)S(1)} %take.3.refs_0_.refs_3_, f32[1,2,512,128]{3,2,1,0:T(8,128)S(1)} %take.2.refs_1_.refs_0_.refs_3_), custom_call_target="tpu_custom_call" | custom-call | flops 99999997952 | bytes 1000000 | tf_op jit(solution)/shard_map/pack/pallas_call | solution.py:355
  4.3 4.5 %collective-permute-start.2 = (f32[2,168,128]{2,1,0:T(8,128)S(1)}, f32[2,168,128]{2,1,0:T(8,128)S(1)}, u32[]{:S(2)}, u32[]{:S(2)}) collective-permute-start(f32[2,168,128]{2,1,0:T(8,128)S(1)} %get-tuple-element.19.refs_1_), channel_id=1, source_target_pairs={{0,8},{1,4},{2,12},{3,0},{4,1},{5,13},{6,5},{7,9},{8,2},{9,14},{10... | collective-permute-start | bytes 516104 | tf_op jit(solution)/shard_map/ppermute | solution.py:455
  8.8 2.1 %collective-permute-start.3 = (f32[2,168,128]{2,1,0:T(8,128)S(1)}, f32[2,168,128]{2,1,0:T(8,128)S(1)}, u32[]{:S(2)}, u32[]{:S(2)}) collective-permute-start(f32[2,168,128]{2,1,0:T(8,128)S(1)} %get-tuple-element.26), channel_id=1, source_target_pairs={{0,0},{1,12},{2,4},{3,8},{4,9},{5,5},{6,13},{7,1},{8,10},{9,6},{10... | collective-permute-start | bytes 516104 | tf_op jit(solution)/shard_map/ppermute | solution.py:455
  10.9 0.0 copy-done
  10.9 0.0 copy-done.2
  10.9 2.5 %prefill.4 = (f32[2,128,1024]{2,1,0:T(8,128)S(1)}, f32[2,8,1024]{2,1,0:T(8,128)S(1)}) custom-call(s32[8]{0:T(128)S(1)} %copy-done.2, f32[2,128,16,128]{3,2,1,0:T(8,128)S(1)} %copy-done, f32[1,2,512,128]{3,2,1,0:T(8,128)S(1)} %take.2.refs_1_.refs_0_.refs_3_, f32[2,168,128]{2,1,0:T(8,128)S(1)} %get-tuple-element.19.refs_1_), custom_call_target="tpu_custom_call" | custom-call | flops 67108864 | bytes 2621440 | tf_op jit(solution)/shard_map/prefill/pallas_call | solution.py:186
  13.4 2.5 %prefill.5 = (f32[2,128,1024]{2,1,0:T(8,128)S(1)}, f32[2,8,1024]{2,1,0:T(8,128)S(1)}) custom-call(s32[8]{0:T(128)S(1)} %copy-done.2, f32[2,128,16,128]{3,2,1,0:T(8,128)S(1)} %copy-done, f32[1,2,512,128]{3,2,1,0:T(8,128)S(1)} %take.3.refs_0_.refs_3_, f32[2,8,1024]{2,1,0:T(8,128)S(1)} %get-tuple-element.21.refs_1_.refs_2_), custom_call_target="tpu_custom_call" | custom-call | flops 67108864 | bytes 2621440 | tf_op jit(solution)/shard_map/prefill/pallas_call | solution.py:186
  16.0 0.0 collective-permute-done.1.refs_0_.refs_4_
  16.0 3.4 %prefill.6 = (f32[2,128,16,128]{3,2,1,0:T(8,128)}, f32[8,128]{1,0:T(8,128)S(1)}) custom-call(s32[8]{0:T(128)S(1)} %copy-done.2, f32[2,128,16,128]{3,2,1,0:T(8,128)S(1)} %copy-done, f32[1,2,512,128]{3,2,1,0:T(8,128)S(1)} %collective-permute-done.1.refs_0_.refs_4_, f32[2,128,1024]{2,1,0:T(8,128)S(1)} %get-tuple-element.22.refs_1_, ...), custom_call_target="tpu_custom_call" | custom-call | flops 67108864 | bytes 2621440 | tf_op jit(solution)/shard_map/prefill/pallas_call | solution.py:186
  19.4 0.5 %collective-permute-done.2.refs_0_ = f32[2,168,128]{2,1,0:T(8,128)S(1)} collective-permute-done((f32[2,168,128]{2,1,0:T(8,128)S(1)}, f32[2,168,128]{2,1,0:T(8,128)S(1)}, u32[]{:S(2)}, u32[]{:S(2)}) %collective-permute-start.2) | collective-permute-done | bytes 172064 | tf_op jit(solution)/shard_map/ppermute | solution.py:455
  19.9 0.0 collective-permute-done.3.refs_1_
  19.9 1.1 %collective-permute-start.4 = (f32[2,168,128]{2,1,0:T(8,128)S(1)}, f32[2,168,128]{2,1,0:T(8,128)S(1)}, u32[]{:S(2)}, u32[]{:S(2)}) collective-permute-start(f32[2,168,128]{2,1,0:T(8,128)S(1)} %other_side.1), channel_id=1, source_target_pairs={{0,4},{4,0},{8,12},{12,8},{1,5},{5,1},{9,13},{13,9},{2,6},{6,2},{1... | collective-permute-start | bytes 516104 | tf_op jit(solution)/shard_map/ppermute | solution.py:467
  21.0 1.0 %collective-permute-done.4.refs_2_ = f32[2,168,128]{2,1,0:T(8,128)S(1)} collective-permute-done((f32[2,168,128]{2,1,0:T(8,128)S(1)}, f32[2,168,128]{2,1,0:T(8,128)S(1)}, u32[]{:S(2)}, u32[]{:S(2)}) %collective-permute-start.4) | collective-permute-done | bytes 172064 | tf_op jit(solution)/shard_map/ppermute | solution.py:467
  22.0 1.5 %decode.3 = (f32[2,1,1,64,128]{4,3,2,1,0:T(8,128)S(1)}, f32[2,1,1,64,128]{4,3,2,1,0:T(8,128)S(1)}) custom-call(f32[2,168,128]{2,1,0:T(8,128)S(1)} %collective-permute-done.2.refs_0_, f32[2,168,128]{2,1,0:T(8,128)S(1)} %collective-permute-done.3.refs_1_, f32[2,168,128]{2,1,0:T(8,128)S(1)} %collective-permute-done.4.refs_2_, ...), custom_call_target="tpu_custom_call" | custom-call | flops 16777216 | bytes 1736704 | tf_op jit(solution)/shard_map/decode/pallas_call | solution.py:297
  23.5 1.1 %decode.4 = (f32[2,128,128]{2,1,0:T(8,128)S(1)}, f32[2,8,128]{2,1,0:T(8,128)S(1)}) custom-call(f32[2,168,128]{2,1,0:T(8,128)S(1)} %collective-permute-done.2.refs_0_, f32[2,168,128]{2,1,0:T(8,128)S(1)} %collective-permute-done.3.refs_1_, f32[2,168,128]{2,1,0:T(8,128)S(1)} %collective-permute-done.4.refs_2_, ...), custom_call_target="tpu_custom_call" | custom-call | flops 8388608 | bytes 1212416 | tf_op jit(solution)/shard_map/decode/pallas_call | solution.py:297
  24.6 1.5 %collective-permute-done.refs_0_.refs_3_ = f32[1,2,512,128]{3,2,1,0:T(8,128)S(1)} collective-permute-done((f32[1,2,512,128]{3,2,1,0:T(8,128)S(1)}, f32[1,2,512,128]{3,2,1,0:T(8,128)S(1)}, u32[]{:S(2)}, u32[]{:S(2)}) %collective-permute-start) | collective-permute-done | bytes 524320 | tf_op jit(solution)/shard_map/ppermute | solution.py:436
  26.0 1.2 %decode.5 = (f32[2,2,1,64,128]{4,3,2,1,0:T(8,128)S(1)}, f32[2,2,1,64,128]{4,3,2,1,0:T(8,128)S(1)}) custom-call(f32[2,168,128]{2,1,0:T(8,128)S(1)} %collective-permute-done.2.refs_0_, f32[2,168,128]{2,1,0:T(8,128)S(1)} %collective-permute-done.3.refs_1_, f32[2,168,128]{2,1,0:T(8,128)S(1)} %collective-permute-done.4.refs_2_, ...), custom_call_target="tpu_custom_call" | custom-call | flops 8388608 | bytes 1212416 | tf_op jit(solution)/shard_map/decode/pallas_call | solution.py:297
  27.2 1.6 %collective-permute-start.5 = (f32[2,2,1,64,128]{4,3,2,1,0:T(8,128)S(1)}, f32[2,2,1,64,128]{4,3,2,1,0:T(8,128)S(1)}, u32[]{:S(2)}, u32[]{:S(2)}) collective-permute-start(f32[2,2,1,64,128]{4,3,2,1,0:T(8,128)S(1)} %get-tuple-element.33), channel_id=1, source_target_pairs={{0,4},{4,0},{8,12},{12,8},{1,5},{5,1},{9,13},{13,9},{2,6},{6,2},{1... | collective-permute-start | bytes 393224 | tf_op jit(solution)/shard_map/ppermute | solution.py:478
  28.8 1.0 %collective-permute-done.5.back = f32[2,2,1,64,128]{4,3,2,1,0:T(8,128)S(1)} collective-permute-done((f32[2,2,1,64,128]{4,3,2,1,0:T(8,128)S(1)}, f32[2,2,1,64,128]{4,3,2,1,0:T(8,128)S(1)}, u32[]{:S(2)}, u32[]{:S(2)}) %collective-permute-start.5) | collective-permute-done | bytes 131104 | tf_op jit(solution)/shard_map/ppermute | solution.py:478
  29.8 2.6 %collective-permute-start.6 = (f32[2,2,1,64,128]{4,3,2,1,0:T(8,128)S(1)}, f32[2,2,1,64,128]{4,3,2,1,0:T(8,128)S(1)}, u32[]{:S(2)}, u32[]{:S(2)}) collective-permute-start(f32[2,2,1,64,128]{4,3,2,1,0:T(8,128)S(1)} %get-tuple-element.34), channel_id=1, source_target_pairs={{8,0},{4,1},{12,2},{0,3},{1,4},{13,5},{5,6},{9,7},{2,8},{14,9},{6,... | collective-permute-start | bytes 393224 | tf_op jit(solution)/shard_map/ppermute | solution.py:479
  32.4 1.9 %collective-permute-start.7 = (f32[2,2,1,64,128]{4,3,2,1,0:T(8,128)S(1)}, f32[2,2,1,64,128]{4,3,2,1,0:T(8,128)S(1)}, u32[]{:S(2)}, u32[]{:S(2)}) collective-permute-start(f32[2,2,1,64,128]{4,3,2,1,0:T(8,128)S(1)} %get-tuple-element.35), channel_id=1, source_target_pairs={{0,0},{12,1},{4,2},{8,3},{9,4},{5,5},{13,6},{1,7},{10,8},{6,9},{14... | collective-permute-start | bytes 393224 | tf_op jit(solution)/shard_map/ppermute | solution.py:479
  34.3 4.0 %prefill.7 = (f32[2,128,16,128]{3,2,1,0:T(8,128)}, f32[8,128]{1,0:T(8,128)}) custom-call(s32[8]{0:T(128)S(1)} %copy-done.2, f32[2,128,16,128]{3,2,1,0:T(8,128)S(1)} %copy-done, f32[1,2,512,128]{3,2,1,0:T(8,128)S(1)} %collective-permute-done.refs_0_.refs_3_, f32[2,128,1024]{2,1,0:T(8,128)S(1)} %get-tuple-element.20.refs_1_, ...), custom_call_target="tpu_custom_call", output_to_operand_aliasing={{0}: (5, {})} | custom-call | flops 67108864 | bytes 2621440 | tf_op jit(solution)/shard_map/prefill/pallas_call | solution.py:186
  38.3 0.0 collective-permute-done.6
  38.3 3.2 %collective-permute-done.7 = f32[2,2,1,64,128]{4,3,2,1,0:T(8,128)S(1)} collective-permute-done((f32[2,2,1,64,128]{4,3,2,1,0:T(8,128)S(1)}, f32[2,2,1,64,128]{4,3,2,1,0:T(8,128)S(1)}, u32[]{:S(2)}, u32[]{:S(2)}) %collective-permute-start.7) | collective-permute-done | bytes 131104 | tf_op jit(solution)/shard_map/ppermute | solution.py:479
  41.4 0.7 %place.1 = f32[8,1,64,128]{3,2,1,0:T(8,128)} custom-call(f32[4,1,64,128]{3,2,1,0:T(8,128)S(1)} %bitcast.10, f32[4,1,64,128]{3,2,1,0:T(8,128)S(1)} %bitcast.11), custom_call_target="tpu_custom_call" | custom-call | tf_op jit(solution)/shard_map/place/pallas_call | solution.py:412
  (4 shorter events, 0.1 us)
Async XLA Ops:
  0.6 3.0 %copy-start.5 = (s32[8,1]{0,1:T(1,128)S(1)}, s32[8,1]{0,1:T(1,128)}, u32[]{:S(2)}) copy-start(s32[8,1]{0,1:T(1,128)} %param.11) | copy-start | bytes 100
  0.6 1.2 %copy-start.1 = (f32[2,2,256,2,128]{4,3,2,1,0:T(2,128)S(1)}, f32[2,2,256,2,128]{4,3,2,1,0:T(2,128)}, u32[]{:S(2)}) copy-start(f32[2,2,256,2,128]{4,3,2,1,0:T(2,128)} %param.6) | copy-start | bytes 3145732
  1.9 1.8 %copy-start.3 = (f32[8,1,4,16,128]{4,3,2,1,0:T(8,128)S(1)}, f32[8,1,4,16,128]{4,3,2,1,0:T(8,128)}, u32[]{:S(2)}) copy-start(f32[8,1,4,16,128]{4,3,2,1,0:T(8,128)} %param.8) | copy-start | bytes 786436
  1.9 1.8 %copy-start.4 = (f32[8,1,4,2,2,128]{5,4,3,2,1,0:T(2,128)S(1)}, f32[8,1,4,2,2,128]{5,4,3,2,1,0:T(2,128)}, u32[]{:S(2)}) copy-start(f32[8,1,4,2,2,128]{5,4,3,2,1,0:T(2,128)} %param.9) | copy-start | bytes 196612
  1.9 14.0 %collective-permute-start.1 = (f32[1,2,512,128]{3,2,1,0:T(8,128)S(1)}, f32[1,2,512,128]{3,2,1,0:T(8,128)S(1)}, u32[]{:S(2)}, u32[]{:S(2)}) collective-permute-start(f32[1,2,512,128]{3,2,1,0:T(8,128)S(1)} %take.3.refs_0_.refs_3_), channel_id=1, source_target_pairs={{16,0},{0,16},{17,1},{1,17},{18,2},{2,18},{19,3},{3,19},{20,4},{4,... | collective-permute-start | bytes 1572872 | tf_op jit(solution)/shard_map/ppermute | solution.py:436
  2.3 23.7 %collective-permute-start = (f32[1,2,512,128]{3,2,1,0:T(8,128)S(1)}, f32[1,2,512,128]{3,2,1,0:T(8,128)S(1)}, u32[]{:S(2)}, u32[]{:S(2)}) collective-permute-start(f32[1,2,512,128]{3,2,1,0:T(8,128)S(1)} %take.2.refs_1_.refs_0_.refs_3_), channel_id=1, source_target_pairs={{16,0},{0,16},{17,1},{1,17},{18,2},{2,18},{19,3},{3,19},{20,4},{4,... | collective-permute-start | bytes 1572872 | tf_op jit(solution)/shard_map/ppermute | solution.py:436
  3.7 7.2 %copy-start = (f32[2,128,16,128]{3,2,1,0:T(8,128)S(1)}, f32[2,128,16,128]{3,2,1,0:T(8,128)}, u32[]{:S(2)}) copy-start(f32[2,128,16,128]{3,2,1,0:T(8,128)} %q_ref.7) | copy-start | bytes 6291460
  3.7 7.2 %copy-start.2 = (s32[8]{0:T(128)S(1)}, s32[8]{0:T(128)}, u32[]{:S(2)}) copy-start(s32[8]{0:T(128)} %lengths.8) | copy-start | bytes 100
  4.3 15.6 %collective-permute-start.2 = (f32[2,168,128]{2,1,0:T(8,128)S(1)}, f32[2,168,128]{2,1,0:T(8,128)S(1)}, u32[]{:S(2)}, u32[]{:S(2)}) collective-permute-start(f32[2,168,128]{2,1,0:T(8,128)S(1)} %get-tuple-element.19.refs_1_), channel_id=1, source_target_pairs={{0,8},{1,4},{2,12},{3,0},{4,1},{5,13},{6,5},{7,9},{8,2},{9,14},{10... | collective-permute-start | bytes 516104 | tf_op jit(solution)/shard_map/ppermute | solution.py:455
  8.8 11.1 %collective-permute-start.3 = (f32[2,168,128]{2,1,0:T(8,128)S(1)}, f32[2,168,128]{2,1,0:T(8,128)S(1)}, u32[]{:S(2)}, u32[]{:S(2)}) collective-permute-start(f32[2,168,128]{2,1,0:T(8,128)S(1)} %get-tuple-element.26), channel_id=1, source_target_pairs={{0,0},{1,12},{2,4},{3,8},{4,9},{5,5},{6,13},{7,1},{8,10},{9,6},{10... | collective-permute-start | bytes 516104 | tf_op jit(solution)/shard_map/ppermute | solution.py:455
  19.9 2.1 %collective-permute-start.4 = (f32[2,168,128]{2,1,0:T(8,128)S(1)}, f32[2,168,128]{2,1,0:T(8,128)S(1)}, u32[]{:S(2)}, u32[]{:S(2)}) collective-permute-start(f32[2,168,128]{2,1,0:T(8,128)S(1)} %other_side.1), channel_id=1, source_target_pairs={{0,4},{4,0},{8,12},{12,8},{1,5},{5,1},{9,13},{13,9},{2,6},{6,2},{1... | collective-permute-start | bytes 516104 | tf_op jit(solution)/shard_map/ppermute | solution.py:467
  27.2 2.6 %collective-permute-start.5 = (f32[2,2,1,64,128]{4,3,2,1,0:T(8,128)S(1)}, f32[2,2,1,64,128]{4,3,2,1,0:T(8,128)S(1)}, u32[]{:S(2)}, u32[]{:S(2)}) collective-permute-start(f32[2,2,1,64,128]{4,3,2,1,0:T(8,128)S(1)} %get-tuple-element.33), channel_id=1, source_target_pairs={{0,4},{4,0},{8,12},{12,8},{1,5},{5,1},{9,13},{13,9},{2,6},{6,2},{1... | collective-permute-start | bytes 393224 | tf_op jit(solution)/shard_map/ppermute | solution.py:478
  29.8 8.4 %collective-permute-start.6 = (f32[2,2,1,64,128]{4,3,2,1,0:T(8,128)S(1)}, f32[2,2,1,64,128]{4,3,2,1,0:T(8,128)S(1)}, u32[]{:S(2)}, u32[]{:S(2)}) collective-permute-start(f32[2,2,1,64,128]{4,3,2,1,0:T(8,128)S(1)} %get-tuple-element.34), channel_id=1, source_target_pairs={{8,0},{4,1},{12,2},{0,3},{1,4},{13,5},{5,6},{9,7},{2,8},{14,9},{6,... | collective-permute-start | bytes 393224 | tf_op jit(solution)/shard_map/ppermute | solution.py:479
  32.4 9.0 %collective-permute-start.7 = (f32[2,2,1,64,128]{4,3,2,1,0:T(8,128)S(1)}, f32[2,2,1,64,128]{4,3,2,1,0:T(8,128)S(1)}, u32[]{:S(2)}, u32[]{:S(2)}) collective-permute-start(f32[2,2,1,64,128]{4,3,2,1,0:T(8,128)S(1)} %get-tuple-element.35), channel_id=1, source_target_pairs={{0,0},{12,1},{4,2},{8,3},{9,4},{5,5},{13,6},{1,7},{10,8},{6,9},{14... | collective-permute-start | bytes 393224 | tf_op jit(solution)/shard_map/ppermute | solution.py:479

commit v8 on v7

--- a/solution.py
+++ b/solution.py
@@ -158,7 +158,7 @@
         copy.wait()
 
 
-CHUNK = 64
+CHUNK = 128
 SMEM_SPEC = pl.BlockSpec(memory_space=pltpu.SMEM)
 VMEM_SPEC = pl.BlockSpec(memory_space=pltpu.VMEM)
 ANY_SPEC = pl.BlockSpec(memory_space=pl.ANY)
@@ -400,10 +400,16 @@
 
 
 def place_kernel(*refs):
-    o_ref, count = refs[-1], len(refs) - 1
+    refs, o_ref, sems = refs[:-2], refs[-2], refs[-1]
+    count = len(refs)
     size = refs[0].shape[0]
+    copies = []
     for j in range(count):
-        o_ref[pl.ds(pair_of(lax.axis_index("head"), lax.axis_index("rep"), j, count) * size, size)] = refs[j][...]
+        pair = pair_of(lax.axis_index("head"), lax.axis_index("rep"), j, count)
+        copies.append(pltpu.make_async_copy(refs[j], o_ref.at[pl.ds(pair * size, size)], sems.at[j]))
+        copies[-1].start()
+    for copy in copies:
+        copy.wait()
 
 
 def place(pieces):
@@ -412,8 +418,9 @@
     return pl.pallas_call(
         place_kernel,
         in_specs=[VMEM_SPEC] * count,
-        out_specs=VMEM_SPEC,
+        out_specs=ANY_SPEC,
         out_shape=jax.ShapeDtypeStruct((count * size, per, rows, dim), F32),
+        scratch_shapes=[pltpu.SemaphoreType.DMA((count,))],
         compiler_params=pltpu.CompilerParams(vmem_limit_bytes=4 * 2**20),
         name="place",
     )(*pieces)

time: 42.3 us -> 42.3 us (level)
  transfers between devices with their start and end apart: 8 -> 8, of which waited for: 5 -> 5; matrix products, arithmetic and copies ran while one was open for 0% -> 0% of each run, Pallas kernels for 37% -> 36%
where the time goes in v8:
time: 42.3 us; the launch traced here: 42.1 us
  Pallas kernels  17.3 us (41%)
  starting transfers between devices  15.3 us (36%)
  waiting for transfers between devices  7.45 us (18%)
  local copies, waits for them, and re-layouts  1.32 us (3%)
  between operations  0.78 us (2%)
    pallas_call x4, Pallas kernels, prefill_request(): pl.pallas_call(functools.partial(prefill_kernel, (index, blocks, first_bl...  12.1 us
    ppermute x2, starting transfers between devices, on_device(): lax.ppermute(packets[j], ('head', 'rep'), routes[j])  6.56 us
    ppermute x2, starting transfers between devices, on_device(): lax.ppermute(joined[j], ('head', 'rep'), [(b, a) for a, b in routes[j]])  4.47 us
    pallas_call x3, Pallas kernels, decode_request(): pl.pallas_call(functools.partial(decode_kernel, plan, heads, group, steps...  3.66 us
    ppermute x2, waiting for transfers between devices, on_device(): lax.ppermute(joined[j], ('head', 'rep'), [(b, a) for a, b in routes[j]])  3.16 us
    ppermute x1, starting transfers between devices, on_device(): joined = join(kept, lax.ppermute(sent, 'head', swap))  1.61 us
    ppermute x2, starting transfers between devices, on_device(): held[i].append(lax.ppermute(own[i], 'ctx', perm))  1.6 us
    ppermute x2, waiting for transfers between devices, on_device(): held[i].append(lax.ppermute(own[i], 'ctx', perm))  1.51 us
  transfers between devices with their start and end apart: 8, of which 5 were waited for; matrix products, arithmetic and copies ran while one was open for 0% of the time, Pallas kernels for 36%

profile of v8, /device:TPU:7, one launch (start us, length us, event | category | flops | bytes accessed | tf_op | source)
XLA Modules:
  0.0 42.1 jit_solution(2058065989409622358)
XLA Ops:
  0.6 0.0 copy-start.5
  0.6 0.0 copy-start.1
  0.7 1.2 %copy-done.1 = f32[2,2,256,2,128]{4,3,2,1,0:T(2,128)S(1)} copy-done((f32[2,2,256,2,128]{4,3,2,1,0:T(2,128)S(1)}, f32[2,2,256,2,128]{4,3,2,1,0:T(2,128)}, u32[]{:S(2)}) %copy-start.1) | copy-done | bytes 1048600
  1.9 0.0 copy-start.3
  1.9 0.0 copy-start.4
  1.9 0.3 collective-permute-start.1
  2.3 1.3 %collective-permute-start = (f32[1,2,512,128]{3,2,1,0:T(8,128)S(1)}, f32[1,2,512,128]{3,2,1,0:T(8,128)S(1)}, u32[]{:S(2)}, u32[]{:S(2)}) collective-permute-start(f32[1,2,512,128]{3,2,1,0:T(8,128)S(1)} %take.2.refs_1_.refs_0_.refs_3_), channel_id=1, source_target_pairs={{16,0},{0,16},{17,1},{1,17},{18,2},{2,18},{19,3},{3,19},{20,4},{4,... | collective-permute-start | bytes 1572872 | tf_op jit(solution)/shard_map/ppermute | solution.py:443
  3.6 0.0 copy-done.5
  3.6 0.1 copy.9.lengths
  3.7 0.0 copy-done.3
  3.7 0.0 copy-done.4
  3.7 0.0 copy-start
  3.7 0.0 copy-start.2
  3.7 0.7 %pack.1 = (f32[2,168,128]{2,1,0:T(8,128)S(1)}, f32[2,168,128]{2,1,0:T(8,128)S(1)}) custom-call(s32[8,1]{1,0:T(8,128)S(1)} %copy.9.lengths, f32[8,1,64,128]{3,2,1,0:T(8,128)S(1)} %bitcast.12, f32[8,1,16,128]{3,2,1,0:T(8,128)S(1)} %bitcast.13, f32[1,2,512,128]{3,2,1,0:T(8,128)S(1)} %take.3.refs_0_.refs_3_, f32[1,2,512,128]{3,2,1,0:T(8,128)S(1)} %take.2.refs_1_.refs_0_.refs_3_), custom_call_target="tpu_custom_call" | custom-call | flops 99999997952 | bytes 1000000 | tf_op jit(solution)/shard_map/pack/pallas_call | solution.py:355
  4.3 4.5 %collective-permute-start.2 = (f32[2,168,128]{2,1,0:T(8,128)S(1)}, f32[2,168,128]{2,1,0:T(8,128)S(1)}, u32[]{:S(2)}, u32[]{:S(2)}) collective-permute-start(f32[2,168,128]{2,1,0:T(8,128)S(1)} %get-tuple-element.19.refs_1_), channel_id=1, source_target_pairs={{0,8},{1,4},{2,12},{3,0},{4,1},{5,13},{6,5},{7,9},{8,2},{9,14},{10... | collective-permute-start | bytes 516104 | tf_op jit(solution)/shard_map/ppermute | solution.py:462
  8.8 2.1 %collective-permute-start.3 = (f32[2,168,128]{2,1,0:T(8,128)S(1)}, f32[2,168,128]{2,1,0:T(8,128)S(1)}, u32[]{:S(2)}, u32[]{:S(2)}) collective-permute-start(f32[2,168,128]{2,1,0:T(8,128)S(1)} %get-tuple-element.26), channel_id=1, source_target_pairs={{0,0},{1,12},{2,4},{3,8},{4,9},{5,5},{6,13},{7,1},{8,10},{9,6},{10... | collective-permute-start | bytes 516104 | tf_op jit(solution)/shard_map/ppermute | solution.py:462
  10.9 0.0 copy-done
  10.9 0.0 copy-done.2
  10.9 2.4 %prefill.4 = (f32[2,128,1024]{2,1,0:T(8,128)S(1)}, f32[2,8,1024]{2,1,0:T(8,128)S(1)}) custom-call(s32[8]{0:T(128)S(1)} %copy-done.2, f32[2,128,16,128]{3,2,1,0:T(8,128)S(1)} %copy-done, f32[1,2,512,128]{3,2,1,0:T(8,128)S(1)} %take.2.refs_1_.refs_0_.refs_3_, f32[2,168,128]{2,1,0:T(8,128)S(1)} %get-tuple-element.19.refs_1_), custom_call_target="tpu_custom_call" | custom-call | flops 67108864 | bytes 2621440 | tf_op jit(solution)/shard_map/prefill/pallas_call | solution.py:186
  13.3 2.4 %prefill.5 = (f32[2,128,1024]{2,1,0:T(8,128)S(1)}, f32[2,8,1024]{2,1,0:T(8,128)S(1)}) custom-call(s32[8]{0:T(128)S(1)} %copy-done.2, f32[2,128,16,128]{3,2,1,0:T(8,128)S(1)} %copy-done, f32[1,2,512,128]{3,2,1,0:T(8,128)S(1)} %take.3.refs_0_.refs_3_, f32[2,8,1024]{2,1,0:T(8,128)S(1)} %get-tuple-element.21.refs_1_.refs_2_), custom_call_target="tpu_custom_call" | custom-call | flops 67108864 | bytes 2621440 | tf_op jit(solution)/shard_map/prefill/pallas_call | solution.py:186
  15.8 0.0 collective-permute-done.1.refs_0_.refs_4_
  15.8 3.4 %prefill.6 = (f32[2,128,16,128]{3,2,1,0:T(8,128)}, f32[8,128]{1,0:T(8,128)S(1)}) custom-call(s32[8]{0:T(128)S(1)} %copy-done.2, f32[2,128,16,128]{3,2,1,0:T(8,128)S(1)} %copy-done, f32[1,2,512,128]{3,2,1,0:T(8,128)S(1)} %collective-permute-done.1.refs_0_.refs_4_, f32[2,128,1024]{2,1,0:T(8,128)S(1)} %get-tuple-element.22.refs_1_, ...), custom_call_target="tpu_custom_call" | custom-call | flops 67108864 | bytes 2621440 | tf_op jit(solution)/shard_map/prefill/pallas_call | solution.py:186
  19.1 0.8 %collective-permute-done.2.refs_0_ = f32[2,168,128]{2,1,0:T(8,128)S(1)} collective-permute-done((f32[2,168,128]{2,1,0:T(8,128)S(1)}, f32[2,168,128]{2,1,0:T(8,128)S(1)}, u32[]{:S(2)}, u32[]{:S(2)}) %collective-permute-start.2) | collective-permute-done | bytes 172064 | tf_op jit(solution)/shard_map/ppermute | solution.py:462
  19.9 0.0 collective-permute-done.3.refs_1_
  19.9 1.0 %collective-permute-start.4 = (f32[2,168,128]{2,1,0:T(8,128)S(1)}, f32[2,168,128]{2,1,0:T(8,128)S(1)}, u32[]{:S(2)}, u32[]{:S(2)}) collective-permute-start(f32[2,168,128]{2,1,0:T(8,128)S(1)} %other_side.1), channel_id=1, source_target_pairs={{0,4},{4,0},{8,12},{12,8},{1,5},{5,1},{9,13},{13,9},{2,6},{6,2},{1... | collective-permute-start | bytes 516104 | tf_op jit(solution)/shard_map/ppermute | solution.py:474
  21.0 1.0 %collective-permute-done.4.refs_2_ = f32[2,168,128]{2,1,0:T(8,128)S(1)} collective-permute-done((f32[2,168,128]{2,1,0:T(8,128)S(1)}, f32[2,168,128]{2,1,0:T(8,128)S(1)}, u32[]{:S(2)}, u32[]{:S(2)}) %collective-permute-start.4) | collective-permute-done | bytes 172064 | tf_op jit(solution)/shard_map/ppermute | solution.py:474
  22.0 1.4 %decode.3 = (f32[2,1,1,64,128]{4,3,2,1,0:T(8,128)S(1)}, f32[2,1,1,64,128]{4,3,2,1,0:T(8,128)S(1)}) custom-call(f32[2,168,128]{2,1,0:T(8,128)S(1)} %collective-permute-done.2.refs_0_, f32[2,168,128]{2,1,0:T(8,128)S(1)} %collective-permute-done.3.refs_1_, f32[2,168,128]{2,1,0:T(8,128)S(1)} %collective-permute-done.4.refs_2_, ...), custom_call_target="tpu_custom_call" | custom-call | flops 16777216 | bytes 1736704 | tf_op jit(solution)/shard_map/decode/pallas_call | solution.py:297
  23.5 1.1 %decode.4 = (f32[2,128,128]{2,1,0:T(8,128)S(1)}, f32[2,8,128]{2,1,0:T(8,128)S(1)}) custom-call(f32[2,168,128]{2,1,0:T(8,128)S(1)} %collective-permute-done.2.refs_0_, f32[2,168,128]{2,1,0:T(8,128)S(1)} %collective-permute-done.3.refs_1_, f32[2,168,128]{2,1,0:T(8,128)S(1)} %collective-permute-done.4.refs_2_, ...), custom_call_target="tpu_custom_call" | custom-call | flops 8388608 | bytes 1212416 | tf_op jit(solution)/shard_map/decode/pallas_call | solution.py:297
  24.5 1.5 %collective-permute-done.refs_0_.refs_3_ = f32[1,2,512,128]{3,2,1,0:T(8,128)S(1)} collective-permute-done((f32[1,2,512,128]{3,2,1,0:T(8,128)S(1)}, f32[1,2,512,128]{3,2,1,0:T(8,128)S(1)}, u32[]{:S(2)}, u32[]{:S(2)}) %collective-permute-start) | collective-permute-done | bytes 524320 | tf_op jit(solution)/shard_map/ppermute | solution.py:443
  26.0 1.2 %decode.5 = (f32[2,2,1,64,128]{4,3,2,1,0:T(8,128)S(1)}, f32[2,2,1,64,128]{4,3,2,1,0:T(8,128)S(1)}) custom-call(f32[2,168,128]{2,1,0:T(8,128)S(1)} %collective-permute-done.2.refs_0_, f32[2,168,128]{2,1,0:T(8,128)S(1)} %collective-permute-done.3.refs_1_, f32[2,168,128]{2,1,0:T(8,128)S(1)} %collective-permute-done.4.refs_2_, ...), custom_call_target="tpu_custom_call" | custom-call | flops 8388608 | bytes 1212416 | tf_op jit(solution)/shard_map/decode/pallas_call | solution.py:297
  27.2 1.6 %collective-permute-start.5 = (f32[2,2,1,64,128]{4,3,2,1,0:T(8,128)S(1)}, f32[2,2,1,64,128]{4,3,2,1,0:T(8,128)S(1)}, u32[]{:S(2)}, u32[]{:S(2)}) collective-permute-start(f32[2,2,1,64,128]{4,3,2,1,0:T(8,128)S(1)} %get-tuple-element.33), channel_id=1, source_target_pairs={{0,4},{4,0},{8,12},{12,8},{1,5},{5,1},{9,13},{13,9},{2,6},{6,2},{1... | collective-permute-start | bytes 393224 | tf_op jit(solution)/shard_map/ppermute | solution.py:485
  28.8 1.0 %collective-permute-done.5.back = f32[2,2,1,64,128]{4,3,2,1,0:T(8,128)S(1)} collective-permute-done((f32[2,2,1,64,128]{4,3,2,1,0:T(8,128)S(1)}, f32[2,2,1,64,128]{4,3,2,1,0:T(8,128)S(1)}, u32[]{:S(2)}, u32[]{:S(2)}) %collective-permute-start.5) | collective-permute-done | bytes 131104 | tf_op jit(solution)/shard_map/ppermute | solution.py:485
  29.8 2.6 %collective-permute-start.6 = (f32[2,2,1,64,128]{4,3,2,1,0:T(8,128)S(1)}, f32[2,2,1,64,128]{4,3,2,1,0:T(8,128)S(1)}, u32[]{:S(2)}, u32[]{:S(2)}) collective-permute-start(f32[2,2,1,64,128]{4,3,2,1,0:T(8,128)S(1)} %get-tuple-element.34), channel_id=1, source_target_pairs={{8,0},{4,1},{12,2},{0,3},{1,4},{13,5},{5,6},{9,7},{2,8},{14,9},{6,... | collective-permute-start | bytes 393224 | tf_op jit(solution)/shard_map/ppermute | solution.py:486
  32.4 1.9 %collective-permute-start.7 = (f32[2,2,1,64,128]{4,3,2,1,0:T(8,128)S(1)}, f32[2,2,1,64,128]{4,3,2,1,0:T(8,128)S(1)}, u32[]{:S(2)}, u32[]{:S(2)}) collective-permute-start(f32[2,2,1,64,128]{4,3,2,1,0:T(8,128)S(1)} %get-tuple-element.35), channel_id=1, source_target_pairs={{0,0},{12,1},{4,2},{8,3},{9,4},{5,5},{13,6},{1,7},{10,8},{6,9},{14... | collective-permute-start | bytes 393224 | tf_op jit(solution)/shard_map/ppermute | solution.py:486
  34.3 4.0 %prefill.7 = (f32[2,128,16,128]{3,2,1,0:T(8,128)}, f32[8,128]{1,0:T(8,128)}) custom-call(s32[8]{0:T(128)S(1)} %copy-done.2, f32[2,128,16,128]{3,2,1,0:T(8,128)S(1)} %copy-done, f32[1,2,512,128]{3,2,1,0:T(8,128)S(1)} %collective-permute-done.refs_0_.refs_3_, f32[2,128,1024]{2,1,0:T(8,128)S(1)} %get-tuple-element.20.refs_1_, ...), custom_call_target="tpu_custom_call", output_to_operand_aliasing={{0}: (5, {})} | custom-call | flops 67108864 | bytes 2621440 | tf_op jit(solution)/shard_map/prefill/pallas_call | solution.py:186
  38.3 0.0 collective-permute-done.6
  38.3 3.2 %collective-permute-done.7 = f32[2,2,1,64,128]{4,3,2,1,0:T(8,128)S(1)} collective-permute-done((f32[2,2,1,64,128]{4,3,2,1,0:T(8,128)S(1)}, f32[2,2,1,64,128]{4,3,2,1,0:T(8,128)S(1)}, u32[]{:S(2)}, u32[]{:S(2)}) %collective-permute-start.7) | collective-permute-done | bytes 131104 | tf_op jit(solution)/shard_map/ppermute | solution.py:486
  41.4 0.7 %place.1 = f32[8,1,64,128]{3,2,1,0:T(8,128)} custom-call(f32[4,1,64,128]{3,2,1,0:T(8,128)S(1)} %bitcast.10, f32[4,1,64,128]{3,2,1,0:T(8,128)S(1)} %bitcast.11), custom_call_target="tpu_custom_call" | custom-call | tf_op jit(solution)/shard_map/place/pallas_call | solution.py:418
  (4 shorter events, 0.1 us)
Async XLA Ops:
  0.6 3.0 %copy-start.5 = (s32[8,1]{0,1:T(1,128)S(1)}, s32[8,1]{0,1:T(1,128)}, u32[]{:S(2)}) copy-start(s32[8,1]{0,1:T(1,128)} %param.11) | copy-start | bytes 100
  0.6 1.2 %copy-start.1 = (f32[2,2,256,2,128]{4,3,2,1,0:T(2,128)S(1)}, f32[2,2,256,2,128]{4,3,2,1,0:T(2,128)}, u32[]{:S(2)}) copy-start(f32[2,2,256,2,128]{4,3,2,1,0:T(2,128)} %param.6) | copy-start | bytes 3145732
  1.9 1.8 %copy-start.3 = (f32[8,1,4,16,128]{4,3,2,1,0:T(8,128)S(1)}, f32[8,1,4,16,128]{4,3,2,1,0:T(8,128)}, u32[]{:S(2)}) copy-start(f32[8,1,4,16,128]{4,3,2,1,0:T(8,128)} %param.8) | copy-start | bytes 786436
  1.9 1.8 %copy-start.4 = (f32[8,1,4,2,2,128]{5,4,3,2,1,0:T(2,128)S(1)}, f32[8,1,4,2,2,128]{5,4,3,2,1,0:T(2,128)}, u32[]{:S(2)}) copy-start(f32[8,1,4,2,2,128]{5,4,3,2,1,0:T(2,128)} %param.9) | copy-start | bytes 196612
  1.9 13.8 %collective-permute-start.1 = (f32[1,2,512,128]{3,2,1,0:T(8,128)S(1)}, f32[1,2,512,128]{3,2,1,0:T(8,128)S(1)}, u32[]{:S(2)}, u32[]{:S(2)}) collective-permute-start(f32[1,2,512,128]{3,2,1,0:T(8,128)S(1)} %take.3.refs_0_.refs_3_), channel_id=1, source_target_pairs={{16,0},{0,16},{17,1},{1,17},{18,2},{2,18},{19,3},{3,19},{20,4},{4,... | collective-permute-start | bytes 1572872 | tf_op jit(solution)/shard_map/ppermute | solution.py:443
  2.3 23.7 %collective-permute-start = (f32[1,2,512,128]{3,2,1,0:T(8,128)S(1)}, f32[1,2,512,128]{3,2,1,0:T(8,128)S(1)}, u32[]{:S(2)}, u32[]{:S(2)}) collective-permute-start(f32[1,2,512,128]{3,2,1,0:T(8,128)S(1)} %take.2.refs_1_.refs_0_.refs_3_), channel_id=1, source_target_pairs={{16,0},{0,16},{17,1},{1,17},{18,2},{2,18},{19,3},{3,19},{20,4},{4,... | collective-permute-start | bytes 1572872 | tf_op jit(solution)/shard_map/ppermute | solution.py:443
  3.7 7.2 %copy-start = (f32[2,128,16,128]{3,2,1,0:T(8,128)S(1)}, f32[2,128,16,128]{3,2,1,0:T(8,128)}, u32[]{:S(2)}) copy-start(f32[2,128,16,128]{3,2,1,0:T(8,128)} %q_ref.7) | copy-start | bytes 6291460
  3.7 7.2 %copy-start.2 = (s32[8]{0:T(128)S(1)}, s32[8]{0:T(128)}, u32[]{:S(2)}) copy-start(s32[8]{0:T(128)} %lengths.8) | copy-start | bytes 100
  4.3 15.6 %collective-permute-start.2 = (f32[2,168,128]{2,1,0:T(8,128)S(1)}, f32[2,168,128]{2,1,0:T(8,128)S(1)}, u32[]{:S(2)}, u32[]{:S(2)}) collective-permute-start(f32[2,168,128]{2,1,0:T(8,128)S(1)} %get-tuple-element.19.refs_1_), channel_id=1, source_target_pairs={{0,8},{1,4},{2,12},{3,0},{4,1},{5,13},{6,5},{7,9},{8,2},{9,14},{10... | collective-permute-start | bytes 516104 | tf_op jit(solution)/shard_map/ppermute | solution.py:462
  8.8 11.1 %collective-permute-start.3 = (f32[2,168,128]{2,1,0:T(8,128)S(1)}, f32[2,168,128]{2,1,0:T(8,128)S(1)}, u32[]{:S(2)}, u32[]{:S(2)}) collective-permute-start(f32[2,168,128]{2,1,0:T(8,128)S(1)} %get-tuple-element.26), channel_id=1, source_target_pairs={{0,0},{1,12},{2,4},{3,8},{4,9},{5,5},{6,13},{7,1},{8,10},{9,6},{10... | collective-permute-start | bytes 516104 | tf_op jit(solution)/shard_map/ppermute | solution.py:462
  19.9 2.1 %collective-permute-start.4 = (f32[2,168,128]{2,1,0:T(8,128)S(1)}, f32[2,168,128]{2,1,0:T(8,128)S(1)}, u32[]{:S(2)}, u32[]{:S(2)}) collective-permute-start(f32[2,168,128]{2,1,0:T(8,128)S(1)} %other_side.1), channel_id=1, source_target_pairs={{0,4},{4,0},{8,12},{12,8},{1,5},{5,1},{9,13},{13,9},{2,6},{6,2},{1... | collective-permute-start | bytes 516104 | tf_op jit(solution)/shard_map/ppermute | solution.py:474
  27.2 2.6 %collective-permute-start.5 = (f32[2,2,1,64,128]{4,3,2,1,0:T(8,128)S(1)}, f32[2,2,1,64,128]{4,3,2,1,0:T(8,128)S(1)}, u32[]{:S(2)}, u32[]{:S(2)}) collective-permute-start(f32[2,2,1,64,128]{4,3,2,1,0:T(8,128)S(1)} %get-tuple-element.33), channel_id=1, source_target_pairs={{0,4},{4,0},{8,12},{12,8},{1,5},{5,1},{9,13},{13,9},{2,6},{6,2},{1... | collective-permute-start | bytes 393224 | tf_op jit(solution)/shard_map/ppermute | solution.py:485
  29.8 8.4 %collective-permute-start.6 = (f32[2,2,1,64,128]{4,3,2,1,0:T(8,128)S(1)}, f32[2,2,1,64,128]{4,3,2,1,0:T(8,128)S(1)}, u32[]{:S(2)}, u32[]{:S(2)}) collective-permute-start(f32[2,2,1,64,128]{4,3,2,1,0:T(8,128)S(1)} %get-tuple-element.34), channel_id=1, source_target_pairs={{8,0},{4,1},{12,2},{0,3},{1,4},{13,5},{5,6},{9,7},{2,8},{14,9},{6,... | collective-permute-start | bytes 393224 | tf_op jit(solution)/shard_map/ppermute | solution.py:486
  32.4 9.0 %collective-permute-start.7 = (f32[2,2,1,64,128]{4,3,2,1,0:T(8,128)S(1)}, f32[2,2,1,64,128]{4,3,2,1,0:T(8,128)S(1)}, u32[]{:S(2)}, u32[]{:S(2)}) collective-permute-start(f32[2,2,1,64,128]{4,3,2,1,0:T(8,128)S(1)} %get-tuple-element.35), channel_id=1, source_target_pairs={{0,0},{12,1},{4,2},{8,3},{9,4},{5,5},{13,6},{1,7},{10,8},{6,9},{14... | collective-permute-start | bytes 393224 | tf_op jit(solution)/shard_map/ppermute | solution.py:486
